TPU v7x, 512 devices: a whole 4x4x16 slice. The times are simulated.
512 devices in a mesh: gz: 16 (over z), gy: 32 (over x, y, core).
Axes of the slice: x: 4, y: 4, z: 16, core: 2. Of those that a mesh axis runs over, the one named last changes fastest.
Arguments:
- source: float32 [2, 256, 512, 128], P(None, 'gz', 'gy'), may hold values from -6 to 6
- labels: int32 [256, 512, 128], P('gz', 'gy'), may hold values from 0 to 3
- phase_table: float32 [4, 4], replicated, may hold values from 0.1 to 3
Outputs:
- potential: float32 [2, 256, 512, 128], P(None, 'gz', 'gy')
All inputs are finite; a program needn't handle non-finite values.
Results may differ from a plain program's by a relative error of at most 0.000065.
Values sent between devices are 32-bit elements; how exact they have to be, the bound alone decides.
No kernel may reach another device: no remote copies, remote signals or barrier semaphores. Data moves between devices by JAX's collectives and lax.ppermute only.
A program may use at most 128 MiB of HBM per device.

v0:
```python
import jax
import jax.numpy as jnp
from jax import lax
from jax.sharding import PartitionSpec as P

PHASES = 4
LEVELS = 4
POST = 2
COARSE_SWEEPS = 8


relax = 0.7
mass_scale = 0.01


def padded_2(shard, sides, width):
    for axis, dim in sides:
        devices, length = (lax.axis_size(axis), shard.shape[dim])
        up = [(i, (i + 1) % devices) for i in range(devices - 1)]
        down = [(j, i) for i, j in up]
        last = lax.slice_in_dim(shard, length - width, length, axis=dim)
        initial = lax.slice_in_dim(shard, 0, width, axis=dim)
        before = lax.ppermute(last, axis, up)
        after = lax.ppermute(initial, axis, down)
        shard = jnp.concatenate([before, shard, after], axis=dim)
    return shard


def coefficients(labels, phase_table):
    scales = jnp.array([1.0, 1.0, mass_scale, mass_scale], jnp.float32)
    scaled = phase_table * scales[None, :]
    phase_ids = jnp.arange(PHASES, dtype=jnp.int32)
    onehot = (labels[None] == phase_ids[:, None, None, None]).astype(jnp.float32)
    return jnp.einsum("pzyx,pc->czyx", onehot, scaled, precision=lax.Precision.HIGHEST)


def neighbours(padded):
    center = padded[:, 1:-1, 1:-1, :]
    xpad = jnp.pad(center, ((0, 0), (0, 0), (0, 0), (1, 1)))
    return [
        padded[:, :-2, 1:-1, :],
        padded[:, 2:, 1:-1, :],
        padded[:, 1:-1, :-2, :],
        padded[:, 1:-1, 2:, :],
        xpad[..., :-2],
        xpad[..., 2:],
    ]


def diagonal(sig_pad):
    center = sig_pad[:, 1:-1, 1:-1, :]
    diag_re = center[2]
    diag_im = center[3]
    for near in neighbours(sig_pad):
        diag_re = diag_re + 0.5 * (center[0] + near[0])
        diag_im = diag_im + 0.5 * (center[1] + near[1])
    return jnp.stack([diag_re, diag_im])


def apply_op(field_pad, sig_pad):
    center = sig_pad[:, 1:-1, 1:-1, :]
    value = field_pad[:, 1:-1, 1:-1, :]
    acc_re = center[2] * value[0] - center[3] * value[1]
    acc_im = center[2] * value[1] + center[3] * value[0]
    for near_s, near_v in zip(neighbours(sig_pad), neighbours(field_pad)):
        face_re = 0.5 * (center[0] + near_s[0])
        face_im = 0.5 * (center[1] + near_s[1])
        diff_re = value[0] - near_v[0]
        diff_im = value[1] - near_v[1]
        acc_re = acc_re + (face_re * diff_re - face_im * diff_im)
        acc_im = acc_im + (face_re * diff_im + face_im * diff_re)
    return jnp.stack([acc_re, acc_im])


def quotient(resid, diag):
    denom = diag[0] * diag[0] + diag[1] * diag[1]
    q_re = (resid[0] * diag[0] + resid[1] * diag[1]) / denom
    q_im = (resid[1] * diag[0] - resid[0] * diag[1]) / denom
    return relax * jnp.stack([q_re, q_im])


def block_sum(field):
    chans, zc, yc, xc = field.shape
    return field.reshape(chans, zc // 2, 2, yc // 2, 2, xc // 2, 2).sum(axis=(2, 4, 6))


def coarse_coeffs(sig):
    mean = block_sum(sig) * 0.125
    return jnp.concatenate([mean[:2], 4.0 * mean[2:]], 0)


def prolong(field):
    return jnp.repeat(jnp.repeat(jnp.repeat(field, 2, axis=1), 2, axis=2), 2, axis=3)


def field_rims(field, width):
    return padded_2(field, (("gz", 1), ("gy", 2)), width)


def coeff_rims(sig, width):
    return padded_2(sig, (("gz", 1), ("gy", 2)), width)


def coarsest(rhs, sig):
    sig_pad = coeff_rims(sig, 1)
    diag = diagonal(sig_pad)
    guess = quotient(rhs, diag)
    for sweep in range(COARSE_SWEEPS - 1):
        guess = guess + quotient(rhs - apply_op(field_rims(guess, 1), sig_pad), diag)
    return guess


def vcycle(level, rhs, sig):
    if level == LEVELS:
        return coarsest(rhs, sig)
    sig_pad = coeff_rims(sig, 1)
    diag = diagonal(sig_pad)
    guess = quotient(rhs, diag)
    guess = guess + quotient(rhs - apply_op(field_rims(guess, 1), sig_pad), diag)
    resid = rhs - apply_op(field_rims(guess, 1), sig_pad)
    correction = vcycle(level + 1, 0.5 * block_sum(resid), coarse_coeffs(sig))
    guess = guess + prolong(correction)
    for sweep in range(POST):
        guess = guess + quotient(rhs - apply_op(field_rims(guess, 1), sig_pad), diag)
    return guess


def body(source, labels, phase_table):
    return vcycle(0, source, coefficients(labels, phase_table))


def solution(mesh):
    in_specs = (P(None, "gz", "gy", None), P("gz", "gy", None), P())
    out_specs = P(None, "gz", "gy", None)
    return jax.shard_map(body, mesh=mesh, in_specs=in_specs, out_specs=out_specs, check_vma=False)
```

profile of v0, /device:TPU:25, one launch (start us, length us, event | category | flops | bytes accessed | tf_op | source)
XLA Modules:
  0.0 580.1 jit_solution(15659877138281195944)
XLA Ops:
  6.6 8.7 %copy.701 = f32[4,16,16,128]{0,3,2,1:T(8,128)} copy(f32[4,16,16,128]{3,0,2,1:T(4,128)S(1)} %fusion.1) | data formatting | bytes 1048576 | tf_op jit(solution)/shard_map/pzyx,pc->czyx/dot_general | solution.py:34
  15.3 13.1 %reduce_sum.87 = f32[4,8,8,64]{0,3,2,1:T(8,128)} reduce(f32[4,8,2,8,2,64,2]{0,6,5,4,3,2,1:T(2,128)} %bitcast.336, f32[]{:T(128)} %constant.7.clone.1), dimensions={2,4,6}, to_apply=%region_1.2 | reduce | flops 114688 | bytes 589828 | tf_op jit(solution)/shard_map/reduce_sum | solution.py:84
  70.0 5.2 collective-permute-done.7
  86.9 5.4 collective-permute-start.10
  94.9 6.1 %collective-permute-start.36 = (f32[4,1,2,16]{3,2,1,0:T(2,128)}, f32[4,1,2,16]{3,2,1,0:T(2,128)}, u32[]{:S(2)}, u32[]{:S(2)}) collective-permute-start(f32[4,1,2,16]{3,2,1,0:T(2,128)} %get-tuple-element.350), channel_id=1, source_target_pairs={{0,32},{32,64},{64,96},{96,128},{128,160},{160,192},{192,224},{224... | collective-permute-start | bytes 1544 | tf_op jit(solution)/shard_map/ppermute | solution.py:23
  104.2 18.1 %reshape.2965 = f32[2,8,2,8,2,64,2]{6,5,4,3,2,1,0:T(8,128)} reshape(f32[2,16,16,128]{3,2,1,0:T(8,128)S(1)} %maximum_subtract_fusion.2) | data formatting | bytes 524288 | tf_op jit(solution)/shard_map/reshape | solution.py:84
  122.4 7.0 %reduce_sum.86 = f32[2,8,8,64]{3,2,1,0:T(8,128)S(1)} reduce(f32[2,8,2,8,2,64,2]{6,5,4,3,2,1,0:T(8,128)} %reshape.2965, f32[]{:T(128)} %constant.7.clone.1), dimensions={2,4,6}, to_apply=%region_0.1 | reduce | flops 57344 | bytes 294916 | tf_op jit(solution)/shard_map/reduce_sum | solution.py:84
  141.0 6.6 %collective-permute-start.18 = (f32[2,10,1,64]{3,0,2,1:T(2,128)S(1)}, f32[2,10,1,64]{3,0,2,1:T(2,128)S(1)}, u32[]{:S(2)}, u32[]{:S(2)}) collective-permute-start(f32[2,10,1,64]{3,0,2,1:T(2,128)S(1)} %copy.795), channel_id=1, source_target_pairs={{0,1},{1,2},{2,3},{3,4},{4,5},{5,6},{6,7},{7,8},{8,9},{9,10},{10,1... | collective-permute-start | bytes 15368 | tf_op jit(solution)/shard_map/ppermute | solution.py:23
  169.5 5.7 collective-permute-start.26
  199.9 6.9 %collective-permute-start.30 = (f32[2,6,1,32]{3,2,1,0:T(1,128)S(1)}, f32[2,6,1,32]{3,2,1,0:T(1,128)S(1)}, u32[]{:S(2)}, u32[]{:S(2)}) collective-permute-start(f32[2,6,1,32]{3,2,1,0:T(1,128)S(1)} %get-tuple-element.298), channel_id=1, source_target_pairs={{0,1},{1,2},{2,3},{3,4},{4,5},{5,6},{6,7},{7,8},{8,9},{9,10},{10,1... | collective-permute-start | bytes 4616 | tf_op jit(solution)/shard_map/ppermute | solution.py:23
  223.8 5.6 collective-permute-start.34
  268.9 7.1 %collective-permute-start.46 = (f32[2,4,1,16]{3,1,2,0:T(4,128)S(1)}, f32[2,4,1,16]{3,1,2,0:T(4,128)S(1)}, u32[]{:S(2)}, u32[]{:S(2)}) collective-permute-start(f32[2,4,1,16]{3,1,2,0:T(4,128)S(1)} %get-tuple-element.342), channel_id=1, source_target_pairs={{0,1},{1,2},{2,3},{3,4},{4,5},{5,6},{6,7},{7,8},{8,9},{9,10},{10,1... | collective-permute-start | bytes 1544 | tf_op jit(solution)/shard_map/ppermute | solution.py:23
  278.0 5.8 collective-permute-start.50
  304.5 5.1 collective-permute-done.55
  342.9 5.1 collective-permute-done.63
  416.8 5.1 collective-permute-done.79
  434.8 5.1 collective-permute-done.83
  452.7 5.1 collective-permute-done.87
  471.1 5.1 collective-permute-done.91
  489.4 5.1 collective-permute-done.95
  511.1 5.1 collective-permute-done.99
  529.6 5.1 collective-permute-done.103
  554.0 5.3 collective-permute-done.107
  573.3 5.3 collective-permute-done.111
  (632 shorter events, 418.9 us)
Async XLA Ops:
  1.7 39.8 %collective-permute-start = (f32[4,1,16,128]{3,2,1,0:T(8,128)S(1)}, f32[4,1,16,128]{3,2,1,0:T(8,128)S(1)}, u32[]{:S(2)}, u32[]{:S(2)}) collective-permute-start(f32[4,1,16,128]{3,2,1,0:T(8,128)S(1)} %get-tuple-element.226), channel_id=1, source_target_pairs={{0,32},{32,64},{64,96},{96,128},{128,160},{160,192},{192,224},{224... | collective-permute-start | bytes 98312 | tf_op jit(solution)/shard_map/ppermute | solution.py:23
  5.3 36.4 %collective-permute-start.1 = (f32[4,1,16,128]{3,2,1,0:T(8,128)S(1)}, f32[4,1,16,128]{3,2,1,0:T(8,128)S(1)}, u32[]{:S(2)}, u32[]{:S(2)}) collective-permute-start(f32[4,1,16,128]{3,2,1,0:T(8,128)S(1)} %get-tuple-element.225), channel_id=1, source_target_pairs={{32,0},{64,32},{96,64},{128,96},{160,128},{192,160},{224,192},{256... | collective-permute-start | bytes 98312 | tf_op jit(solution)/shard_map/ppermute | solution.py:24
  30.8 51.5 %collective-permute-start.12 = (f32[4,1,8,64]{3,2,1,0:T(8,128)S(1)}, f32[4,1,8,64]{3,2,1,0:T(8,128)S(1)}, u32[]{:S(2)}, u32[]{:S(2)}) collective-permute-start(f32[4,1,8,64]{3,2,1,0:T(8,128)S(1)} %get-tuple-element.252), channel_id=1, source_target_pairs={{0,32},{32,64},{64,96},{96,128},{128,160},{160,192},{192,224},{224... | collective-permute-start | bytes 24584 | tf_op jit(solution)/shard_map/ppermute | solution.py:23
  34.9 47.3 %collective-permute-start.13 = (f32[4,1,8,64]{3,2,1,0:T(8,128)S(1)}, f32[4,1,8,64]{3,2,1,0:T(8,128)S(1)}, u32[]{:S(2)}, u32[]{:S(2)}) collective-permute-start(f32[4,1,8,64]{3,2,1,0:T(8,128)S(1)} %get-tuple-element.251), channel_id=1, source_target_pairs={{32,0},{64,32},{96,64},{128,96},{160,128},{192,160},{224,192},{256... | collective-permute-start | bytes 24584 | tf_op jit(solution)/shard_map/ppermute | solution.py:24
  76.1 10.6 %collective-permute-start.8 = (f32[2,1,16,128]{3,2,1,0:T(8,128)S(1)}, f32[2,1,16,128]{3,2,1,0:T(8,128)S(1)}, u32[]{:S(2)}, u32[]{:S(2)}) collective-permute-start(f32[2,1,16,128]{3,2,1,0:T(8,128)S(1)} %get-tuple-element.240), channel_id=1, source_target_pairs={{0,32},{32,64},{64,96},{96,128},{128,160},{160,192},{192,224},{224... | collective-permute-start | bytes 49160 | tf_op jit(solution)/shard_map/ppermute | solution.py:23
  82.3 18.6 %collective-permute-start.14 = (f32[4,10,1,64]{3,0,2,1:T(4,128)S(1)}, f32[4,10,1,64]{3,0,2,1:T(4,128)S(1)}, u32[]{:S(2)}, u32[]{:S(2)}) collective-permute-start(f32[4,10,1,64]{3,0,2,1:T(4,128)S(1)} %copy.793), channel_id=1, source_target_pairs={{0,1},{1,2},{2,3},{3,4},{4,5},{5,6},{6,7},{7,8},{8,9},{9,10},{10,1... | collective-permute-start | bytes 30728 | tf_op jit(solution)/shard_map/ppermute | solution.py:23
  84.6 18.3 %collective-permute-start.15 = (f32[4,10,1,64]{3,0,2,1:T(4,128)S(1)}, f32[4,10,1,64]{3,0,2,1:T(4,128)S(1)}, u32[]{:S(2)}, u32[]{:S(2)}) collective-permute-start(f32[4,10,1,64]{3,0,2,1:T(4,128)S(1)} %copy.794), channel_id=1, source_target_pairs={{1,0},{2,1},{3,2},{4,3},{5,4},{6,5},{7,6},{8,7},{9,8},{10,9},{11,1... | collective-permute-start | bytes 30728 | tf_op jit(solution)/shard_map/ppermute | solution.py:24
  86.9 16.5 %collective-permute-start.10 = (f32[2,18,1,128]{3,2,1,0:T(1,128)S(1)}, f32[2,18,1,128]{3,2,1,0:T(1,128)S(1)}, u32[]{:S(2)}, u32[]{:S(2)}) collective-permute-start(f32[2,18,1,128]{3,2,1,0:T(1,128)S(1)} %get-tuple-element.232), channel_id=1, source_target_pairs={{0,1},{1,2},{2,3},{3,4},{4,5},{5,6},{6,7},{7,8},{8,9},{9,10},{10,1... | collective-permute-start | bytes 55304 | tf_op jit(solution)/shard_map/ppermute | solution.py:23
  92.3 11.2 %collective-permute-start.11 = (f32[2,18,1,128]{3,2,1,0:T(1,128)S(1)}, f32[2,18,1,128]{3,2,1,0:T(1,128)S(1)}, u32[]{:S(2)}, u32[]{:S(2)}) collective-permute-start(f32[2,18,1,128]{3,2,1,0:T(1,128)S(1)} %get-tuple-element.231), channel_id=1, source_target_pairs={{1,0},{2,1},{3,2},{4,3},{5,4},{6,5},{7,6},{8,7},{9,8},{10,9},{11,1... | collective-permute-start | bytes 55304 | tf_op jit(solution)/shard_map/ppermute | solution.py:24
  94.9 113.8 %collective-permute-start.36 = (f32[4,1,2,16]{3,2,1,0:T(2,128)}, f32[4,1,2,16]{3,2,1,0:T(2,128)}, u32[]{:S(2)}, u32[]{:S(2)}) collective-permute-start(f32[4,1,2,16]{3,2,1,0:T(2,128)} %get-tuple-element.350), channel_id=1, source_target_pairs={{0,32},{32,64},{64,96},{96,128},{128,160},{160,192},{192,224},{224... | collective-permute-start | bytes 1544 | tf_op jit(solution)/shard_map/ppermute | solution.py:23
  100.9 107.8 %collective-permute-start.37 = (f32[4,1,2,16]{3,2,1,0:T(2,128)}, f32[4,1,2,16]{3,2,1,0:T(2,128)}, u32[]{:S(2)}, u32[]{:S(2)}) collective-permute-start(f32[4,1,2,16]{3,2,1,0:T(2,128)} %get-tuple-element.349), channel_id=1, source_target_pairs={{32,0},{64,32},{96,64},{128,96},{160,128},{192,160},{224,192},{256... | collective-permute-start | bytes 1544 | tf_op jit(solution)/shard_map/ppermute | solution.py:24
  129.8 11.1 %collective-permute-start.16 = (f32[2,1,8,64]{3,2,1,0:T(8,128)S(1)}, f32[2,1,8,64]{3,2,1,0:T(8,128)S(1)}, u32[]{:S(2)}, u32[]{:S(2)}) collective-permute-start(f32[2,1,8,64]{3,2,1,0:T(8,128)S(1)} %get-tuple-element.270), channel_id=1, source_target_pairs={{0,32},{32,64},{64,96},{96,128},{128,160},{160,192},{192,224},{224... | collective-permute-start | bytes 12296 | tf_op jit(solution)/shard_map/ppermute | solution.py:23
  136.6 30.3 %collective-permute-start.24 = (f32[4,1,4,32]{3,2,1,0:T(4,128)}, f32[4,1,4,32]{3,2,1,0:T(4,128)S(1)}, u32[]{:S(2)}, u32[]{:S(2)}) collective-permute-start(f32[4,1,4,32]{3,2,1,0:T(4,128)} %get-tuple-element.280), channel_id=1, source_target_pairs={{0,32},{32,64},{64,96},{96,128},{128,160},{160,192},{192,224},{224... | collective-permute-start | bytes 6152 | tf_op jit(solution)/shard_map/ppermute | solution.py:23
  163.8 15.0 %collective-permute-start.22 = (f32[2,10,1,64]{3,0,2,1:T(2,128)S(1)}, f32[2,10,1,64]{3,0,2,1:T(2,128)S(1)}, u32[]{:S(2)}, u32[]{:S(2)}) collective-permute-start(f32[2,10,1,64]{3,0,2,1:T(2,128)S(1)} %copy.797), channel_id=1, source_target_pairs={{0,1},{1,2},{2,3},{3,4},{4,5},{5,6},{6,7},{7,8},{8,9},{9,10},{10,1... | collective-permute-start | bytes 15368 | tf_op jit(solution)/shard_map/ppermute | solution.py:23
  167.0 13.8 %collective-permute-start.23 = (f32[2,10,1,64]{3,0,2,1:T(2,128)S(1)}, f32[2,10,1,64]{3,0,2,1:T(2,128)S(1)}, u32[]{:S(2)}, u32[]{:S(2)}) collective-permute-start(f32[2,10,1,64]{3,0,2,1:T(2,128)S(1)} %copy.798), channel_id=1, source_target_pairs={{1,0},{2,1},{3,2},{4,3},{5,4},{6,5},{7,6},{8,7},{9,8},{10,9},{11,1... | collective-permute-start | bytes 15368 | tf_op jit(solution)/shard_map/ppermute | solution.py:24
  169.5 19.9 %collective-permute-start.26 = (f32[4,6,1,32]{3,2,1,0:T(1,128)}, f32[4,6,1,32]{3,2,1,0:T(1,128)}, u32[]{:S(2)}, u32[]{:S(2)}) collective-permute-start(f32[4,6,1,32]{3,2,1,0:T(1,128)} %get-tuple-element.272), channel_id=1, source_target_pairs={{0,1},{1,2},{2,3},{3,4},{4,5},{5,6},{6,7},{7,8},{8,9},{9,10},{10,1... | collective-permute-start | bytes 9224 | tf_op jit(solution)/shard_map/ppermute | solution.py:23
  178.8 10.6 %collective-permute-start.27 = (f32[4,6,1,32]{3,2,1,0:T(1,128)}, f32[4,6,1,32]{3,2,1,0:T(1,128)}, u32[]{:S(2)}, u32[]{:S(2)}) collective-permute-start(f32[4,6,1,32]{3,2,1,0:T(1,128)} %get-tuple-element.271), channel_id=1, source_target_pairs={{1,0},{2,1},{3,2},{4,3},{5,4},{6,5},{7,6},{8,7},{9,8},{10,9},{11,1... | collective-permute-start | bytes 9224 | tf_op jit(solution)/shard_map/ppermute | solution.py:24
  214.1 9.7 %collective-permute-start.32 = (f32[2,1,4,32]{3,2,1,0:T(4,128)S(1)}, f32[2,1,4,32]{3,2,1,0:T(4,128)S(1)}, u32[]{:S(2)}, u32[]{:S(2)}) collective-permute-start(f32[2,1,4,32]{3,2,1,0:T(4,128)S(1)} %get-tuple-element.308), channel_id=1, source_target_pairs={{0,32},{32,64},{64,96},{96,128},{128,160},{160,192},{192,224},{224... | collective-permute-start | bytes 3080 | tf_op jit(solution)/shard_map/ppermute | solution.py:23
  219.5 11.9 %collective-permute-start.38 = (f32[4,4,1,16]{3,1,2,0:T(4,128)S(1)}, f32[4,4,1,16]{3,1,2,0:T(4,128)S(1)}, u32[]{:S(2)}, u32[]{:S(2)}) collective-permute-start(f32[4,4,1,16]{3,1,2,0:T(4,128)S(1)} %get-tuple-element.306), channel_id=1, source_target_pairs={{0,1},{1,2},{2,3},{3,4},{4,5},{5,6},{6,7},{7,8},{8,9},{9,10},{10,1... | collective-permute-start | bytes 3080 | tf_op jit(solution)/shard_map/ppermute | solution.py:23
  221.7 9.7 %collective-permute-start.39 = (f32[4,4,1,16]{3,1,2,0:T(4,128)S(1)}, f32[4,4,1,16]{3,1,2,0:T(4,128)S(1)}, u32[]{:S(2)}, u32[]{:S(2)}) collective-permute-start(f32[4,4,1,16]{3,1,2,0:T(4,128)S(1)} %get-tuple-element.305), channel_id=1, source_target_pairs={{1,0},{2,1},{3,2},{4,3},{5,4},{6,5},{7,6},{8,7},{9,8},{10,9},{11,1... | collective-permute-start | bytes 3080 | tf_op jit(solution)/shard_map/ppermute | solution.py:24
  247.9 10.0 %collective-permute-start.42 = (f32[2,4,1,16]{3,1,2,0:T(4,128)S(1)}, f32[2,4,1,16]{3,1,2,0:T(4,128)S(1)}, u32[]{:S(2)}, u32[]{:S(2)}) collective-permute-start(f32[2,4,1,16]{3,1,2,0:T(4,128)S(1)} %get-tuple-element.348), channel_id=1, source_target_pairs={{0,1},{1,2},{2,3},{3,4},{4,5},{5,6},{6,7},{7,8},{8,9},{9,10},{10,1... | collective-permute-start | bytes 1544 | tf_op jit(solution)/shard_map/ppermute | solution.py:23
  253.0 25.0 %collective-permute-start.48 = (f32[4,1,1,8]{3,2,1,0:T(1,128)S(1)}, f32[4,1,1,8]{3,2,1,0:T(1,128)S(1)}, u32[]{:S(2)}, u32[]{:S(2)}) collective-permute-start(f32[4,1,1,8]{3,2,1,0:T(1,128)S(1)} %pad_maximum_fusion.234), channel_id=1, source_target_pairs={{0,32},{32,64},{64,96},{96,128},{128,160},{160,192},{192,224},{224... | collective-permute-start | bytes 392 | tf_op jit(solution)/shard_map/ppermute | solution.py:23
  256.6 21.4 %collective-permute-start.49 = (f32[4,1,1,8]{3,2,1,0:T(1,128)S(1)}, f32[4,1,1,8]{3,2,1,0:T(1,128)S(1)}, u32[]{:S(2)}, u32[]{:S(2)}) collective-permute-start(f32[4,1,1,8]{3,2,1,0:T(1,128)S(1)} %pad_maximum_fusion.234), channel_id=1, source_target_pairs={{32,0},{64,32},{96,64},{128,96},{160,128},{192,160},{224,192},{256... | collective-permute-start | bytes 392 | tf_op jit(solution)/shard_map/ppermute | solution.py:24
  268.9 16.8 %collective-permute-start.46 = (f32[2,4,1,16]{3,1,2,0:T(4,128)S(1)}, f32[2,4,1,16]{3,1,2,0:T(4,128)S(1)}, u32[]{:S(2)}, u32[]{:S(2)}) collective-permute-start(f32[2,4,1,16]{3,1,2,0:T(4,128)S(1)} %get-tuple-element.342), channel_id=1, source_target_pairs={{0,1},{1,2},{2,3},{3,4},{4,5},{5,6},{6,7},{7,8},{8,9},{9,10},{10,1... | collective-permute-start | bytes 1544 | tf_op jit(solution)/shard_map/ppermute | solution.py:23
  (167 other events, 3091.6 us)
where the time goes:
time: 584 us; the launch traced here: 580 us
  starting transfers between devices  307 us (53%)
  waiting for transfers between devices  171 us (29%)
  local copies, waits for them, and re-layouts  52.7 us (9%)
  other arithmetic  44.5 us (8%)
    ppermute x56, starting transfers between devices, padded_2(): before = lax.ppermute(last, axis, up)  217 us
    ppermute x56, waiting for transfers between devices, padded_2(): after = lax.ppermute(initial, axis, down)  170 us
    ppermute x56, starting transfers between devices, padded_2(): after = lax.ppermute(initial, axis, down)  90.5 us
    reduce_sum x10, other arithmetic, block_sum(): field.reshape(chans, zc // 2, 2, yc // 2, 2, xc // 2, 2).sum(axis=(2, 4, 6))  26.3 us
    reshape x1, local copies, waits for them, and re-layouts, block_sum(): field.reshape(chans, zc // 2, 2, yc // 2, 2, xc // 2, 2).sum(axis=(2, 4, 6))  18.1 us
  transfers between devices with their start and end apart: 112, of which 43 were waited for; matrix products, arithmetic and copies ran while one was open for 14% of the time, Pallas kernels for 0%

commit v1 on v0

v1 whole, which is shorter than its diff:
```python
import jax
import jax.numpy as jnp
from jax import lax
from jax.experimental import pallas as pl
from jax.experimental.pallas import tpu as pltpu
from jax.sharding import PartitionSpec as P

PHASES = 4
COARSE_SWEEPS = 8
LANES = 128
relax = 0.7
keep = 1.0 - relax
mass_scale = 0.01
F32 = jnp.float32
VMEM_BYTES = 40 * 1024 * 1024


def lanes(rows):
    return lax.broadcasted_iota(jnp.int32, (rows, LANES), 1)


def row_ids(rows):
    return lax.broadcasted_iota(jnp.int32, (rows, LANES), 0)


def ahead_x(q, k):
    return pltpu.roll(q, (-k) % LANES, 1)


def ahead_y(q, k):
    return pltpu.roll(q, (-k) % q.shape[0], 0)


def pair_x(q, k):
    return q + swap_x(q, k)


def swap_x(q, k):
    return jnp.where((lanes(q.shape[0]) & k) == 0, ahead_x(q, k), ahead_x(q, -k))


def interleave(re, im):
    return jnp.where((lanes(re.shape[0]) & 1) == 0, re, im)


def separate(q):
    even = (lanes(q.shape[0]) & 1) == 0
    return jnp.where(even, q, ahead_x(q, -1)), jnp.where(even, ahead_x(q, 1), q)


def each(lo, hi, body, step=2):
    full = (hi - lo) // step

    def run(i, carry):
        for j in range(step):
            body(lo + i * step + j)
        return carry

    lax.fori_loop(0, full, run, 0)
    for z in range(lo + full * step, hi):
        body(z)


def times(t, q):
    return t[0] * q[0] - t[1] * q[1], t[0] * q[1] + t[1] * q[0]


def pair(ref, z):
    return ref[0, z], ref[1, z]


def put(ref, z, q):
    ref[0, z] = q[0]
    ref[1, z] = q[1]


def add(*terms):
    return sum(t[0] for t in terms[1:]) + terms[0][0], sum(t[1] for t in terms[1:]) + terms[0][1]


def both(fn, q, k):
    return fn(q[0], k), fn(q[1], k)


def inside(rows, wrap, z, first_z, first_y, size_z, size_y, dead=()):
    r = row_ids(rows)
    y = jnp.where(r >= wrap, r - rows, r) + first_y
    ok = (y >= 0) & (y < size_y)
    plane = jnp.full((rows, LANES), first_z + z, jnp.int32)
    ok = ok & (plane >= 0) & (plane < size_z)
    if dead:
        ok = ok & ((r < dead[0]) | (r >= dead[1]))
    return ok


def make_faces(z, shift, ok, s, m, tz, ty, tx, w, g=None):
    lane = lanes(s.shape[2])
    last = lane >= LANES - shift
    initial = lane < shift
    diag = []
    for c in (0, 1):
        here = s[c, z]
        up = 0.5 * (here + s[c, z + 1])
        down = 0.5 * (here + s[c, z - 1])
        side = 0.5 * (here + ahead_y(here, 1))
        right = 0.5 * (here + jnp.where(last, 0.0, ahead_x(here, shift)))
        left = 0.5 * (here + jnp.where(initial, 0.0, ahead_x(here, -shift)))
        tz[c, z] = up
        ty[c, z] = side
        tx[c, z] = jnp.where(last, 0.0, right)
        diag.append(m[c, z] + (up + down) + (side + ahead_y(side, -1)) + (right + left))
    inv = jnp.where(ok, relax / (diag[0] * diag[0] + diag[1] * diag[1]), 0.0)
    q = (diag[0] * inv, -(diag[1] * inv))
    put(w, z, q)
    if g is not None:
        put(g, z, diag)
    return q


def inflow(z, shift, v, tz, ty, tx):
    here = pair(v, z)
    side, right = pair(ty, z), pair(tx, z)
    return add(
        times(pair(tz, z), pair(v, z + 1)),
        times(pair(tz, z - 1), pair(v, z - 1)),
        times(side, both(ahead_y, here, 1)),
        both(ahead_y, times(side, here), -1),
        times(right, both(ahead_x, here, shift)),
        both(ahead_x, times(right, here), -shift),
    )


def swept(z, shift, v, f, tz, ty, tx, w):
    here = pair(v, z)
    step = times(pair(w, z), add(pair(f, z), inflow(z, shift, v, tz, ty, tx)))
    return keep * here[0] + step[0], keep * here[1] + step[1]


def residual(z, shift, v, f, tz, ty, tx, g):
    out = times(pair(g, z), pair(v, z))
    gain = add(pair(f, z), inflow(z, shift, v, tz, ty, tx))
    return gain[0] - out[0], gain[1] - out[1]


def rows_paired(buf, at, start, count):
    plane = buf.at[at]
    return plane[pl.ds(start, count, stride=2), :] + plane[pl.ds(start + 1, count, stride=2), :]


def packed_row(stack):
    lane, row = lanes(8), row_ids(8)
    cells = jnp.take_along_axis(stack, 8 * (lane % 16), axis=1)
    return jnp.sum(jnp.where(lane // 16 == row, cells, 0.0), axis=0, keepdims=True)


def lookup(lab, table):
    out = []
    for c in range(4):
        scale = 1.0 if c < 2 else mass_scale
        val = [table[p, c] * F32(scale) for p in range(PHASES)]
        out.append(jnp.where(lab == 0, val[0], jnp.where(lab == 1, val[1], jnp.where(lab == 2, val[2], val[3]))))
    return out


def coeff_kernel(labels, table, near_out, far_out, buf, c1, c2, stack):
    for z in range(8):
        a, b = lookup(labels[2 * z], table), lookup(labels[2 * z + 1], table)
        for c in range(4):
            buf[c, z] = a[c] + b[c]
    for z in range(8):
        for c in range(4):
            c1[c, z] = pair_x(rows_paired(buf, (c, z), 0, 8), 1) * (0.125 if c < 2 else 0.5)
    for z in range(8):
        near_out[0, z] = interleave(c1[0, z], c1[1, z])
        near_out[1, z] = interleave(c1[2, z], c1[3, z])
    for c in range(4):
        scale = 0.125 if c < 2 else 0.5
        for z in range(4):
            buf[c, z, 0:8] = c1[c, 2 * z] + c1[c, 2 * z + 1]
        for z in range(4):
            c2[c, z] = pair_x(rows_paired(buf, (c, z), 0, 4), 2) * scale
        for z in range(2):
            buf[c, 4 + z, 0:4] = c2[c, 2 * z] + c2[c, 2 * z + 1]
        for z in range(2):
            stack[c // 2, (c % 2) * 4 + 2 * z : (c % 2) * 4 + 2 * z + 2] = (
                pair_x(rows_paired(buf, (c, 4 + z), 0, 2), 4) * scale
            )
    far_out[:, 0:LANES] = packed_row(stack[0])
    far_out[:, LANES : 2 * LANES] = packed_row(stack[1])


def fine_kernel(sizes, mid, left, right, table, rhs_out, v, f, tz, ty, tx, w, lab, s, m, g, first, buf):
    first_z = lax.axis_index("gz") * 16 - 4
    first_y = lax.axis_index("gy") * 16

    def load(z):
        for c, ref in ((0, f), (1, f), (2, None)):
            dst = lab.at[z] if ref is None else ref.at[c, z]
            dst[0:16] = mid[c, z]
            dst[16:20] = right[c, z]
            dst[20:24] = left[c, z]
        ok = inside(24, 20, z, first_z, first_y, *sizes)
        vals = lookup(lab[z], table)
        for c in (0, 1):
            s[c, z] = jnp.where(ok, vals[c], 0.0)
            m[c, z] = vals[2 + c]

    each(0, 24, load)

    def faces(z):
        ok = inside(24, 20, z, first_z, first_y, *sizes)
        put(first, z, times(make_faces(z, 1, ok, s, m, tz, ty, tx, w, g), pair(f, z)))

    each(1, 23, faces)
    each(2, 22, lambda z: put(v, z, swept(z, 1, first, f, tz, ty, tx, w)))

    def restrict(z):
        a = residual(2 * z + 4, 1, v, f, tz, ty, tx, g)
        b = residual(2 * z + 5, 1, v, f, tz, ty, tx, g)
        put(buf, z, add(a, b))

    each(0, 8, restrict, 1)

    def finish(z):
        re, im = (0.5 * pair_x(rows_paired(buf, (c, z), 0, 8), 1) for c in (0, 1))
        rhs_out[z] = interleave(re, im)

    each(0, 8, finish)


def middle_kernel(
    sizes, dmid, dleft, dright, bmid, bleft, bright,
    row_out, c_out, v, f, tz, ty, tx, w, tz2, ty2, tx2, w2,
    s, m, g, first, buf, s2, m2, f2, g2, first2, v2, buf2, stack,
):
    gz, gy = lax.axis_index("gz"), lax.axis_index("gy")

    def load(z):
        for lo, d, b in ((0, dmid, bmid), (8, dright, bright), (16, dleft, bleft)):
            for ref, q in ((s, d[0, z]), (m, d[1, z]), (f, b[z])):
                re, im = separate(q)
                ref[0, z, lo : lo + 8] = re
                ref[1, z, lo : lo + 8] = im

    each(0, 24, load)

    def faces(z):
        ok = inside(24, 16, z, gz * 8 - 8, gy * 8, *sizes[0])
        put(first, z, times(make_faces(z, 2, ok, s, m, tz, ty, tx, w, g), pair(f, z)))

    each(1, 23, faces)
    each(2, 22, lambda z: put(v, z, swept(z, 2, first, f, tz, ty, tx, w)))

    def coarser(dst, scale, z):
        for c in (0, 1):
            dst[c, z, 0:8] = scale * pair_x(rows_paired(buf, (c, z), 0, 8), 2)
            dst[c, z, 8:12] = jnp.zeros((4, LANES), F32)
            dst[c, z, 12:16] = scale * pair_x(rows_paired(buf, (c, z), 16, 4), 2)

    for src, dst, scale in ((s, s2, 0.125), (m, m2, 0.5)):
        each(0, 12, lambda z: put(buf, z, add(pair(src, 2 * z), pair(src, 2 * z + 1))))
        each(0, 12, lambda z: coarser(dst, scale, z))

    def restrict(z):
        put(buf, z, add(residual(2 * z, 2, v, f, tz, ty, tx, g), residual(2 * z + 1, 2, v, f, tz, ty, tx, g)))

    each(2, 10, restrict, 1)
    each(2, 10, lambda z: coarser(f2, 0.5, z))

    def faces2(z):
        ok = inside(16, 12, z, gz * 4 - 4, gy * 4, *sizes[1], dead=(8, 12))
        return make_faces(z, 4, ok, s2, m2, tz2, ty2, tx2, w2, g2)

    faces2(1)
    tz2[0, 0] = 0.5 * (s2[0, 0] + s2[0, 1])
    tz2[1, 0] = 0.5 * (s2[1, 0] + s2[1, 1])
    each(2, 10, lambda z: put(first2, z, times(faces2(z), pair(f2, z))))
    faces2(10)
    each(3, 9, lambda z: put(v2, z, swept(z, 4, first2, f2, tz2, ty2, tx2, w2)))
    which = lanes(4) & 3
    for z in range(4):
        a, b = pair(v2, z + 4), pair(f2, z + 4)
        c_out[z] = jnp.where(
            which < 2, jnp.where(which == 0, a[0][0:4], a[1][0:4]), jnp.where(which == 2, b[0][0:4], b[1][0:4])
        )
    for z in range(2):
        a = residual(2 * z + 4, 4, v2, f2, tz2, ty2, tx2, g2)
        b = residual(2 * z + 5, 4, v2, f2, tz2, ty2, tx2, g2)
        put(buf2, z, add(a, b))
    for z in range(2):
        for c in (0, 1):
            stack[4 * c + 2 * z : 4 * c + 2 * z + 2] = 0.5 * pair_x(rows_paired(buf2, (c, z), 0, 2), 4)
    row_out[...] = packed_row(stack[...])


def real_lanes(rows):
    return lanes(rows) < 64


def flip(q):
    return pltpu.roll(q, 64, 1)


def as_factors(q):
    real, other = real_lanes(q.shape[0]), flip(q)
    return jnp.where(real, q, other), jnp.where(real, -other, q)


def product(a, b, q):
    return a * q + b * flip(q)


def shifted_rows(q, k):
    edge = q.shape[0] - 1 if k > 0 else 0
    return jnp.where(row_ids(q.shape[0]) == edge, 0.0, ahead_y(q, k))


def near_level3(ref, p):
    q = ref[p]
    lane = lanes(q.shape[0])
    low_z, low_y, x = (lane & 32) == 0, (lane & 16) == 0, lane & 15
    qz, qy = swap_x(q, 32), swap_x(q, 16)
    return (
        jnp.where(low_z, qz, swap_x(ref[p + 1], 32)),
        jnp.where(low_z, swap_x(ref[p - 1], 32), qz),
        jnp.where(low_y, qy, shifted_rows(qy, 1)),
        jnp.where(low_y, shifted_rows(qy, -1), qy),
        jnp.where(x == 15, 0.0, ahead_x(q, 1)),
        jnp.where(x == 0, 0.0, ahead_x(q, -1)),
    )


def near_level4(ref, p):
    q = ref[p]
    x = lanes(q.shape[0]) & 15
    return (
        ref[p + 1],
        ref[p - 1],
        shifted_rows(q, 1),
        shifted_rows(q, -1),
        jnp.where(x >= 14, 0.0, ahead_x(q, 2)),
        jnp.where(x < 2, 0.0, ahead_x(q, -2)),
    )


def set_level(near, s, ps, m, t, w, g, p):
    here = s[ps]
    diag = m
    for i, other in enumerate(near(s, ps)):
        face = 0.5 * (here + other)
        diag = diag + face
        t[2 * i, p], t[2 * i + 1, p] = as_factors(face)
    real, other = real_lanes(here.shape[0]), flip(diag)
    inv = relax / (diag * diag + other * other)
    w[0, p] = jnp.where(real, diag, other) * inv
    w[1, p] = jnp.where(real, other, -diag) * inv
    if g is not None:
        g[0, p], g[1, p] = as_factors(diag)


def gathered_inflow(near, v, pv, t, p):
    total = None
    for i, q in enumerate(near(v, pv)):
        term = product(t[2 * i, p], t[2 * i + 1, p], q)
        total = term if total is None else total + term
    return total


def eightfold(q):
    return pair_x(pair_x(pair_x(q, 32), 16), 1)


def coarse_solve(counts, rhs, coef, s3, s4, t3, w3, g3, t4, w4, f4, va, vb, ea, eb, near_out):
    nz, ny = counts
    zero = jnp.zeros((ny, LANES), F32)
    for ref in (s3, s4, ea, eb):
        ref[0] = zero
        ref[nz + 1] = zero
    for ref in (va, vb):
        for p in (0, 1, 2, nz + 3, nz + 4, nz + 5):
            ref[p] = zero
    for p in (0, 1, nz + 2, nz + 3):
        for i in range(12):
            t3[i, p] = zero
        w3[0, p] = zero
        w3[1, p] = zero

    def load(p):
        q = coef[p, :, 0:LANES]
        s3[p + 1] = q
        s4[p + 1] = 0.125 * eightfold(q)

    each(0, nz, load)

    def setup(p):
        q = coef[p, :, LANES : 2 * LANES]
        set_level(near_level3, s3, p + 1, q, t3, w3, g3, p + 2)
        set_level(near_level4, s4, p + 1, 0.5 * eightfold(q), t4, w4, None, p)
        va[p + 3] = product(w3[0, p + 2], w3[1, p + 2], rhs[p])

    each(0, nz, setup, 1)

    def sweep3(src, p):
        gain = rhs[jnp.clip(p, 0, nz - 1)] + gathered_inflow(near_level3, src, p + 3, t3, p + 2)
        return keep * src[p + 3] + product(w3[0, p + 2], w3[1, p + 2], gain)

    def pre(p):
        vb[p + 3] = sweep3(va, p)

    each(0, nz, pre, 1)

    def restrict(p):
        gain = rhs[p] + gathered_inflow(near_level3, vb, p + 3, t3, p + 2)
        gain = 0.5 * eightfold(gain - product(g3[0, p + 2], g3[1, p + 2], vb[p + 3]))
        f4[p] = gain
        ea[p + 1] = product(w4[0, p], w4[1, p], gain)

    each(0, nz, restrict, 1)
    src, dst = ea, eb
    for sweep in range(COARSE_SWEEPS - 1):

        def relaxed(p, src=src, dst=dst):
            gain = f4[p] + gathered_inflow(near_level4, src, p + 1, t4, p)
            dst[p + 1] = keep * src[p + 1] + product(w4[0, p], w4[1, p], gain)

        each(0, nz, relaxed, 2)
        src, dst = dst, src

    def correct(p):
        vb[p + 3] = vb[p + 3] + src[p + 1]

    each(0, nz, correct)
    mine = lax.axis_index("gz")
    for d in range(-2, 3):
        va[mine + d + 3] = sweep3(vb, mine + d)
    for d in range(-1, 2):
        near_out[d + 1] = sweep3(va, mine + d)


def up_kernel(
    counts, rhs, coef, cmid, cleft, cright, tz2, ty2, tx2, w2, v1, f1, tz1, ty1, tx1, w1, v0, f0, tz0, ty0, tx0, w0, out,
    s3, s4, t3, w3, g3, t4, w4, f4, va, vb, ea, eb, near, a2, b2, f2, e1, a1, b1, e0, a0, b0,
):
    ny = counts[1]
    gy = lax.axis_index("gy")
    coarse_solve(counts, rhs, coef, s3, s4, t3, w3, g3, t4, w4, f4, va, vb, ea, eb, near)

    lane4, zero4 = lanes(4), jnp.zeros((4, LANES), F32)

    def unpack(z):
        for ref in (a2, f2):
            for c in (0, 1):
                ref[c, z, 8:12] = zero4
        for lo, src in ((0, cmid), (4, cright), (12, cleft)):
            q = src[z]
            turned = {k: ahead_x(q, k) if k else q for k in range(-3, 4)}
            for k, (ref, c) in enumerate(((a2, 0), (a2, 1), (f2, 0), (f2, 1))):
                val = turned[k]
                for i in range(1, 4):
                    val = jnp.where((lane4 & 3) == i, turned[k - i], val)
                ref[c, z, lo : lo + 4] = val

    each(0, 12, unpack)
    r16, l16 = row_ids(16), lanes(16)
    cell = 16 * ((r16 // 2) & 1) + l16 // 8
    for d in range(3):
        own = near[d, pl.ds(gy, 1), :]
        after = near[d, pl.ds(jnp.minimum(gy + 1, ny - 1), 1), :] * jnp.where(gy == ny - 1, 0.0, 1.0)
        before = near[d, pl.ds(jnp.maximum(gy - 1, 0), 1), :] * jnp.where(gy == 0, 0.0, 1.0)
        rows = jnp.where(r16 < 4, own, jnp.where(r16 < 8, after, jnp.where(r16 < 12, 0.0, before)))
        for c in (0, 1):
            for zz in (0, 1):
                corr = jnp.take_along_axis(rows, cell + (64 * c + 32 * zz), axis=1)
                for z in (4 * d + 2 * zz, 4 * d + 2 * zz + 1):
                    a2[c, z] = a2[c, z] + corr

    each(1, 11, lambda z: put(b2, z, swept(z, 4, a2, f2, tz2, ty2, tx2, w2)))
    each(2, 10, lambda z: put(a2, z, swept(z, 4, b2, f2, tz2, ty2, tx2, w2)))

    def widen1(z):
        for c in (0, 1):
            q = a2[c, z]
            for k in (0, 1):
                e1.at[c, z][pl.ds(k, 8, stride=2), :] = q[0:8]
                e1.at[c, z][pl.ds(16 + k, 4, stride=2), :] = q[12:16]

    each(2, 10, widen1)
    each(5, 19, lambda z: put(a1, z, add(pair(v1, z), pair(e1, z // 2))))
    each(6, 18, lambda z: put(b1, z, swept(z, 2, a1, f1, tz1, ty1, tx1, w1)))
    each(7, 17, lambda z: put(a1, z, swept(z, 2, b1, f1, tz1, ty1, tx1, w1)))

    def widen0(z):
        for c in (0, 1):
            q = a1[c, z]
            for k in (0, 1):
                e0.at[c, z][pl.ds(k, 8, stride=2), :] = q[0:8]
                e0.at[c, z][pl.ds(16 + k, 2, stride=2), :] = q[8:10]
                e0.at[c, z][pl.ds(20 + k, 2, stride=2), :] = q[22:24]

    each(7, 17, widen0)
    each(2, 22, lambda z: put(a0, z, add(pair(v0, z), pair(e0, z // 2 + 6))))
    each(3, 21, lambda z: put(b0, z, swept(z, 1, a0, f0, tz0, ty0, tx0, w0)))

    def last(z):
        q = swept(z, 1, b0, f0, tz0, ty0, tx0, w0)
        out[0, z - 4] = q[0][0:16]
        out[1, z - 4] = q[1][0:16]

    each(4, 20, last)


def spec_all(n, smem=()):
    return [pl.BlockSpec(memory_space=pltpu.SMEM if i in smem else pltpu.VMEM) for i in range(n)]


def run(kernel, name, args, outs, scratch, smem=()):
    shapes = [jax.ShapeDtypeStruct(s, F32) for s in outs]
    return pl.pallas_call(
        kernel,
        name=name,
        out_shape=shapes,
        in_specs=spec_all(len(args), smem),
        out_specs=spec_all(len(outs)),
        scratch_shapes=[pltpu.VMEM(s, F32) for s in scratch],
        compiler_params=pltpu.CompilerParams(vmem_limit_bytes=VMEM_BYTES),
    )(*args)


def shifts(axis):
    n = lax.axis_size(axis)
    up = [(i, i + 1) for i in range(n - 1)]
    return up, [(j, i) for i, j in up]


def around(block, axis, dim, width):
    up, down = shifts(axis)
    size = block.shape[dim]
    before = lax.ppermute(lax.slice_in_dim(block, size - width, size, axis=dim), axis, up)
    after = lax.ppermute(lax.slice_in_dim(block, 0, width, axis=dim), axis, down)
    return before, after


def window(block, dim, width):
    before, after = around(block, "gz", dim, width)
    mid = jnp.concatenate([before, block, after], axis=dim)
    left, right = around(mid, "gy", dim + 1, width)
    return mid, left, right


def body(source, labels, phase_table):
    nz, ny = lax.axis_size("gz"), lax.axis_size("gy")
    lab = labels.astype(jnp.int32)
    near_c, far_c = run(
        coeff_kernel, "coefficients", (lab, phase_table),
        [(2, 8, 8, LANES), (1, 2 * LANES)],
        [(4, 8, 16, LANES), (4, 8, 8, LANES), (4, 4, 4, LANES), (2, 8, LANES)], smem=(1,),
    )
    far_c = lax.all_gather(far_c, ("gz", "gy"), axis=0, tiled=True).reshape(nz, ny, 2 * LANES)
    fine = jnp.concatenate([source, labels.astype(F32)[None]], axis=0)
    coef1 = window(near_c, 1, 8)

    win = (2, 24, 24, LANES)
    rhs1, *state0 = run(
        lambda *refs: fine_kernel((16 * nz, 16 * ny), *refs), "fine_down", (*window(fine, 1, 4), phase_table),
        [(8, 8, LANES)] + [win] * 6,
        [(24, 24, LANES)] + [win] * 4 + [(2, 8, 24, LANES)], smem=(3,),
    )
    win2 = (2, 12, 16, LANES)
    row, c_own, *state = run(
        lambda *refs: middle_kernel(((8 * nz, 8 * ny), (4 * nz, 4 * ny)), *refs), "middle_down",
        (*coef1, *window(rhs1, 0, 8)),
        [(1, LANES), (4, 4, LANES)] + [win] * 6 + [win2] * 4,
        [win] * 4 + [(2, 12, 24, LANES)] + [win2] * 6 + [(2, 2, 16, LANES), (8, LANES)],
    )
    state1, state2 = state[:6], state[6:]
    rhs3 = lax.all_gather(row, ("gz", "gy"), axis=0, tiled=True).reshape(nz, ny, LANES)
    cwin = window(c_own, 0, 4)

    def whole(n, pad):
        return (n, nz + 2 * pad, ny, LANES)

    return run(
        lambda *refs: up_kernel((nz, ny), *refs), "coarse_and_up",
        (rhs3, far_c, *cwin, *state2, *state1, *state0),
        [(2, 16, 16, LANES)],
        [whole(1, 1)[1:]] * 2
        + [whole(12, 2), whole(2, 2), whole(2, 2), whole(12, 0), whole(2, 0), whole(1, 0)[1:]]
        + [whole(1, 3)[1:]] * 2 + [whole(1, 1)[1:]] * 2 + [(3, ny, LANES)]
        + [win2] * 3 + [(2, 12, 24, LANES), win, win, win, win, win],
    )[0]


def solution(mesh):
    in_specs = (P(None, "gz", "gy", None), P("gz", "gy", None), P())
    out_specs = P(None, "gz", "gy", None)
    return jax.shard_map(body, mesh=mesh, in_specs=in_specs, out_specs=out_specs, check_vma=False)
```

time: 584 us -> 346 us (0.59)
  the two profiles are of different devices: /device:TPU:25 before, /device:TPU:1 now
where the time goes in v1:
time: 346 us; the launch traced here: 345 us
  blocking collectives  232 us (67%)
  Pallas kernels  50.8 us (15%)
  starting transfers between devices  45.6 us (13%)
  waiting for transfers between devices  14.6 us (4%)
    all_gather x1, blocking collectives, body(): lax.all_gather(far_c, ('gz', 'gy'), axis=0, tiled=True)  124 us
    all_gather x1, blocking collectives, body(): lax.all_gather(row, ('gz', 'gy'), axis=0, tiled=True).reshape(nz, ny, LANES)  108 us
    pallas_call x4, Pallas kernels, run(): pl.pallas_call(kernel, name=name, out_shape=shapes, in_specs=spec_all(len...  50.8 us
    ppermute x8, starting transfers between devices, around(): lax.ppermute(lax.slice_in_dim(block, size - width, size, axis=dim), axis,...  30.6 us
    ppermute x8, starting transfers between devices, around(): lax.ppermute(lax.slice_in_dim(block, 0, width, axis=dim), axis, down)  15 us
    ppermute x8, waiting for transfers between devices, around(): lax.ppermute(lax.slice_in_dim(block, 0, width, axis=dim), axis, down)  14.6 us
  transfers between devices with their start and end apart: 16, of which 4 were waited for; matrix products, arithmetic and copies ran while one was open for 0% of the time, Pallas kernels for 2%

profile of v1, /device:TPU:1, one launch (start us, length us, event | category | flops | bytes accessed | tf_op | source)
XLA Modules:
  0.0 344.9 jit_solution(6501424796322039066)
XLA Ops:
  1.0 1.4 collective-permute-start.5
  2.5 5.0 %collective-permute-start.4 = (f32[3,4,16,128]{3,2,1,0:T(8,128)S(1)}, f32[3,4,16,128]{3,2,1,0:T(8,128)S(1)}, u32[]{:S(2)}, u32[]{:S(2)}) collective-permute-start(f32[3,4,16,128]{3,2,1,0:T(8,128)S(1)} %get-tuple-element.49), channel_id=1, source_target_pairs={{0,32},{32,64},{64,96},{96,128},{128,160},{160,192},{192,224},{224... | collective-permute-start | bytes 294920 | tf_op jit(solution)/shard_map/ppermute | solution.py:538
  8.5 3.5 %collective-permute-start = (f32[2,8,8,128]{3,2,1,0:T(8,128)S(1)}, f32[2,8,8,128]{3,2,1,0:T(8,128)S(1)}, u32[]{:S(2)}, u32[]{:S(2)}) collective-permute-start(f32[2,8,8,128]{3,2,1,0:T(8,128)S(1)} %get-tuple-element.26), channel_id=1, source_target_pairs={{0,32},{32,64},{64,96},{96,128},{128,160},{160,192},{192,224},{224... | collective-permute-start | bytes 196616 | tf_op jit(solution)/shard_map/ppermute | solution.py:538
  12.1 1.3 collective-permute-start.1
  13.5 4.4 %collective-permute-start.6 = (f32[3,24,4,128]{3,2,1,0:T(4,128)S(1)}, f32[3,24,4,128]{3,2,1,0:T(4,128)S(1)}, u32[]{:S(2)}, u32[]{:S(2)}) collective-permute-start(f32[3,24,4,128]{3,2,1,0:T(4,128)S(1)} %get-tuple-element.48), channel_id=1, source_target_pairs={{0,1},{1,2},{2,3},{3,4},{4,5},{5,6},{6,7},{7,8},{8,9},{9,10},{10,1... | collective-permute-start | bytes 442376 | tf_op jit(solution)/shard_map/ppermute | solution.py:538
  17.9 3.6 %collective-permute-start.7 = (f32[3,24,4,128]{3,2,1,0:T(4,128)S(1)}, f32[3,24,4,128]{3,2,1,0:T(4,128)S(1)}, u32[]{:S(2)}, u32[]{:S(2)}) collective-permute-start(f32[3,24,4,128]{3,2,1,0:T(4,128)S(1)} %get-tuple-element.47), channel_id=1, source_target_pairs={{1,0},{2,1},{3,2},{4,3},{5,4},{6,5},{7,6},{8,7},{9,8},{10,9},{11,1... | collective-permute-start | bytes 442376 | tf_op jit(solution)/shard_map/ppermute | solution.py:539
  21.6 2.8 collective-permute-done.7.refs_2_
  24.4 4.4 %fine_down.1 = (f32[8,8,128]{2,1,0:T(8,128)S(1)}, f32[2,24,24,128]{3,2,1,0:T(8,128)S(1)}, f32[2,24,24,128]{3,2,1,0:T(8,128)S(1)}, f32[2,24,24,128]{3,2,1,0:T(8,1...) custom-call(f32[3,24,16,128]{3,2,1,0:T(8,128)S(1)} %pad_maximum_fusion.refs_, ...), custom_call_target="tpu_custom_call" | custom-call | tf_op jit(solution)/shard_map/fine_down/pallas_call | solution.py:518
  28.8 4.3 %collective-permute-start.8 = (f32[8,8,128]{2,1,0:T(8,128)S(1)}, f32[8,8,128]{2,1,0:T(8,128)S(1)}, u32[]{:S(2)}, u32[]{:S(2)}) collective-permute-start(f32[8,8,128]{2,1,0:T(8,128)S(1)} %get-tuple-element.27), channel_id=1, source_target_pairs={{0,32},{32,64},{64,96},{96,128},{128,160},{160,192},{192,224},{224... | collective-permute-start | bytes 98312 | tf_op jit(solution)/shard_map/ppermute | solution.py:538
  33.1 2.0 collective-permute-start.2
  35.2 2.3 collective-permute-start.3
  37.5 1.3 collective-permute-start.9
  38.8 4.6 %collective-permute-done.9 = f32[8,8,128]{2,1,0:T(8,128)S(1)} collective-permute-done((f32[8,8,128]{2,1,0:T(8,128)S(1)}, f32[8,8,128]{2,1,0:T(8,128)S(1)}, u32[]{:S(2)}, u32[]{:S(2)}) %collective-permute-start.9) | collective-permute-done | bytes 32800 | tf_op jit(solution)/shard_map/ppermute | solution.py:539
  43.4 4.1 %collective-permute-start.10 = (f32[24,8,128]{2,1,0:T(8,128)S(1)}, f32[24,8,128]{2,1,0:T(8,128)S(1)}, u32[]{:S(2)}, u32[]{:S(2)}) collective-permute-start(f32[24,8,128]{2,1,0:T(8,128)S(1)} %constant_dynamic-update-slice_fusion.3.refs_3_), channel_id=1, source_target_pairs={{0,1},{1,2},{2,3},{3,4},{4,5},{5,6},{6,7},{7,8},{8,9},{9,10},{10,1... | collective-permute-start | bytes 294920 | tf_op jit(solution)/shard_map/ppermute | solution.py:538
  47.6 1.9 collective-permute-start.11
  49.5 4.0 %collective-permute-done.11.refs_5_ = f32[24,8,128]{2,1,0:T(8,128)S(1)} collective-permute-done((f32[24,8,128]{2,1,0:T(8,128)S(1)}, f32[24,8,128]{2,1,0:T(8,128)S(1)}, u32[]{:S(2)}, u32[]{:S(2)}) %collective-permute-start.11) | collective-permute-done | bytes 98336 | tf_op jit(solution)/shard_map/ppermute | solution.py:539
  53.5 7.0 %middle_down.1 = (f32[1,128]{1,0:T(1,128)S(1)}, f32[4,4,128]{2,1,0:T(4,128)S(1)}, f32[2,24,24,128]{3,2,1,0:T(8,128)S(1)}, f32[2,24,24,128]{3,2,1,0:T(8,128)S(1)}...) custom-call(f32[2,24,8,128]{3,2,1,0:T(8,128)S(1)} %constant_dynamic-, ...), custom_call_target="tpu_custom_call" | custom-call | tf_op jit(solution)/shard_map/middle_down/pallas_call | solution.py:518
  60.5 3.6 %collective-permute-start.12 = (f32[4,4,128]{2,1,0:T(4,128)S(1)}, f32[4,4,128]{2,1,0:T(4,128)S(1)}, u32[]{:S(2)}, u32[]{:S(2)}) collective-permute-start(f32[4,4,128]{2,1,0:T(4,128)S(1)} %get-tuple-element.30), channel_id=1, source_target_pairs={{0,32},{32,64},{64,96},{96,128},{128,160},{160,192},{192,224},{224... | collective-permute-start | bytes 24584 | tf_op jit(solution)/shard_map/ppermute | solution.py:538
  64.2 123.9 %all-gather.1 = f32[512,1,256]{2,1,0:T(1,128)S(1)} all-gather(f32[1,1,256]{2,1,0:T(1,128)S(1)} %bitcast.8), channel_id=1, replica_groups=mesh['gz'=16,'gy'=32] {'gz','gy'}, dimensions={0}, use_global_device_ids=true | all-gather | bytes 525312 | tf_op jit(solution)/shard_map/all_gather | solution.py:558
  189.4 3.1 collective-permute-done.13
  192.6 3.5 %collective-permute-start.14 = (f32[12,4,128]{2,1,0:T(4,128)S(1)}, f32[12,4,128]{2,1,0:T(4,128)S(1)}, u32[]{:S(2)}, u32[]{:S(2)}) collective-permute-start(f32[12,4,128]{2,1,0:T(4,128)S(1)} %constant_dynamic-update-slice_fusion.6.refs_2_), channel_id=1, source_target_pairs={{0,1},{1,2},{2,3},{3,4},{4,5},{5,6},{6,7},{7,8},{8,9},{9,10},{10,1... | collective-permute-start | bytes 73736 | tf_op jit(solution)/shard_map/ppermute | solution.py:538
  196.1 1.9 collective-permute-start.15
  198.1 108.5 %all-gather = f32[512,1,128]{2,1,0:T(1,128)S(1)} all-gather(f32[1,1,128]{2,1,0:T(1,128)S(1)} %bitcast.9), channel_id=1, replica_groups=mesh['gz'=16,'gy'=32] {'gz','gy'}, dimensions={0}, use_global_device_ids=true | all-gather | bytes 262656 | tf_op jit(solution)/shard_map/all_gather | solution.py:576
  306.5 38.4 %coarse_and_up.1 = f32[2,16,16,128]{3,2,1,0:T(8,128)} custom-call(f32[16,32,128]{2,1,0:T(8,128)S(1)} %bitcast.7, f32[16,32,256]{2,1,0:T(8,128)S(1)} %bitcast.6, f32[12,4,128]{2,1,0:T(4,128)S(1)} %constant_dynamic-update-slice_fusion.6.refs_2_, f32[12,4,128]{2,1,0:T(4,128)S(1)} %collective-permute-done.14.refs_3_, ...), custom_call_target="tpu_custom_call" | custom-call | tf_op jit(solution)/shard_map/coarse_and_up/pallas_call | solution.py:518
  (34 shorter events, 3.6 us)
Async XLA Ops:
  0.0 1.0 copy-start.2
  1.0 6.5 %copy-start = (s32[16,16,128]{2,1,0:T(8,128)S(1)}, s32[16,16,128]{2,1,0:T(8,128)}, u32[]{:S(2)}) copy-start(s32[16,16,128]{2,1,0:T(8,128)} %labels.1) | copy-start | bytes 393220
  1.0 6.5 %copy-start.1 = (f32[4,4]{1,0:T(4,128)S(1)}, f32[4,4]{1,0:T(4,128)}, u32[]{:S(2)}) copy-start(f32[4,4]{1,0:T(4,128)} %refs_3_.1) | copy-start | bytes 196
  1.0 12.3 %collective-permute-start.5 = (f32[3,4,16,128]{3,2,1,0:T(8,128)S(1)}, f32[3,4,16,128]{3,2,1,0:T(8,128)S(1)}, u32[]{:S(2)}, u32[]{:S(2)}) collective-permute-start(f32[3,4,16,128]{3,2,1,0:T(8,128)S(1)} %get-tuple-element.50), channel_id=1, source_target_pairs={{32,0},{64,32},{96,64},{128,96},{160,128},{192,160},{224,192},{256... | collective-permute-start | bytes 294920 | tf_op jit(solution)/shard_map/ppermute | solution.py:539
  2.5 10.9 %collective-permute-start.4 = (f32[3,4,16,128]{3,2,1,0:T(8,128)S(1)}, f32[3,4,16,128]{3,2,1,0:T(8,128)S(1)}, u32[]{:S(2)}, u32[]{:S(2)}) collective-permute-start(f32[3,4,16,128]{3,2,1,0:T(8,128)S(1)} %get-tuple-element.49), channel_id=1, source_target_pairs={{0,32},{32,64},{64,96},{96,128},{128,160},{160,192},{192,224},{224... | collective-permute-start | bytes 294920 | tf_op jit(solution)/shard_map/ppermute | solution.py:538
  8.5 13.0 %collective-permute-start = (f32[2,8,8,128]{3,2,1,0:T(8,128)S(1)}, f32[2,8,8,128]{3,2,1,0:T(8,128)S(1)}, u32[]{:S(2)}, u32[]{:S(2)}) collective-permute-start(f32[2,8,8,128]{3,2,1,0:T(8,128)S(1)} %get-tuple-element.26), channel_id=1, source_target_pairs={{0,32},{32,64},{64,96},{96,128},{128,160},{160,192},{192,224},{224... | collective-permute-start | bytes 196616 | tf_op jit(solution)/shard_map/ppermute | solution.py:538
  12.1 21.0 %collective-permute-start.1 = (f32[2,8,8,128]{3,2,1,0:T(8,128)S(1)}, f32[2,8,8,128]{3,2,1,0:T(8,128)S(1)}, u32[]{:S(2)}, u32[]{:S(2)}) collective-permute-start(f32[2,8,8,128]{3,2,1,0:T(8,128)S(1)} %get-tuple-element.26), channel_id=1, source_target_pairs={{32,0},{64,32},{96,64},{128,96},{160,128},{192,160},{224,192},{256... | collective-permute-start | bytes 196616 | tf_op jit(solution)/shard_map/ppermute | solution.py:539
  13.5 8.1 %collective-permute-start.6 = (f32[3,24,4,128]{3,2,1,0:T(4,128)S(1)}, f32[3,24,4,128]{3,2,1,0:T(4,128)S(1)}, u32[]{:S(2)}, u32[]{:S(2)}) collective-permute-start(f32[3,24,4,128]{3,2,1,0:T(4,128)S(1)} %get-tuple-element.48), channel_id=1, source_target_pairs={{0,1},{1,2},{2,3},{3,4},{4,5},{5,6},{6,7},{7,8},{8,9},{9,10},{10,1... | collective-permute-start | bytes 442376 | tf_op jit(solution)/shard_map/ppermute | solution.py:538
  17.9 6.5 %collective-permute-start.7 = (f32[3,24,4,128]{3,2,1,0:T(4,128)S(1)}, f32[3,24,4,128]{3,2,1,0:T(4,128)S(1)}, u32[]{:S(2)}, u32[]{:S(2)}) collective-permute-start(f32[3,24,4,128]{3,2,1,0:T(4,128)S(1)} %get-tuple-element.47), channel_id=1, source_target_pairs={{1,0},{2,1},{3,2},{4,3},{5,4},{6,5},{7,6},{8,7},{9,8},{10,9},{11,1... | collective-permute-start | bytes 442376 | tf_op jit(solution)/shard_map/ppermute | solution.py:539
  28.8 10.0 %collective-permute-start.8 = (f32[8,8,128]{2,1,0:T(8,128)S(1)}, f32[8,8,128]{2,1,0:T(8,128)S(1)}, u32[]{:S(2)}, u32[]{:S(2)}) collective-permute-start(f32[8,8,128]{2,1,0:T(8,128)S(1)} %get-tuple-element.27), channel_id=1, source_target_pairs={{0,32},{32,64},{64,96},{96,128},{128,160},{160,192},{192,224},{224... | collective-permute-start | bytes 98312 | tf_op jit(solution)/shard_map/ppermute | solution.py:538
  33.1 16.4 %collective-permute-start.2 = (f32[2,24,8,128]{3,2,1,0:T(8,128)S(1)}, f32[2,24,8,128]{3,2,1,0:T(8,128)S(1)}, u32[]{:S(2)}, u32[]{:S(2)}) collective-permute-start(f32[2,24,8,128]{3,2,1,0:T(8,128)S(1)} %constant_dynamic-update-slice_fusion.refs_0_), channel_id=1, source_target_pairs={{0,1},{1,2},{2,3},{3,4},{4,5},{5,6},{6,7},{7,8},{8,9},{9,10},{10,1... | collective-permute-start | bytes 589832 | tf_op jit(solution)/shard_map/ppermute | solution.py:538
  35.2 14.3 %collective-permute-start.3 = (f32[2,24,8,128]{3,2,1,0:T(8,128)S(1)}, f32[2,24,8,128]{3,2,1,0:T(8,128)S(1)}, u32[]{:S(2)}, u32[]{:S(2)}) collective-permute-start(f32[2,24,8,128]{3,2,1,0:T(8,128)S(1)} %constant_dynamic-update-slice_fusion.refs_0_), channel_id=1, source_target_pairs={{1,0},{2,1},{3,2},{4,3},{5,4},{6,5},{7,6},{8,7},{9,8},{10,9},{11,1... | collective-permute-start | bytes 589832 | tf_op jit(solution)/shard_map/ppermute | solution.py:539
  37.5 6.0 %collective-permute-start.9 = (f32[8,8,128]{2,1,0:T(8,128)S(1)}, f32[8,8,128]{2,1,0:T(8,128)S(1)}, u32[]{:S(2)}, u32[]{:S(2)}) collective-permute-start(f32[8,8,128]{2,1,0:T(8,128)S(1)} %get-tuple-element.27), channel_id=1, source_target_pairs={{32,0},{64,32},{96,64},{128,96},{160,128},{192,160},{224,192},{256... | collective-permute-start | bytes 98312 | tf_op jit(solution)/shard_map/ppermute | solution.py:539
  43.4 6.1 %collective-permute-start.10 = (f32[24,8,128]{2,1,0:T(8,128)S(1)}, f32[24,8,128]{2,1,0:T(8,128)S(1)}, u32[]{:S(2)}, u32[]{:S(2)}) collective-permute-start(f32[24,8,128]{2,1,0:T(8,128)S(1)} %constant_dynamic-update-slice_fusion.3.refs_3_), channel_id=1, source_target_pairs={{0,1},{1,2},{2,3},{3,4},{4,5},{5,6},{6,7},{7,8},{8,9},{9,10},{10,1... | collective-permute-start | bytes 294920 | tf_op jit(solution)/shard_map/ppermute | solution.py:538
  47.6 5.9 %collective-permute-start.11 = (f32[24,8,128]{2,1,0:T(8,128)S(1)}, f32[24,8,128]{2,1,0:T(8,128)S(1)}, u32[]{:S(2)}, u32[]{:S(2)}) collective-permute-start(f32[24,8,128]{2,1,0:T(8,128)S(1)} %constant_dynamic-update-slice_fusion.3.refs_3_), channel_id=1, source_target_pairs={{1,0},{2,1},{3,2},{4,3},{5,4},{6,5},{7,6},{8,7},{9,8},{10,9},{11,1... | collective-permute-start | bytes 294920 | tf_op jit(solution)/shard_map/ppermute | solution.py:539
  60.5 128.9 %collective-permute-start.12 = (f32[4,4,128]{2,1,0:T(4,128)S(1)}, f32[4,4,128]{2,1,0:T(4,128)S(1)}, u32[]{:S(2)}, u32[]{:S(2)}) collective-permute-start(f32[4,4,128]{2,1,0:T(4,128)S(1)} %get-tuple-element.30), channel_id=1, source_target_pairs={{0,32},{32,64},{64,96},{96,128},{128,160},{160,192},{192,224},{224... | collective-permute-start | bytes 24584 | tf_op jit(solution)/shard_map/ppermute | solution.py:538
  188.1 4.5 %collective-permute-start.13 = (f32[4,4,128]{2,1,0:T(4,128)S(1)}, f32[4,4,128]{2,1,0:T(4,128)S(1)}, u32[]{:S(2)}, u32[]{:S(2)}) collective-permute-start(f32[4,4,128]{2,1,0:T(4,128)S(1)} %get-tuple-element.30), channel_id=1, source_target_pairs={{32,0},{64,32},{96,64},{128,96},{160,128},{192,160},{224,192},{256... | collective-permute-start | bytes 24584 | tf_op jit(solution)/shard_map/ppermute | solution.py:539
  192.6 114.0 %collective-permute-start.14 = (f32[12,4,128]{2,1,0:T(4,128)S(1)}, f32[12,4,128]{2,1,0:T(4,128)S(1)}, u32[]{:S(2)}, u32[]{:S(2)}) collective-permute-start(f32[12,4,128]{2,1,0:T(4,128)S(1)} %constant_dynamic-update-slice_fusion.6.refs_2_), channel_id=1, source_target_pairs={{0,1},{1,2},{2,3},{3,4},{4,5},{5,6},{6,7},{7,8},{8,9},{9,10},{10,1... | collective-permute-start | bytes 73736 | tf_op jit(solution)/shard_map/ppermute | solution.py:538
  196.1 110.4 %collective-permute-start.15 = (f32[12,4,128]{2,1,0:T(4,128)S(1)}, f32[12,4,128]{2,1,0:T(4,128)S(1)}, u32[]{:S(2)}, u32[]{:S(2)}) collective-permute-start(f32[12,4,128]{2,1,0:T(4,128)S(1)} %constant_dynamic-update-slice_fusion.6.refs_2_), channel_id=1, source_target_pairs={{1,0},{2,1},{3,2},{4,3},{5,4},{6,5},{7,6},{8,7},{9,8},{10,9},{11,1... | collective-permute-start | bytes 73736 | tf_op jit(solution)/shard_map/ppermute | solution.py:539

commit v2 on v1

--- a/solution.py
+++ b/solution.py
@@ -48,7 +48,7 @@
     return jnp.where(even, q, ahead_x(q, -1)), jnp.where(even, ahead_x(q, 1), q)
 
 
-def each(lo, hi, body, step=2):
+def each(lo, hi, body, step=4):
     full = (hi - lo) // step
 
     def run(i, carry):
@@ -189,7 +189,7 @@
     far_out[:, LANES : 2 * LANES] = packed_row(stack[1])
 
 
-def fine_kernel(sizes, mid, left, right, table, rhs_out, v, f, tz, ty, tx, w, lab, s, m, g, first, buf):
+def fine_kernel(sizes, mid, left, right, table, near_c, msg_out, v, f, tz, ty, tx, w, lab, s, m, g, first, buf):
     first_z = lax.axis_index("gz") * 16 - 4
     first_y = lax.axis_index("gy") * 16
 
@@ -219,26 +219,28 @@
         b = residual(2 * z + 5, 1, v, f, tz, ty, tx, g)
         put(buf, z, add(a, b))
 
-    each(0, 8, restrict, 1)
+    each(0, 8, restrict, 2)
 
     def finish(z):
         re, im = (0.5 * pair_x(rows_paired(buf, (c, z), 0, 8), 1) for c in (0, 1))
-        rhs_out[z] = interleave(re, im)
+        msg_out[2, z] = interleave(re, im)
+        msg_out[0, z] = near_c[0, z]
+        msg_out[1, z] = near_c[1, z]
 
     each(0, 8, finish)
 
 
 def middle_kernel(
-    sizes, dmid, dleft, dright, bmid, bleft, bright,
+    sizes, mid, left, right, far_c,
     row_out, c_out, v, f, tz, ty, tx, w, tz2, ty2, tx2, w2,
     s, m, g, first, buf, s2, m2, f2, g2, first2, v2, buf2, stack,
 ):
     gz, gy = lax.axis_index("gz"), lax.axis_index("gy")
 
     def load(z):
-        for lo, d, b in ((0, dmid, bmid), (8, dright, bright), (16, dleft, bleft)):
-            for ref, q in ((s, d[0, z]), (m, d[1, z]), (f, b[z])):
-                re, im = separate(q)
+        for lo, src in ((0, mid), (8, right), (16, left)):
+            for i, ref in enumerate((s, m, f)):
+                re, im = separate(src[i, z])
                 ref[0, z, lo : lo + 8] = re
                 ref[1, z, lo : lo + 8] = im
 
@@ -264,7 +266,7 @@
     def restrict(z):
         put(buf, z, add(residual(2 * z, 2, v, f, tz, ty, tx, g), residual(2 * z + 1, 2, v, f, tz, ty, tx, g)))
 
-    each(2, 10, restrict, 1)
+    each(2, 10, restrict, 2)
     each(2, 10, lambda z: coarser(f2, 0.5, z))
 
     def faces2(z):
@@ -290,7 +292,8 @@
     for z in range(2):
         for c in (0, 1):
             stack[4 * c + 2 * z : 4 * c + 2 * z + 2] = 0.5 * pair_x(rows_paired(buf2, (c, z), 0, 2), 4)
-    row_out[...] = packed_row(stack[...])
+    row_out[:, 0:LANES] = packed_row(stack[...])
+    row_out[:, LANES : 3 * LANES] = far_c[...]
 
 
 def real_lanes(rows):
@@ -303,11 +306,17 @@
 
 def as_factors(q):
     real, other = real_lanes(q.shape[0]), flip(q)
-    return jnp.where(real, q, other), jnp.where(real, -other, q)
-
-
-def product(a, b, q):
-    return a * q + b * flip(q)
+    return jnp.where(real, q, other), jnp.where(real, other, -q)
+
+
+def product(t, q):
+    return t[0] * q + flip(t[1] * q)
+
+
+def inverse_factors(diag):
+    real, other = real_lanes(diag.shape[0]), flip(diag)
+    inv = relax / (diag * diag + other * other)
+    return jnp.where(real, diag, other) * inv, jnp.where(real, -other, diag) * inv
 
 
 def shifted_rows(q, k):
@@ -315,135 +324,198 @@
     return jnp.where(row_ids(q.shape[0]) == edge, 0.0, ahead_y(q, k))
 
 
-def near_level3(ref, p):
-    q = ref[p]
-    lane = lanes(q.shape[0])
+def near_level3(planes):
+    n = planes[0].shape[0]
+    lane = lanes(n)
     low_z, low_y, x = (lane & 32) == 0, (lane & 16) == 0, lane & 15
-    qz, qy = swap_x(q, 32), swap_x(q, 16)
-    return (
-        jnp.where(low_z, qz, swap_x(ref[p + 1], 32)),
-        jnp.where(low_z, swap_x(ref[p - 1], 32), qz),
-        jnp.where(low_y, qy, shifted_rows(qy, 1)),
-        jnp.where(low_y, shifted_rows(qy, -1), qy),
-        jnp.where(x == 15, 0.0, ahead_x(q, 1)),
-        jnp.where(x == 0, 0.0, ahead_x(q, -1)),
-    )
-
-
-def near_level4(ref, p):
-    q = ref[p]
-    x = lanes(q.shape[0]) & 15
-    return (
-        ref[p + 1],
-        ref[p - 1],
-        shifted_rows(q, 1),
-        shifted_rows(q, -1),
-        jnp.where(x >= 14, 0.0, ahead_x(q, 2)),
-        jnp.where(x < 2, 0.0, ahead_x(q, -2)),
-    )
-
-
-def set_level(near, s, ps, m, t, w, g, p):
-    here = s[ps]
+    turned = [swap_x(q, 16) for q in planes]
+    out = []
+    for i, q in enumerate(planes[1:-1]):
+        qz = swap_x(q, 32)
+        out.append(
+            (
+                jnp.where(low_y, turned[i + 1], turned[i + 2]),
+                jnp.where(low_y, turned[i], turned[i + 1]),
+                jnp.where(low_z, qz, shifted_rows(qz, 1)),
+                jnp.where(low_z, shifted_rows(qz, -1), qz),
+                jnp.where(x == 15, 0.0, ahead_x(q, 1)),
+                jnp.where(x == 0, 0.0, ahead_x(q, -1)),
+            )
+        )
+    return out
+
+
+def slot_lanes(lane, slot):
+    return (lane & 78) | ((slot & 4) << 3) | ((slot & 2) << 3) | (slot & 1)
+
+
+def slot_of(lane):
+    return ((lane >> 3) & 4) | ((lane >> 3) & 2) | (lane & 1)
+
+
+def near_level4(groups):
+    n = groups[0].shape[0]
+    lane = lanes(n)
+    slot, x = slot_of(lane), lane & 14
+    nxt, prv = slot_lanes(lane, slot + 1), slot_lanes(lane, slot + 7)
+    zero = jnp.zeros_like(groups[0])
+    up = [jnp.take_along_axis(q, nxt, axis=1) for q in groups] + [zero]
+    down = [zero] + [jnp.take_along_axis(q, prv, axis=1) for q in groups]
+    return [
+        (
+            jnp.where(slot == 7, up[i + 1], up[i]),
+            jnp.where(slot == 0, down[i], down[i + 1]),
+            shifted_rows(q, 1),
+            shifted_rows(q, -1),
+            jnp.where(x == 14, 0.0, ahead_x(q, 2)),
+            jnp.where(x == 0, 0.0, ahead_x(q, -2)),
+        )
+        for i, q in enumerate(groups)
+    ]
+
+
+def set_level(here, near, m, t, w, g, p):
     diag = m
-    for i, other in enumerate(near(s, ps)):
+    for i, other in enumerate(near):
         face = 0.5 * (here + other)
         diag = diag + face
         t[2 * i, p], t[2 * i + 1, p] = as_factors(face)
-    real, other = real_lanes(here.shape[0]), flip(diag)
-    inv = relax / (diag * diag + other * other)
-    w[0, p] = jnp.where(real, diag, other) * inv
-    w[1, p] = jnp.where(real, other, -diag) * inv
+    w[0, p], w[1, p] = inverse_factors(diag)
     if g is not None:
         g[0, p], g[1, p] = as_factors(diag)
 
 
-def gathered_inflow(near, v, pv, t, p):
-    total = None
-    for i, q in enumerate(near(v, pv)):
-        term = product(t[2 * i, p], t[2 * i + 1, p], q)
-        total = term if total is None else total + term
-    return total
+def gathered_inflow(near, t, p):
+    a = sum(t[2 * i, p] * q for i, q in enumerate(near[1:], 1)) + t[0, p] * near[0]
+    b = sum(t[2 * i + 1, p] * q for i, q in enumerate(near[1:], 1)) + t[1, p] * near[0]
+    return a + flip(b)
+
+
+def factors(ref, p):
+    return ref[0, p], ref[1, p]
 
 
 def eightfold(q):
     return pair_x(pair_x(pair_x(q, 32), 16), 1)
 
 
-def coarse_solve(counts, rhs, coef, s3, s4, t3, w3, g3, t4, w4, f4, va, vb, ea, eb, near_out):
+BATCH = 8
+
+
+def batches(n, body):
+    def run(i, carry):
+        body(pl.multiple_of(i * BATCH, BATCH))
+        return carry
+
+    lax.fori_loop(0, n // BATCH, run, 0)
+
+
+def coarse_solve(counts, cells, t3, w3, g3, t4, w4, s3, va, vb, ea, near_out):
     nz, ny = counts
-    zero = jnp.zeros((ny, LANES), F32)
-    for ref in (s3, s4, ea, eb):
-        ref[0] = zero
-        ref[nz + 1] = zero
+    groups = ny // 8
+    zero = jnp.zeros((nz, LANES), F32)
+    slot = slot_of(lanes(nz))
+    s3[0] = zero
+    s3[ny + 1] = zero
     for ref in (va, vb):
-        for p in (0, 1, 2, nz + 3, nz + 4, nz + 5):
+        for p in (0, 1, 2, ny + 3, ny + 4, ny + 5):
             ref[p] = zero
-    for p in (0, 1, nz + 2, nz + 3):
+    for p in (0, 1, ny + 2, ny + 3):
         for i in range(12):
             t3[i, p] = zero
         w3[0, p] = zero
         w3[1, p] = zero
 
-    def load(p):
-        q = coef[p, :, 0:LANES]
-        s3[p + 1] = q
-        s4[p + 1] = 0.125 * eightfold(q)
-
-    each(0, nz, load)
-
-    def setup(p):
-        q = coef[p, :, LANES : 2 * LANES]
-        set_level(near_level3, s3, p + 1, q, t3, w3, g3, p + 2)
-        set_level(near_level4, s4, p + 1, 0.5 * eightfold(q), t4, w4, None, p)
-        va[p + 3] = product(w3[0, p + 2], w3[1, p + 2], rhs[p])
-
-    each(0, nz, setup, 1)
-
-    def sweep3(src, p):
-        gain = rhs[jnp.clip(p, 0, nz - 1)] + gathered_inflow(near_level3, src, p + 3, t3, p + 2)
-        return keep * src[p + 3] + product(w3[0, p + 2], w3[1, p + 2], gain)
-
-    def pre(p):
-        vb[p + 3] = sweep3(va, p)
-
-    each(0, nz, pre, 1)
-
-    def restrict(p):
-        gain = rhs[p] + gathered_inflow(near_level3, vb, p + 3, t3, p + 2)
-        gain = 0.5 * eightfold(gain - product(g3[0, p + 2], g3[1, p + 2], vb[p + 3]))
-        f4[p] = gain
-        ea[p + 1] = product(w4[0, p], w4[1, p], gain)
-
-    each(0, nz, restrict, 1)
-    src, dst = ea, eb
+    def rhs(p):
+        return cells[p, :, 0:LANES]
+
+    def compacted(planes):
+        out = planes[0]
+        for j in range(1, 8):
+            out = jnp.where(slot == j, planes[j], out)
+        return out
+
+    def load(p0):
+        for i in range(BATCH):
+            s3[p0 + i + 1] = cells[p0 + i, :, LANES : 2 * LANES]
+
+    batches(ny, load)
+
+    def setup(p0):
+        planes = [s3[p0 + i] for i in range(BATCH + 2)]
+        for i, near in enumerate(near_level3(planes)):
+            p = p0 + i
+            set_level(planes[i + 1], near, cells[p, :, 2 * LANES : 3 * LANES], t3, w3, g3, p + 2)
+            va[p + 3] = product(factors(w3, p + 2), rhs(p))
+
+    batches(ny, setup)
+
+    s4, m4 = [], []
+    for k in range(groups):
+        s4.append(0.125 * eightfold_compact([s3[8 * k + j + 1] for j in range(8)], compacted))
+        m4.append(0.5 * eightfold_compact([cells[8 * k + j, :, 2 * LANES : 3 * LANES] for j in range(8)], compacted))
+    for k, near in enumerate(near_level4(s4)):
+        set_level(s4[k], near, m4[k], t4, w4, None, k)
+
+    def sweep3(src, rows, p):
+        near = near_level3([src[p + 2], src[p + 3], src[p + 4]])[0]
+        gain = rows + gathered_inflow(near, t3, p + 2)
+        return keep * src[p + 3] + product(factors(w3, p + 2), gain)
+
+    def pre(p0):
+        planes = [va[p0 + i + 2] for i in range(BATCH + 2)]
+        for i, near in enumerate(near_level3(planes)):
+            p = p0 + i
+            gain = rhs(p) + gathered_inflow(near, t3, p + 2)
+            vb[p + 3] = keep * planes[i + 1] + product(factors(w3, p + 2), gain)
+
+    batches(ny, pre)
+
+    def restrict(p0):
+        planes = [vb[p0 + i + 2] for i in range(BATCH + 2)]
+        gains = []
+        for i, near in enumerate(near_level3(planes)):
+            p = p0 + i
+            gain = rhs(p) + gathered_inflow(near, t3, p + 2)
+            gains.append(gain - product(factors(g3, p + 2), planes[i + 1]))
+        ea[p0 // BATCH] = 0.5 * eightfold_compact(gains, compacted)
+
+    batches(ny, restrict)
+    f4 = [ea[k] for k in range(groups)]
+    e4 = [product(factors(w4, k), f4[k]) for k in range(groups)]
     for sweep in range(COARSE_SWEEPS - 1):
-
-        def relaxed(p, src=src, dst=dst):
-            gain = f4[p] + gathered_inflow(near_level4, src, p + 1, t4, p)
-            dst[p + 1] = keep * src[p + 1] + product(w4[0, p], w4[1, p], gain)
-
-        each(0, nz, relaxed, 2)
-        src, dst = dst, src
-
-    def correct(p):
-        vb[p + 3] = vb[p + 3] + src[p + 1]
-
-    each(0, nz, correct)
-    mine = lax.axis_index("gz")
+        e4 = [
+            keep * e4[k] + product(factors(w4, k), f4[k] + gathered_inflow(near, t4, k))
+            for k, near in enumerate(near_level4(e4))
+        ]
+    for k in range(groups):
+        ea[k] = e4[k]
+
+    mine = lax.axis_index("gy")
+    lane = lanes(nz)
+    for d in range(-3, 4):
+        p = mine + d
+        on = jnp.where((p >= 0) & (p < ny), 1.0, 0.0)
+        q = jnp.clip(p, 0, ny - 1)
+        corr = jnp.take_along_axis(ea[q // 8], slot_lanes(lane, jnp.full((nz, LANES), q % 8, jnp.int32)), axis=1)
+        vb[p + 3] = vb[p + 3] + on * corr
     for d in range(-2, 3):
-        va[mine + d + 3] = sweep3(vb, mine + d)
+        va[mine + d + 3] = sweep3(vb, rhs(jnp.clip(mine + d, 0, ny - 1)), mine + d)
     for d in range(-1, 2):
-        near_out[d + 1] = sweep3(va, mine + d)
+        near_out[d + 1] = sweep3(va, rhs(jnp.clip(mine + d, 0, ny - 1)), mine + d)
+
+
+def eightfold_compact(planes, compacted):
+    return compacted([eightfold(q) for q in planes])
 
 
 def up_kernel(
-    counts, rhs, coef, cmid, cleft, cright, tz2, ty2, tx2, w2, v1, f1, tz1, ty1, tx1, w1, v0, f0, tz0, ty0, tx0, w0, out,
-    s3, s4, t3, w3, g3, t4, w4, f4, va, vb, ea, eb, near, a2, b2, f2, e1, a1, b1, e0, a0, b0,
+    counts, cells, cmid, cleft, cright, tz2, ty2, tx2, w2, v1, f1, tz1, ty1, tx1, w1, v0, f0, tz0, ty0, tx0, w0, out,
+    t3, w3, g3, t4, w4, s3, va, vb, ea, near, a2, b2, f2, e1, a1, b1, e0, a0, b0,
 ):
-    ny = counts[1]
-    gy = lax.axis_index("gy")
-    coarse_solve(counts, rhs, coef, s3, s4, t3, w3, g3, t4, w4, f4, va, vb, ea, eb, near)
+    nz = counts[0]
+    gz = lax.axis_index("gz")
+    coarse_solve(counts, cells, t3, w3, g3, t4, w4, s3, va, vb, ea, near)
 
     lane4, zero4 = lanes(4), jnp.zeros((4, LANES), F32)
 
@@ -462,16 +534,16 @@
 
     each(0, 12, unpack)
     r16, l16 = row_ids(16), lanes(16)
-    cell = 16 * ((r16 // 2) & 1) + l16 // 8
-    for d in range(3):
-        own = near[d, pl.ds(gy, 1), :]
-        after = near[d, pl.ds(jnp.minimum(gy + 1, ny - 1), 1), :] * jnp.where(gy == ny - 1, 0.0, 1.0)
-        before = near[d, pl.ds(jnp.maximum(gy - 1, 0), 1), :] * jnp.where(gy == 0, 0.0, 1.0)
+    cell = l16 // 8
+    for dz in (-1, 0, 1):
+        row = jnp.clip(gz + dz, 0, nz - 1)
+        on = jnp.where((gz + dz >= 0) & (gz + dz < nz), 1.0, 0.0)
+        before, own, after = (near[d, pl.ds(row, 1), :] * on for d in range(3))
         rows = jnp.where(r16 < 4, own, jnp.where(r16 < 8, after, jnp.where(r16 < 12, 0.0, before)))
         for c in (0, 1):
             for zz in (0, 1):
-                corr = jnp.take_along_axis(rows, cell + (64 * c + 32 * zz), axis=1)
-                for z in (4 * d + 2 * zz, 4 * d + 2 * zz + 1):
+                corr = jnp.take_along_axis(rows, cell + 16 * ((r16 // 2) & 1) + (64 * c + 32 * zz), axis=1)
+                for z in (4 * dz + 4 + 2 * zz, 4 * dz + 5 + 2 * zz):
                     a2[c, z] = a2[c, z] + corr
 
     each(1, 11, lambda z: put(b2, z, swept(z, 4, a2, f2, tz2, ty2, tx2, w2)))
@@ -547,45 +619,49 @@
     return mid, left, right
 
 
+def shared(block, axis):
+    n = lax.axis_size(axis)
+    return lax.all_to_all(jnp.broadcast_to(block[None], (n, *block.shape)), axis, 0, 0)
+
+
 def body(source, labels, phase_table):
     nz, ny = lax.axis_size("gz"), lax.axis_size("gy")
-    lab = labels.astype(jnp.int32)
     near_c, far_c = run(
-        coeff_kernel, "coefficients", (lab, phase_table),
+        coeff_kernel, "coefficients", (labels, phase_table),
         [(2, 8, 8, LANES), (1, 2 * LANES)],
         [(4, 8, 16, LANES), (4, 8, 8, LANES), (4, 4, 4, LANES), (2, 8, LANES)], smem=(1,),
     )
-    far_c = lax.all_gather(far_c, ("gz", "gy"), axis=0, tiled=True).reshape(nz, ny, 2 * LANES)
     fine = jnp.concatenate([source, labels.astype(F32)[None]], axis=0)
-    coef1 = window(near_c, 1, 8)
 
     win = (2, 24, 24, LANES)
-    rhs1, *state0 = run(
-        lambda *refs: fine_kernel((16 * nz, 16 * ny), *refs), "fine_down", (*window(fine, 1, 4), phase_table),
-        [(8, 8, LANES)] + [win] * 6,
+    msg, *state0 = run(
+        lambda *refs: fine_kernel((16 * nz, 16 * ny), *refs), "fine_down",
+        (*window(fine, 1, 4), phase_table, near_c),
+        [(3, 8, 8, LANES)] + [win] * 6,
         [(24, 24, LANES)] + [win] * 4 + [(2, 8, 24, LANES)], smem=(3,),
     )
     win2 = (2, 12, 16, LANES)
     row, c_own, *state = run(
         lambda *refs: middle_kernel(((8 * nz, 8 * ny), (4 * nz, 4 * ny)), *refs), "middle_down",
-        (*coef1, *window(rhs1, 0, 8)),
-        [(1, LANES), (4, 4, LANES)] + [win] * 6 + [win2] * 4,
+        (*window(msg, 1, 8), far_c),
+        [(1, 3 * LANES), (4, 4, LANES)] + [win] * 6 + [win2] * 4,
         [win] * 4 + [(2, 12, 24, LANES)] + [win2] * 6 + [(2, 2, 16, LANES), (8, LANES)],
     )
     state1, state2 = state[:6], state[6:]
-    rhs3 = lax.all_gather(row, ("gz", "gy"), axis=0, tiled=True).reshape(nz, ny, LANES)
+    column = shared(row[0], "gz")
+    cells = shared(column, "gy")
     cwin = window(c_own, 0, 4)
 
     def whole(n, pad):
-        return (n, nz + 2 * pad, ny, LANES)
-
+        return (n, ny + 2 * pad, nz, LANES)
+
+    small = (ny // 8, nz, LANES)
     return run(
         lambda *refs: up_kernel((nz, ny), *refs), "coarse_and_up",
-        (rhs3, far_c, *cwin, *state2, *state1, *state0),
+        (cells, *cwin, *state2, *state1, *state0),
         [(2, 16, 16, LANES)],
-        [whole(1, 1)[1:]] * 2
-        + [whole(12, 2), whole(2, 2), whole(2, 2), whole(12, 0), whole(2, 0), whole(1, 0)[1:]]
-        + [whole(1, 3)[1:]] * 2 + [whole(1, 1)[1:]] * 2 + [(3, ny, LANES)]
+        [whole(12, 2), whole(2, 2), whole(2, 2), (12, *small), (2, *small)]
+        + [whole(1, 1)[1:]] + [whole(1, 3)[1:]] * 2 + [small, (3, nz, LANES)]
         + [win2] * 3 + [(2, 12, 24, LANES), win, win, win, win, win],
     )[0]
 

time: 346 us -> 148 us (0.43)
  blocking collectives: 232 us -> 28.7 us
  local copies, waits for them, and re-layouts: 0.2 us -> 23.4 us
  Pallas kernels: 50.8 us -> 28 us
    all_gather x2 -> x0, blocking collectives: 232 us -> none  [the longest x1 124 us: body(): lax.all_gather(far_c, ('gz', 'gy'), axis=0, tiled=True)]
    all_to_all x0 -> x1, blocking collectives: none -> 28.7 us  [shared(): lax.all_to_all(jnp.broadcast_to(block[None], (n, *block.shape)), axis, 0, 0)]
    pallas_call x4, Pallas kernels: 50.8 us -> 28 us  [run(): pl.pallas_call(kernel, name=name, out_shape=shapes, in_specs=spec_all(len...]
    unnamed x13 -> x63, local copies, waits for them, and re-layouts: 0.13 us -> 22.4 us
    all_to_all x0 -> x1, starting transfers between devices: none -> 10 us  [shared(): lax.all_to_all(jnp.broadcast_to(block[None], (n, *block.shape)), axis, 0, 0)]
    ppermute x8 -> x6, starting transfers between devices: 30.6 us -> 23.7 us  [around(): lax.ppermute(lax.slice_in_dim(block, size - width, size, axis=dim), axis,...]
    ppermute x8 -> x6, waiting for transfers between devices: 0.02 us -> 3.87 us  [around(): lax.ppermute(lax.slice_in_dim(block, size - width, size, axis=dim), axis,...]
    ppermute x8 -> x6, starting transfers between devices: 15 us -> 13.2 us  [around(): lax.ppermute(lax.slice_in_dim(block, 0, width, axis=dim), axis, down)]
  transfers between devices with their start and end apart: 16 -> 13, of which waited for: 4 -> 8; matrix products, arithmetic and copies ran while one was open for 0% -> 0% of each run, Pallas kernels for 2% -> 1%
where the time goes in v2:
time: 148 us; the launch traced here: 146 us
  starting transfers between devices  46.9 us (32%)
  blocking collectives  28.7 us (19%)
  Pallas kernels  28 us (19%)
  local copies, waits for them, and re-layouts  23.4 us (16%)
  waiting for transfers between devices  17.7 us (12%)
    all_to_all x1, blocking collectives, shared(): lax.all_to_all(jnp.broadcast_to(block[None], (n, *block.shape)), axis, 0, 0)  28.7 us
    pallas_call x4, Pallas kernels, run(): pl.pallas_call(kernel, name=name, out_shape=shapes, in_specs=spec_all(len...  28 us
    ppermute x6, starting transfers between devices, around(): lax.ppermute(lax.slice_in_dim(block, size - width, size, axis=dim), axis,...  23.7 us
    unnamed x63, local copies, waits for them, and re-layouts  22.4 us
    ppermute x6, waiting for transfers between devices, around(): lax.ppermute(lax.slice_in_dim(block, 0, width, axis=dim), axis, down)  13.8 us
    ppermute x6, starting transfers between devices, around(): lax.ppermute(lax.slice_in_dim(block, 0, width, axis=dim), axis, down)  13.2 us
    all_to_all x1, starting transfers between devices, shared(): lax.all_to_all(jnp.broadcast_to(block[None], (n, *block.shape)), axis, 0, 0)  10 us
    ppermute x6, waiting for transfers between devices, around(): lax.ppermute(lax.slice_in_dim(block, size - width, size, axis=dim), axis,...  3.87 us
  transfers between devices with their start and end apart: 13, of which 8 were waited for; matrix products, arithmetic and copies ran while one was open for 0% of the time, Pallas kernels for 1%

profile of v2, /device:TPU:1, one launch (start us, length us, event | category | flops | bytes accessed | tf_op | source)
XLA Modules:
  0.0 145.9 jit_solution(14120046812248876531)
XLA Ops:
  1.0 1.3 collective-permute-start.1
  2.3 5.0 %collective-permute-start = (f32[3,4,16,128]{3,2,1,0:T(8,128)S(1)}, f32[3,4,16,128]{3,2,1,0:T(8,128)S(1)}, u32[]{:S(2)}, u32[]{:S(2)}) collective-permute-start(f32[3,4,16,128]{3,2,1,0:T(8,128)S(1)} %get-tuple-element.49), channel_id=1, source_target_pairs={{0,32},{32,64},{64,96},{96,128},{128,160},{160,192},{192,224},{224... | collective-permute-start | bytes 294920 | tf_op jit(solution)/shard_map/ppermute | solution.py:610
  7.4 1.6 %collective-permute-done = f32[3,4,16,128]{3,2,1,0:T(8,128)S(1)} collective-permute-done((f32[3,4,16,128]{3,2,1,0:T(8,128)S(1)}, f32[3,4,16,128]{3,2,1,0:T(8,128)S(1)}, u32[]{:S(2)}, u32[]{:S(2)}) %collective-permute-start) | collective-permute-done | bytes 98336 | tf_op jit(solution)/shard_map/ppermute | solution.py:610
  9.1 4.7 %collective-permute-start.2 = (f32[3,24,4,128]{3,2,1,0:T(4,128)S(1)}, f32[3,24,4,128]{3,2,1,0:T(4,128)S(1)}, u32[]{:S(2)}, u32[]{:S(2)}) collective-permute-start(f32[3,24,4,128]{3,2,1,0:T(4,128)S(1)} %get-tuple-element.48), channel_id=1, source_target_pairs={{0,1},{1,2},{2,3},{3,4},{4,5},{5,6},{6,7},{7,8},{8,9},{9,10},{10,1... | collective-permute-start | bytes 442376 | tf_op jit(solution)/shard_map/ppermute | solution.py:610
  13.8 5.5 %collective-permute-start.3 = (f32[3,24,4,128]{3,2,1,0:T(4,128)S(1)}, f32[3,24,4,128]{3,2,1,0:T(4,128)S(1)}, u32[]{:S(2)}, u32[]{:S(2)}) collective-permute-start(f32[3,24,4,128]{3,2,1,0:T(4,128)S(1)} %get-tuple-element.47), channel_id=1, source_target_pairs={{1,0},{2,1},{3,2},{4,3},{5,4},{6,5},{7,6},{8,7},{9,8},{10,9},{11,1... | collective-permute-start | bytes 442376 | tf_op jit(solution)/shard_map/ppermute | solution.py:611
  20.4 3.1 %fine_down.1 = (f32[3,8,8,128]{3,2,1,0:T(8,128)S(1)}, f32[2,24,24,128]{3,2,1,0:T(8,128)S(1)}, f32[2,24,24,128]{3,2,1,0:T(8,128)S(1)}, f32[2,24,24,128]{3,2,1,0:T...) custom-call(f32[3,24,16,128]{3,2,1,0:T(8,128)S(1)} %pad_maximum_fusion.r, ...), custom_call_target="tpu_custom_call" | custom-call | tf_op jit(solution)/shard_map/fine_down/pallas_call | solution.py:590
  25.1 4.0 %collective-permute-start.4 = (f32[3,8,8,128]{3,2,1,0:T(8,128)S(1)}, f32[3,8,8,128]{3,2,1,0:T(8,128)S(1)}, u32[]{:S(2)}, u32[]{:S(2)}) collective-permute-start(f32[3,8,8,128]{3,2,1,0:T(8,128)S(1)} %get-tuple-element.27), channel_id=1, source_target_pairs={{0,32},{32,64},{64,96},{96,128},{128,160},{160,192},{192,224},{224... | collective-permute-start | bytes 294920 | tf_op jit(solution)/shard_map/ppermute | solution.py:610
  29.2 1.3 collective-permute-start.5
  31.1 3.9 %collective-permute-done.5 = f32[3,8,8,128]{3,2,1,0:T(8,128)S(1)} collective-permute-done((f32[3,8,8,128]{3,2,1,0:T(8,128)S(1)}, f32[3,8,8,128]{3,2,1,0:T(8,128)S(1)}, u32[]{:S(2)}, u32[]{:S(2)}) %collective-permute-start.5) | collective-permute-done | bytes 98336 | tf_op jit(solution)/shard_map/ppermute | solution.py:611
  35.0 2.9 %collective-permute-start.6 = (f32[3,24,8,128]{3,2,1,0:T(8,128)S(1)}, f32[3,24,8,128]{3,2,1,0:T(8,128)S(1)}, u32[]{:S(2)}, u32[]{:S(2)}) collective-permute-start(f32[3,24,8,128]{3,2,1,0:T(8,128)S(1)} %constant_dynamic-update-slice_fusion.refs_0_), channel_id=1, source_target_pairs={{0,1},{1,2},{2,3},{3,4},{4,5},{5,6},{6,7},{7,8},{8,9},{9,10},{10,1... | collective-permute-start | bytes 884744 | tf_op jit(solution)/shard_map/ppermute | solution.py:610
  37.9 1.9 %collective-permute-start.7 = (f32[3,24,8,128]{3,2,1,0:T(8,128)S(1)}, f32[3,24,8,128]{3,2,1,0:T(8,128)S(1)}, u32[]{:S(2)}, u32[]{:S(2)}) collective-permute-start(f32[3,24,8,128]{3,2,1,0:T(8,128)S(1)} %constant_dynamic-update-slice_fusion.refs_0_), channel_id=1, source_target_pairs={{1,0},{2,1},{3,2},{4,3},{5,4},{6,5},{7,6},{8,7},{9,8},{10,9},{11,1... | collective-permute-start | bytes 884744 | tf_op jit(solution)/shard_map/ppermute | solution.py:611
  39.9 1.7 %collective-permute-done.6.refs_1_ = f32[3,24,8,128]{3,2,1,0:T(8,128)S(1)} collective-permute-done((f32[3,24,8,128]{3,2,1,0:T(8,128)S(1)}, f32[3,24,8,128]{3,2,1,0:T(8,128)S(1)}, u32[]{:S(2)}, u32[]{:S(2)}) %collective-permute-start.6) | collective-permute-done | bytes 294944 | tf_op jit(solution)/shard_map/ppermute | solution.py:610
  41.6 4.4 %collective-permute-done.7.refs_2_ = f32[3,24,8,128]{3,2,1,0:T(8,128)S(1)} collective-permute-done((f32[3,24,8,128]{3,2,1,0:T(8,128)S(1)}, f32[3,24,8,128]{3,2,1,0:T(8,128)S(1)}, u32[]{:S(2)}, u32[]{:S(2)}) %collective-permute-start.7) | collective-permute-done | bytes 294944 | tf_op jit(solution)/shard_map/ppermute | solution.py:611
  46.0 4.6 %middle_down.1 = (f32[1,384]{1,0:T(1,128)S(1)}, f32[4,4,128]{2,1,0:T(4,128)S(1)}, f32[2,24,24,128]{3,2,1,0:T(8,128)S(1)}, f32[2,24,24,128]{3,2,1,0:T(8,128)S(1)}...) custom-call(f32[3,24,8,128]{3,2,1,0:T(8,128)S(1)} %constant_dynamic-, ...), custom_call_target="tpu_custom_call" | custom-call | tf_op jit(solution)/shard_map/middle_down/pallas_call | solution.py:590
  56.9 28.7 %all_to_all.11 = f32[16,1,384]{2,1,0:T(1,128)S(1)} all-to-all(f32[16,1,384]{2,1,0:T(1,128)S(1)} %broadcast_in_dim.17), channel_id=1, replica_groups=mesh['gz'=16,'gy'=32] {'gz'}, dimensions={0} | all-to-all | bytes 49152 | tf_op jit(solution)/shard_map/all_to_all | solution.py:624
  86.5 10.0 %all-to-all-start.1 = ((f32[32,16,384]{2,1,0:T(8,128)}), f32[32,16,384]{2,1,0:T(8,128)S(1)}, u32[]{:S(2)}, u32[]{:S(2)}) async-start(f32[32,16,384]{2,1,0:T(8,128)} %broadcast_in_dim.19), calls=%async_computation.1 | async-start | bytes 1572864 | tf_op jit(solution)/shard_map/all_to_all | solution.py:624
  96.5 2.4 %collective-permute-start.8 = (f32[4,4,128]{2,1,0:T(4,128)S(1)}, f32[4,4,128]{2,1,0:T(4,128)S(1)}, u32[]{:S(2)}, u32[]{:S(2)}) collective-permute-start(f32[4,4,128]{2,1,0:T(4,128)S(1)} %get-tuple-element.30), channel_id=1, source_target_pairs={{0,32},{32,64},{64,96},{96,128},{128,160},{160,192},{192,224},{224... | collective-permute-start | bytes 24584 | tf_op jit(solution)/shard_map/ppermute | solution.py:610
  98.9 1.3 collective-permute-start.9
  100.2 3.4 %collective-permute-done.9 = f32[4,4,128]{2,1,0:T(4,128)S(1)} collective-permute-done((f32[4,4,128]{2,1,0:T(4,128)S(1)}, f32[4,4,128]{2,1,0:T(4,128)S(1)}, u32[]{:S(2)}, u32[]{:S(2)}) %collective-permute-start.9) | collective-permute-done | bytes 8224 | tf_op jit(solution)/shard_map/ppermute | solution.py:611
  103.6 4.7 %collective-permute-start.10 = (f32[12,4,128]{2,1,0:T(4,128)S(1)}, f32[12,4,128]{2,1,0:T(4,128)S(1)}, u32[]{:S(2)}, u32[]{:S(2)}) collective-permute-start(f32[12,4,128]{2,1,0:T(4,128)S(1)} %constant_dynamic-update-slice_fusion.3.refs_1_), channel_id=1, source_target_pairs={{0,1},{1,2},{2,3},{3,4},{4,5},{5,6},{6,7},{7,8},{8,9},{9,10},{10,1... | collective-permute-start | bytes 73736 | tf_op jit(solution)/shard_map/ppermute | solution.py:610
  108.2 1.9 %collective-permute-start.11 = (f32[12,4,128]{2,1,0:T(4,128)S(1)}, f32[12,4,128]{2,1,0:T(4,128)S(1)}, u32[]{:S(2)}, u32[]{:S(2)}) collective-permute-start(f32[12,4,128]{2,1,0:T(4,128)S(1)} %constant_dynamic-update-slice_fusion.3.refs_1_), channel_id=1, source_target_pairs={{1,0},{2,1},{3,2},{4,3},{5,4},{6,5},{7,6},{8,7},{9,8},{10,9},{11,1... | collective-permute-start | bytes 73736 | tf_op jit(solution)/shard_map/ppermute | solution.py:611
  111.4 2.0 %collective-permute-done.11.refs_3_ = f32[12,4,128]{2,1,0:T(4,128)S(1)} collective-permute-done((f32[12,4,128]{2,1,0:T(4,128)S(1)}, f32[12,4,128]{2,1,0:T(4,128)S(1)}, u32[]{:S(2)}, u32[]{:S(2)}) %collective-permute-start.11) | collective-permute-done | bytes 24608 | tf_op jit(solution)/shard_map/ppermute | solution.py:611
  120.0 1.1 copy-done.11
  126.6 19.3 %coarse_and_up.1 = f32[2,16,16,128]{3,2,1,0:T(8,128)} custom-call(f32[32,16,384]{2,1,0:T(8,128)S(1)} %all-to-all-done.1.refs_0_, f32[12,4,128]{2,1,0:T(4,128)S(1)} %copy-done.22, f32[12,4,128]{2,1,0:T(4,128)S(1)} %copy-done.24, f32[12,4,128]{2,1,0:T(4,128)S(1)} %copy-done.26, f32[2,12,16,128]{3,2,1,0:T(8,128)S(1)} %get-tuple-element.31.refs_4_, ...), custom_call_target="tpu_custom_call" | custom-call | tf_op jit(solution)/shard_map/coarse_and_up/pallas_call | solution.py:590
  (79 shorter events, 25.1 us)
Async XLA Ops:
  0.0 1.0 copy-start.28
  1.0 6.4 %collective-permute-start.1 = (f32[3,4,16,128]{3,2,1,0:T(8,128)S(1)}, f32[3,4,16,128]{3,2,1,0:T(8,128)S(1)}, u32[]{:S(2)}, u32[]{:S(2)}) collective-permute-start(f32[3,4,16,128]{3,2,1,0:T(8,128)S(1)} %get-tuple-element.50), channel_id=1, source_target_pairs={{32,0},{64,32},{96,64},{128,96},{160,128},{192,160},{224,192},{256... | collective-permute-start | bytes 294920 | tf_op jit(solution)/shard_map/ppermute | solution.py:611
  2.3 6.6 %collective-permute-start = (f32[3,4,16,128]{3,2,1,0:T(8,128)S(1)}, f32[3,4,16,128]{3,2,1,0:T(8,128)S(1)}, u32[]{:S(2)}, u32[]{:S(2)}) collective-permute-start(f32[3,4,16,128]{3,2,1,0:T(8,128)S(1)} %get-tuple-element.49), channel_id=1, source_target_pairs={{0,32},{32,64},{64,96},{96,128},{128,160},{160,192},{192,224},{224... | collective-permute-start | bytes 294920 | tf_op jit(solution)/shard_map/ppermute | solution.py:610
  9.0 10.3 %copy-start.16 = (s32[16,16,128]{2,1,0:T(8,128)S(1)}, s32[16,16,128]{2,1,0:T(8,128)}, u32[]{:S(2)}) copy-start(s32[16,16,128]{2,1,0:T(8,128)} %labels.1) | copy-start | bytes 393220
  9.1 10.2 %copy-start.27 = (f32[4,4]{1,0:T(4,128)S(1)}, f32[4,4]{1,0:T(4,128)}, u32[]{:S(2)}) copy-start(f32[4,4]{1,0:T(4,128)} %refs_3_.1) | copy-start | bytes 196
  9.1 11.3 %collective-permute-start.2 = (f32[3,24,4,128]{3,2,1,0:T(4,128)S(1)}, f32[3,24,4,128]{3,2,1,0:T(4,128)S(1)}, u32[]{:S(2)}, u32[]{:S(2)}) collective-permute-start(f32[3,24,4,128]{3,2,1,0:T(4,128)S(1)} %get-tuple-element.48), channel_id=1, source_target_pairs={{0,1},{1,2},{2,3},{3,4},{4,5},{5,6},{6,7},{7,8},{8,9},{9,10},{10,1... | collective-permute-start | bytes 442376 | tf_op jit(solution)/shard_map/ppermute | solution.py:610
  13.8 6.6 %collective-permute-start.3 = (f32[3,24,4,128]{3,2,1,0:T(4,128)S(1)}, f32[3,24,4,128]{3,2,1,0:T(4,128)S(1)}, u32[]{:S(2)}, u32[]{:S(2)}) collective-permute-start(f32[3,24,4,128]{3,2,1,0:T(4,128)S(1)} %get-tuple-element.47), channel_id=1, source_target_pairs={{1,0},{2,1},{3,2},{4,3},{5,4},{6,5},{7,6},{8,7},{9,8},{10,9},{11,1... | collective-permute-start | bytes 442376 | tf_op jit(solution)/shard_map/ppermute | solution.py:611
  25.1 5.9 %collective-permute-start.4 = (f32[3,8,8,128]{3,2,1,0:T(8,128)S(1)}, f32[3,8,8,128]{3,2,1,0:T(8,128)S(1)}, u32[]{:S(2)}, u32[]{:S(2)}) collective-permute-start(f32[3,8,8,128]{3,2,1,0:T(8,128)S(1)} %get-tuple-element.27), channel_id=1, source_target_pairs={{0,32},{32,64},{64,96},{96,128},{128,160},{160,192},{192,224},{224... | collective-permute-start | bytes 294920 | tf_op jit(solution)/shard_map/ppermute | solution.py:610
  29.2 5.9 %collective-permute-start.5 = (f32[3,8,8,128]{3,2,1,0:T(8,128)S(1)}, f32[3,8,8,128]{3,2,1,0:T(8,128)S(1)}, u32[]{:S(2)}, u32[]{:S(2)}) collective-permute-start(f32[3,8,8,128]{3,2,1,0:T(8,128)S(1)} %get-tuple-element.27), channel_id=1, source_target_pairs={{32,0},{64,32},{96,64},{128,96},{160,128},{192,160},{224,192},{256... | collective-permute-start | bytes 294920 | tf_op jit(solution)/shard_map/ppermute | solution.py:611
  35.0 6.6 %collective-permute-start.6 = (f32[3,24,8,128]{3,2,1,0:T(8,128)S(1)}, f32[3,24,8,128]{3,2,1,0:T(8,128)S(1)}, u32[]{:S(2)}, u32[]{:S(2)}) collective-permute-start(f32[3,24,8,128]{3,2,1,0:T(8,128)S(1)} %constant_dynamic-update-slice_fusion.refs_0_), channel_id=1, source_target_pairs={{0,1},{1,2},{2,3},{3,4},{4,5},{5,6},{6,7},{7,8},{8,9},{9,10},{10,1... | collective-permute-start | bytes 884744 | tf_op jit(solution)/shard_map/ppermute | solution.py:610
  37.9 8.0 %collective-permute-start.7 = (f32[3,24,8,128]{3,2,1,0:T(8,128)S(1)}, f32[3,24,8,128]{3,2,1,0:T(8,128)S(1)}, u32[]{:S(2)}, u32[]{:S(2)}) collective-permute-start(f32[3,24,8,128]{3,2,1,0:T(8,128)S(1)} %constant_dynamic-update-slice_fusion.refs_0_), channel_id=1, source_target_pairs={{1,0},{2,1},{3,2},{4,3},{5,4},{6,5},{7,6},{8,7},{9,8},{10,9},{11,1... | collective-permute-start | bytes 884744 | tf_op jit(solution)/shard_map/ppermute | solution.py:611
  86.5 27.5 %all-to-all-start.1 = ((f32[32,16,384]{2,1,0:T(8,128)}), f32[32,16,384]{2,1,0:T(8,128)S(1)}, u32[]{:S(2)}, u32[]{:S(2)}) async-start(f32[32,16,384]{2,1,0:T(8,128)} %broadcast_in_dim.19), calls=%async_computation.1 | async-start | bytes 1572864 | tf_op jit(solution)/shard_map/all_to_all | solution.py:624
  96.5 3.7 %collective-permute-start.8 = (f32[4,4,128]{2,1,0:T(4,128)S(1)}, f32[4,4,128]{2,1,0:T(4,128)S(1)}, u32[]{:S(2)}, u32[]{:S(2)}) collective-permute-start(f32[4,4,128]{2,1,0:T(4,128)S(1)} %get-tuple-element.30), channel_id=1, source_target_pairs={{0,32},{32,64},{64,96},{96,128},{128,160},{160,192},{192,224},{224... | collective-permute-start | bytes 24584 | tf_op jit(solution)/shard_map/ppermute | solution.py:610
  98.9 4.7 %collective-permute-start.9 = (f32[4,4,128]{2,1,0:T(4,128)S(1)}, f32[4,4,128]{2,1,0:T(4,128)S(1)}, u32[]{:S(2)}, u32[]{:S(2)}) collective-permute-start(f32[4,4,128]{2,1,0:T(4,128)S(1)} %get-tuple-element.30), channel_id=1, source_target_pairs={{32,0},{64,32},{96,64},{128,96},{160,128},{192,160},{224,192},{256... | collective-permute-start | bytes 24584 | tf_op jit(solution)/shard_map/ppermute | solution.py:611
  103.6 7.2 %collective-permute-start.10 = (f32[12,4,128]{2,1,0:T(4,128)S(1)}, f32[12,4,128]{2,1,0:T(4,128)S(1)}, u32[]{:S(2)}, u32[]{:S(2)}) collective-permute-start(f32[12,4,128]{2,1,0:T(4,128)S(1)} %constant_dynamic-update-slice_fusion.3.refs_1_), channel_id=1, source_target_pairs={{0,1},{1,2},{2,3},{3,4},{4,5},{5,6},{6,7},{7,8},{8,9},{9,10},{10,1... | collective-permute-start | bytes 73736 | tf_op jit(solution)/shard_map/ppermute | solution.py:610
  108.2 5.1 %collective-permute-start.11 = (f32[12,4,128]{2,1,0:T(4,128)S(1)}, f32[12,4,128]{2,1,0:T(4,128)S(1)}, u32[]{:S(2)}, u32[]{:S(2)}) collective-permute-start(f32[12,4,128]{2,1,0:T(4,128)S(1)} %constant_dynamic-update-slice_fusion.3.refs_1_), channel_id=1, source_target_pairs={{1,0},{2,1},{3,2},{4,3},{5,4},{6,5},{7,6},{8,7},{9,8},{10,9},{11,1... | collective-permute-start | bytes 73736 | tf_op jit(solution)/shard_map/ppermute | solution.py:611
  114.7 1.1 copy-start.1
  115.8 1.1 copy-start.3
  116.9 1.1 copy-start.5
  117.9 1.1 copy-start.7
  119.0 1.1 copy-start.9
  120.0 1.1 copy-start.11
  121.1 1.1 copy-start.13
  122.2 1.1 copy-start.15
  (18 other events, 13.8 us)

commit v3 on v2

--- a/solution.py
+++ b/solution.py
@@ -48,17 +48,31 @@
     return jnp.where(even, q, ahead_x(q, -1)), jnp.where(even, ahead_x(q, 1), q)
 
 
-def each(lo, hi, body, step=4):
-    full = (hi - lo) // step
+def each(lo, hi, body, most=11):
+    n = hi - lo
+    step = max(k for k in range(1, most + 1) if n % k == 0)
+    if step == n:
+        for z in range(lo, hi):
+            body(z)
+        return
 
     def run(i, carry):
         for j in range(step):
             body(lo + i * step + j)
         return carry
 
-    lax.fori_loop(0, full, run, 0)
-    for z in range(lo + full * step, hi):
-        body(z)
+    lax.fori_loop(0, n // step, run, 0)
+
+
+def sent(copies):
+    for copy in copies:
+        copy.start()
+    return copies
+
+
+def landed(copies):
+    for copy in copies:
+        copy.wait()
 
 
 def times(t, q):
@@ -189,37 +203,53 @@
     far_out[:, LANES : 2 * LANES] = packed_row(stack[1])
 
 
-def fine_kernel(sizes, mid, left, right, table, near_c, msg_out, v, f, tz, ty, tx, w, lab, s, m, g, first, buf):
+KEPT0 = slice(2, 22)
+KEPT1 = slice(5, 19)
+
+
+def fine_kernel(
+    sizes, source, labels, zb, za, left, right, table, near_c, msg_out, *rest
+):
+    keeps, (v, f, tz, ty, tx, w, lab, s, m, g, first, buf, sem) = rest[:6], rest[6:]
     first_z = lax.axis_index("gz") * 16 - 4
     first_y = lax.axis_index("gy") * 16
 
-    def load(z):
-        for c, ref in ((0, f), (1, f), (2, None)):
-            dst = lab.at[z] if ref is None else ref.at[c, z]
-            dst[0:16] = mid[c, z]
-            dst[16:20] = right[c, z]
-            dst[20:24] = left[c, z]
+    def load(z, own):
+        dst = (f.at[0, z], f.at[1, z], lab.at[z])
+        for c in range(3):
+            dst[c][0:16] = own[c]
+            dst[c][16:20] = right[c, z].astype(dst[c].dtype)
+            dst[c][20:24] = left[c, z].astype(dst[c].dtype)
         ok = inside(24, 20, z, first_z, first_y, *sizes)
         vals = lookup(lab[z], table)
         for c in (0, 1):
             s[c, z] = jnp.where(ok, vals[c], 0.0)
             m[c, z] = vals[2 + c]
 
-    each(0, 24, load)
+    for z in range(4):
+        load(z, (zb[0, z], zb[1, z], zb[2, z].astype(jnp.int32)))
+        load(z + 20, (za[0, z], za[1, z], za[2, z].astype(jnp.int32)))
+    each(0, 16, lambda z: load(z + 4, (source[0, z], source[1, z], labels[z])))
 
     def faces(z):
         ok = inside(24, 20, z, first_z, first_y, *sizes)
         put(first, z, times(make_faces(z, 1, ok, s, m, tz, ty, tx, w, g), pair(f, z)))
 
     each(1, 23, faces)
+
+    def kept(i, ref):
+        return pltpu.make_async_copy(ref.at[:, KEPT0], keeps[i], sem.at[i])
+
+    copies = sent([kept(i, ref) for i, ref in enumerate((v, f, tz, ty, tx, w)) if i])
     each(2, 22, lambda z: put(v, z, swept(z, 1, first, f, tz, ty, tx, w)))
+    copies += sent([kept(0, v)])
 
     def restrict(z):
         a = residual(2 * z + 4, 1, v, f, tz, ty, tx, g)
         b = residual(2 * z + 5, 1, v, f, tz, ty, tx, g)
         put(buf, z, add(a, b))
 
-    each(0, 8, restrict, 2)
+    each(0, 8, restrict, 4)
 
     def finish(z):
         re, im = (0.5 * pair_x(rows_paired(buf, (c, z), 0, 8), 1) for c in (0, 1))
@@ -228,13 +258,15 @@
         msg_out[1, z] = near_c[1, z]
 
     each(0, 8, finish)
+    landed(copies)
 
 
 def middle_kernel(
     sizes, mid, left, right, far_c,
-    row_out, c_out, v, f, tz, ty, tx, w, tz2, ty2, tx2, w2,
-    s, m, g, first, buf, s2, m2, f2, g2, first2, v2, buf2, stack,
+    row_out, c_out, *rest
 ):
+    keeps, rest = rest[:10], rest[10:]
+    v, f, tz, ty, tx, w, tz2, ty2, tx2, w2, s, m, g, first, buf, s2, m2, f2, g2, first2, v2, buf2, stack, sem = rest
     gz, gy = lax.axis_index("gz"), lax.axis_index("gy")
 
     def load(z):
@@ -251,7 +283,13 @@
         put(first, z, times(make_faces(z, 2, ok, s, m, tz, ty, tx, w, g), pair(f, z)))
 
     each(1, 23, faces)
+
+    def kept(i, ref):
+        return pltpu.make_async_copy(ref.at[:, KEPT1], keeps[i], sem.at[i])
+
+    copies = sent([kept(i, ref) for i, ref in enumerate((v, f, tz, ty, tx, w)) if i])
     each(2, 22, lambda z: put(v, z, swept(z, 2, first, f, tz, ty, tx, w)))
+    copies += sent([kept(0, v)])
 
     def coarser(dst, scale, z):
         for c in (0, 1):
@@ -266,7 +304,7 @@
     def restrict(z):
         put(buf, z, add(residual(2 * z, 2, v, f, tz, ty, tx, g), residual(2 * z + 1, 2, v, f, tz, ty, tx, g)))
 
-    each(2, 10, restrict, 2)
+    each(2, 10, restrict, 4)
     each(2, 10, lambda z: coarser(f2, 0.5, z))
 
     def faces2(z):
@@ -278,6 +316,7 @@
     tz2[1, 0] = 0.5 * (s2[1, 0] + s2[1, 1])
     each(2, 10, lambda z: put(first2, z, times(faces2(z), pair(f2, z))))
     faces2(10)
+    copies += sent([pltpu.make_async_copy(ref, keeps[6 + i], sem.at[6 + i]) for i, ref in enumerate((tz2, ty2, tx2, w2))])
     each(3, 9, lambda z: put(v2, z, swept(z, 4, first2, f2, tz2, ty2, tx2, w2)))
     which = lanes(4) & 3
     for z in range(4):
@@ -292,8 +331,11 @@
     for z in range(2):
         for c in (0, 1):
             stack[4 * c + 2 * z : 4 * c + 2 * z + 2] = 0.5 * pair_x(rows_paired(buf2, (c, z), 0, 2), 4)
-    row_out[:, 0:LANES] = packed_row(stack[...])
-    row_out[:, LANES : 3 * LANES] = far_c[...]
+    row_out[0:1] = packed_row(stack[...])
+    row_out[1:2] = far_c[:, 0:LANES]
+    row_out[2:3] = far_c[:, LANES : 2 * LANES]
+    row_out[3:8] = jnp.zeros((5, LANES), F32)
+    landed(copies)
 
 
 def real_lanes(rows):
@@ -395,8 +437,14 @@
     return ref[0, p], ref[1, p]
 
 
-def eightfold(q):
-    return pair_x(pair_x(pair_x(q, 32), 16), 1)
+def folded(planes):
+    lane = lanes(planes[0].shape[0])
+    for bit in (1, 16, 32):
+        low = (lane & bit) == 0
+        planes = [
+            jnp.where(low, a, b) + swap_x(jnp.where(low, b, a), bit) for a, b in zip(planes[0::2], planes[1::2])
+        ]
+    return planes[0]
 
 
 BATCH = 8
@@ -410,11 +458,37 @@
     lax.fori_loop(0, n // BATCH, run, 0)
 
 
-def coarse_solve(counts, cells, t3, w3, g3, t4, w4, s3, va, vb, ea, near_out):
+def level4(f4, s4, m4, t4):
+    real = real_lanes(s4[0].shape[0])
+    start = []
+    for k, near in enumerate(near_level4(s4)):
+        faces = [0.5 * (s4[k] + other) for other in near]
+        fa = inverse_factors(sum(faces[1:]) + faces[0] + m4[k])
+        start.append(product(fa, f4[k]))
+        for i, face in enumerate(faces):
+            q = product(fa, face)
+            other = flip(q)
+            t4[2 * i, k] = jnp.where(real, q, other)
+            t4[2 * i + 1, k] = jnp.where(real, -other, q)
+    turned = [flip(q) for q in start]
+    e, o = start, turned
+    for sweep in range(COARSE_SWEEPS - 1):
+        pairs = list(zip(near_level4(e), near_level4(o)))
+        e_next, o_next = [], []
+        for k, (ne, no) in enumerate(pairs):
+            ab = [(t4[2 * i, k], t4[2 * i + 1, k]) for i in range(6)]
+            x = [a * p + b * q for (a, b), p, q in zip(ab, ne, no)]
+            y = [a * q - b * p for (a, b), p, q in zip(ab, ne, no)]
+            e_next.append((keep * e[k] + start[k] + x[0]) + (x[1] + x[2]) + (x[3] + x[4]) + x[5])
+            o_next.append((keep * o[k] + turned[k] + y[0]) + (y[1] + y[2]) + (y[3] + y[4]) + y[5])
+        e, o = e_next, o_next
+    return e
+
+
+def coarse_solve(counts, cells, t3, w3, g3, t4, s3, va, vb, ea):
     nz, ny = counts
     groups = ny // 8
     zero = jnp.zeros((nz, LANES), F32)
-    slot = slot_of(lanes(nz))
     s3[0] = zero
     s3[ny + 1] = zero
     for ref in (va, vb):
@@ -426,18 +500,9 @@
         w3[0, p] = zero
         w3[1, p] = zero
 
-    def rhs(p):
-        return cells[p, :, 0:LANES]
-
-    def compacted(planes):
-        out = planes[0]
-        for j in range(1, 8):
-            out = jnp.where(slot == j, planes[j], out)
-        return out
-
     def load(p0):
         for i in range(BATCH):
-            s3[p0 + i + 1] = cells[p0 + i, :, LANES : 2 * LANES]
+            s3[p0 + i + 1] = cells[p0 + i, 1]
 
     batches(ny, load)
 
@@ -445,28 +510,22 @@
         planes = [s3[p0 + i] for i in range(BATCH + 2)]
         for i, near in enumerate(near_level3(planes)):
             p = p0 + i
-            set_level(planes[i + 1], near, cells[p, :, 2 * LANES : 3 * LANES], t3, w3, g3, p + 2)
-            va[p + 3] = product(factors(w3, p + 2), rhs(p))
+            set_level(planes[i + 1], near, cells[p, 2], t3, w3, g3, p + 2)
+            va[p + 3] = product(factors(w3, p + 2), cells[p, 0])
 
     batches(ny, setup)
-
-    s4, m4 = [], []
-    for k in range(groups):
-        s4.append(0.125 * eightfold_compact([s3[8 * k + j + 1] for j in range(8)], compacted))
-        m4.append(0.5 * eightfold_compact([cells[8 * k + j, :, 2 * LANES : 3 * LANES] for j in range(8)], compacted))
-    for k, near in enumerate(near_level4(s4)):
-        set_level(s4[k], near, m4[k], t4, w4, None, k)
-
-    def sweep3(src, rows, p):
-        near = near_level3([src[p + 2], src[p + 3], src[p + 4]])[0]
-        gain = rows + gathered_inflow(near, t3, p + 2)
-        return keep * src[p + 3] + product(factors(w3, p + 2), gain)
+    s4 = [0.125 * folded([cells[8 * k + j, 1] for j in range(8)]) for k in range(groups)]
+    m4 = [0.5 * folded([cells[8 * k + j, 2] for j in range(8)]) for k in range(groups)]
+
+    def swept3(here, near, p):
+        gain = cells[jnp.clip(p, 0, ny - 1), 0] + gathered_inflow(near, t3, p + 2)
+        return keep * here + product(factors(w3, p + 2), gain)
 
     def pre(p0):
         planes = [va[p0 + i + 2] for i in range(BATCH + 2)]
         for i, near in enumerate(near_level3(planes)):
             p = p0 + i
-            gain = rhs(p) + gathered_inflow(near, t3, p + 2)
+            gain = cells[p, 0] + gathered_inflow(near, t3, p + 2)
             vb[p + 3] = keep * planes[i + 1] + product(factors(w3, p + 2), gain)
 
     batches(ny, pre)
@@ -476,46 +535,44 @@
         gains = []
         for i, near in enumerate(near_level3(planes)):
             p = p0 + i
-            gain = rhs(p) + gathered_inflow(near, t3, p + 2)
+            gain = cells[p, 0] + gathered_inflow(near, t3, p + 2)
             gains.append(gain - product(factors(g3, p + 2), planes[i + 1]))
-        ea[p0 // BATCH] = 0.5 * eightfold_compact(gains, compacted)
+        ea[p0 // BATCH] = 0.5 * folded(gains)
 
     batches(ny, restrict)
-    f4 = [ea[k] for k in range(groups)]
-    e4 = [product(factors(w4, k), f4[k]) for k in range(groups)]
-    for sweep in range(COARSE_SWEEPS - 1):
-        e4 = [
-            keep * e4[k] + product(factors(w4, k), f4[k] + gathered_inflow(near, t4, k))
-            for k, near in enumerate(near_level4(e4))
-        ]
-    for k in range(groups):
-        ea[k] = e4[k]
+    for k, q in enumerate(level4([ea[k] for k in range(groups)], s4, m4, t4)):
+        ea[k] = q
 
     mine = lax.axis_index("gy")
     lane = lanes(nz)
+    planes = []
     for d in range(-3, 4):
         p = mine + d
         on = jnp.where((p >= 0) & (p < ny), 1.0, 0.0)
         q = jnp.clip(p, 0, ny - 1)
         corr = jnp.take_along_axis(ea[q // 8], slot_lanes(lane, jnp.full((nz, LANES), q % 8, jnp.int32)), axis=1)
-        vb[p + 3] = vb[p + 3] + on * corr
-    for d in range(-2, 3):
-        va[mine + d + 3] = sweep3(vb, rhs(jnp.clip(mine + d, 0, ny - 1)), mine + d)
-    for d in range(-1, 2):
-        near_out[d + 1] = sweep3(va, rhs(jnp.clip(mine + d, 0, ny - 1)), mine + d)
-
-
-def eightfold_compact(planes, compacted):
-    return compacted([eightfold(q) for q in planes])
-
-
-def up_kernel(
-    counts, cells, cmid, cleft, cright, tz2, ty2, tx2, w2, v1, f1, tz1, ty1, tx1, w1, v0, f0, tz0, ty0, tx0, w0, out,
-    t3, w3, g3, t4, w4, s3, va, vb, ea, near, a2, b2, f2, e1, a1, b1, e0, a0, b0,
-):
+        planes.append(vb[p + 3] + on * corr)
+    for reach in (2, 1):
+        planes = [
+            swept3(here, near, mine + d)
+            for d, here, near in zip(range(-reach, reach + 1), planes[1:-1], near_level3(planes))
+        ]
+    return planes
+
+
+def up_kernel(counts, cells, cmid, cleft, cright, *rest):
+    keeps, out, rest = rest[:16], rest[16], rest[17:]
+    tz2, ty2, tx2, w2, v1, f1, tz1, ty1, tx1, w1, v0, f0, tz0, ty0, tx0, w0 = rest[:16]
+    t3, w3, g3, t4, s3, va, vb, ea, near, a2, b2, f2, e1, a1, b1, e0, a0, b0, sem = rest[16:]
+    copies = []
+    for i, dst in enumerate(rest[:16]):
+        dst = dst if i < 4 else dst.at[:, KEPT1] if i < 10 else dst.at[:, KEPT0]
+        copies.append(pltpu.make_async_copy(keeps[i], dst, sem.at[i]))
+    sent(copies)
     nz = counts[0]
     gz = lax.axis_index("gz")
-    coarse_solve(counts, cells, t3, w3, g3, t4, w4, s3, va, vb, ea, near)
+    for d, q in enumerate(coarse_solve(counts, cells, t3, w3, g3, t4, s3, va, vb, ea)):
+        near[d] = q
 
     lane4, zero4 = lanes(4), jnp.zeros((4, LANES), F32)
 
@@ -546,6 +603,7 @@
                 for z in (4 * dz + 4 + 2 * zz, 4 * dz + 5 + 2 * zz):
                     a2[c, z] = a2[c, z] + corr
 
+    landed(copies)
     each(1, 11, lambda z: put(b2, z, swept(z, 4, a2, f2, tz2, ty2, tx2, w2)))
     each(2, 10, lambda z: put(a2, z, swept(z, 4, b2, f2, tz2, ty2, tx2, w2)))
 
@@ -557,7 +615,14 @@
                 e1.at[c, z][pl.ds(16 + k, 4, stride=2), :] = q[12:16]
 
     each(2, 10, widen1)
-    each(5, 19, lambda z: put(a1, z, add(pair(v1, z), pair(e1, z // 2))))
+    def correct1(z):
+        e = pair(e1, z)
+        for k in (2 * z, 2 * z + 1):
+            put(a1, k, add(pair(v1, k), e))
+
+    each(3, 9, correct1)
+    for k, z in ((5, 2), (18, 9)):
+        put(a1, k, add(pair(v1, k), pair(e1, z)))
     each(6, 18, lambda z: put(b1, z, swept(z, 2, a1, f1, tz1, ty1, tx1, w1)))
     each(7, 17, lambda z: put(a1, z, swept(z, 2, b1, f1, tz1, ty1, tx1, w1)))
 
@@ -570,7 +635,12 @@
                 e0.at[c, z][pl.ds(20 + k, 2, stride=2), :] = q[22:24]
 
     each(7, 17, widen0)
-    each(2, 22, lambda z: put(a0, z, add(pair(v0, z), pair(e0, z // 2 + 6))))
+    def correct0(z):
+        e = pair(e0, z)
+        for k in (2 * z - 12, 2 * z - 11):
+            put(a0, k, add(pair(v0, k), e))
+
+    each(7, 17, correct0)
     each(3, 21, lambda z: put(b0, z, swept(z, 1, a0, f0, tz0, ty0, tx0, w0)))
 
     def last(z):
@@ -581,19 +651,19 @@
     each(4, 20, last)
 
 
-def spec_all(n, smem=()):
-    return [pl.BlockSpec(memory_space=pltpu.SMEM if i in smem else pltpu.VMEM) for i in range(n)]
-
-
-def run(kernel, name, args, outs, scratch, smem=()):
-    shapes = [jax.ShapeDtypeStruct(s, F32) for s in outs]
+def run(kernel, name, args, outs, scratch, smem=(), far_in=(), far_out=(), copies=0):
+    def specs(n, smem, far):
+        spaces = [pltpu.SMEM if i in smem else pltpu.HBM if i in far else pltpu.VMEM for i in range(n)]
+        return [pl.BlockSpec(memory_space=space) for space in spaces]
+
     return pl.pallas_call(
         kernel,
         name=name,
-        out_shape=shapes,
-        in_specs=spec_all(len(args), smem),
-        out_specs=spec_all(len(outs)),
-        scratch_shapes=[pltpu.VMEM(s, F32) for s in scratch],
+        out_shape=[jax.ShapeDtypeStruct(s, F32) for s in outs],
+        in_specs=specs(len(args), smem, far_in),
+        out_specs=specs(len(outs), (), far_out),
+        scratch_shapes=[pltpu.VMEM(s, F32) if isinstance(s, tuple) else s for s in scratch]
+        + ([pltpu.SemaphoreType.DMA((copies,))] if copies else []),
         compiler_params=pltpu.CompilerParams(vmem_limit_bytes=VMEM_BYTES),
     )(*args)
 
@@ -626,29 +696,46 @@
 
 def body(source, labels, phase_table):
     nz, ny = lax.axis_size("gz"), lax.axis_size("gy")
+
+    def edge(lo, hi):
+        return jnp.concatenate([source[:, lo:hi], labels[None, lo:hi].astype(F32)], axis=0)
+
+    up, down = shifts("gz")
+    zb = lax.ppermute(edge(12, 16), "gz", up)
+    za = lax.ppermute(edge(0, 4), "gz", down)
+
+    def side(lo, hi):
+        own = jnp.concatenate([source[:, :, lo:hi], labels[None, :, lo:hi].astype(F32)], axis=0)
+        return jnp.concatenate([zb[:, :, lo:hi], own, za[:, :, lo:hi]], axis=1)
+
+    up, down = shifts("gy")
+    left = lax.ppermute(side(12, 16), "gy", up)
+    right = lax.ppermute(side(0, 4), "gy", down)
+
     near_c, far_c = run(
         coeff_kernel, "coefficients", (labels, phase_table),
         [(2, 8, 8, LANES), (1, 2 * LANES)],
         [(4, 8, 16, LANES), (4, 8, 8, LANES), (4, 4, 4, LANES), (2, 8, LANES)], smem=(1,),
     )
-    fine = jnp.concatenate([source, labels.astype(F32)[None]], axis=0)
-
-    win = (2, 24, 24, LANES)
+    win, win2 = (2, 24, 24, LANES), (2, 12, 16, LANES)
+    win0 = (2, KEPT0.stop - KEPT0.start, 24, LANES)
+    win1 = (2, KEPT1.stop - KEPT1.start, 24, LANES)
     msg, *state0 = run(
         lambda *refs: fine_kernel((16 * nz, 16 * ny), *refs), "fine_down",
-        (*window(fine, 1, 4), phase_table, near_c),
-        [(3, 8, 8, LANES)] + [win] * 6,
-        [(24, 24, LANES)] + [win] * 4 + [(2, 8, 24, LANES)], smem=(3,),
+        (source, labels, zb, za, left, right, phase_table, near_c),
+        [(3, 8, 8, LANES)] + [win0] * 6,
+        [win] * 6 + [pltpu.VMEM((24, 24, LANES), jnp.int32)] + [win] * 4 + [(2, 8, 24, LANES)],
+        smem=(6,), far_out=range(1, 7), copies=6,
     )
-    win2 = (2, 12, 16, LANES)
     row, c_own, *state = run(
         lambda *refs: middle_kernel(((8 * nz, 8 * ny), (4 * nz, 4 * ny)), *refs), "middle_down",
         (*window(msg, 1, 8), far_c),
-        [(1, 3 * LANES), (4, 4, LANES)] + [win] * 6 + [win2] * 4,
-        [win] * 4 + [(2, 12, 24, LANES)] + [win2] * 6 + [(2, 2, 16, LANES), (8, LANES)],
+        [(8, LANES), (4, 4, LANES)] + [win1] * 6 + [win2] * 4,
+        [win] * 6 + [win2] * 4 + [win] * 4 + [(2, 12, 24, LANES)] + [win2] * 6 + [(2, 2, 16, LANES), (8, LANES)],
+        far_out=range(2, 12), copies=10,
     )
     state1, state2 = state[:6], state[6:]
-    column = shared(row[0], "gz")
+    column = shared(row, "gz")[:, 0:3].transpose(1, 0, 2)
     cells = shared(column, "gy")
     cwin = window(c_own, 0, 4)
 
@@ -660,9 +747,11 @@
         lambda *refs: up_kernel((nz, ny), *refs), "coarse_and_up",
         (cells, *cwin, *state2, *state1, *state0),
         [(2, 16, 16, LANES)],
-        [whole(12, 2), whole(2, 2), whole(2, 2), (12, *small), (2, *small)]
+        [win2] * 4 + [win] * 12
+        + [whole(12, 2), whole(2, 2), whole(2, 2), (12, *small)]
         + [whole(1, 1)[1:]] + [whole(1, 3)[1:]] * 2 + [small, (3, nz, LANES)]
         + [win2] * 3 + [(2, 12, 24, LANES), win, win, win, win, win],
+        far_in=range(4, 20), copies=16,
     )[0]
 
 

time: 148 us -> 138 us (0.932)
  waiting for transfers between devices: 17.7 us -> 24.7 us
  local copies, waits for them, and re-layouts: 23.4 us -> 18.1 us
  Pallas kernels: 28 us -> 23.1 us
  blocking collectives: 28.7 us -> 24.5 us
  starting transfers between devices: 46.9 us -> 44.5 us
    ppermute x0 -> x4, starting transfers between devices: none -> 13.9 us  [the longest x1 5.01 us: body(): left = lax.ppermute(side(12, 16), 'gy', up)]
    ppermute x6 -> x4, starting transfers between devices: 23.7 us -> 14 us  [around(): lax.ppermute(lax.slice_in_dim(block, size - width, size, axis=dim), axis,...]
    ppermute x6 -> x4, starting transfers between devices: 13.2 us -> 6.43 us  [around(): lax.ppermute(lax.slice_in_dim(block, 0, width, axis=dim), axis, down)]
    ppermute x0 -> x4, waiting for transfers between devices: none -> 6.63 us  [the longest x1 4.17 us: body(): za = lax.ppermute(edge(0, 4), 'gz', down)]
    unnamed x63 -> x50, local copies, waits for them, and re-layouts: 22.4 us -> 16.2 us
    pallas_call x4, Pallas kernels: 28 us -> 23.1 us  [run(): pl.pallas_call(kernel, name=name, out_shape=[jax.ShapeDtypeStruct(s, F32)...]
    all_to_all x1, blocking collectives: 28.7 us -> 24.5 us  [shared(): lax.all_to_all(jnp.broadcast_to(block[None], (n, *block.shape)), axis, 0, 0)]
    ppermute x6 -> x4, waiting for transfers between devices: 13.8 us -> 16 us  [around(): lax.ppermute(lax.slice_in_dim(block, 0, width, axis=dim), axis, down)]
where the time goes in v3:
time: 138 us; the launch traced here: 136 us
  starting transfers between devices  44.5 us (32%)
  waiting for transfers between devices  24.7 us (18%)
  blocking collectives  24.5 us (18%)
  Pallas kernels  23.1 us (17%)
  local copies, waits for them, and re-layouts  18.1 us (13%)
    all_to_all x1, blocking collectives, shared(): lax.all_to_all(jnp.broadcast_to(block[None], (n, *block.shape)), axis, 0, 0)  24.5 us
    pallas_call x4, Pallas kernels, run(): pl.pallas_call(kernel, name=name, out_shape=[jax.ShapeDtypeStruct(s, F32)...  23.1 us
    unnamed x50, local copies, waits for them, and re-layouts  16.2 us
    ppermute x4, waiting for transfers between devices, around(): lax.ppermute(lax.slice_in_dim(block, 0, width, axis=dim), axis, down)  16 us
    ppermute x4, starting transfers between devices, around(): lax.ppermute(lax.slice_in_dim(block, size - width, size, axis=dim), axis,...  14 us
    all_to_all x1, starting transfers between devices, shared(): lax.all_to_all(jnp.broadcast_to(block[None], (n, *block.shape)), axis, 0, 0)  10.2 us
    ppermute x4, starting transfers between devices, around(): lax.ppermute(lax.slice_in_dim(block, 0, width, axis=dim), axis, down)  6.43 us
    ppermute x1, starting transfers between devices, body(): left = lax.ppermute(side(12, 16), 'gy', up)  5.01 us
  transfers between devices with their start and end apart: 13, of which 8 were waited for; matrix products, arithmetic and copies ran while one was open for 0% of the time, Pallas kernels for 1%

profile of v3, /device:TPU:1, one launch (start us, length us, event | category | flops | bytes accessed | tf_op | source)
XLA Modules:
  0.0 136.1 jit_solution(2940354554999542732)
XLA Ops:
  1.7 4.5 %collective-permute-start = (f32[3,4,16,128]{3,2,1,0:T(8,128)S(1)}, f32[3,4,16,128]{3,2,1,0:T(8,128)S(1)}, u32[]{:S(2)}, u32[]{:S(2)}) collective-permute-start(f32[3,4,16,128]{3,2,1,0:T(8,128)S(1)} %pad_maximum_fusion.2), channel_id=1, source_target_pairs={{0,32},{32,64},{64,96},{96,128},{128,160},{160,192},{192,224},{224... | collective-permute-start | bytes 294920 | tf_op jit(solution)/shard_map/ppermute | solution.py:704
  6.2 1.4 %collective-permute-start.1 = (f32[3,4,16,128]{3,2,1,0:T(8,128)S(1)}, f32[3,4,16,128]{3,2,1,0:T(8,128)S(1)}, u32[]{:S(2)}, u32[]{:S(2)}) collective-permute-start(f32[3,4,16,128]{3,2,1,0:T(8,128)S(1)} %pad_maximum_fusion.3), channel_id=1, source_target_pairs={{32,0},{64,32},{96,64},{128,96},{160,128},{192,160},{224,192},{256... | collective-permute-start | bytes 294920 | tf_op jit(solution)/shard_map/ppermute | solution.py:705
  7.7 4.2 %collective-permute-done.1.refs_3_ = f32[3,4,16,128]{3,2,1,0:T(8,128)S(1)} collective-permute-done((f32[3,4,16,128]{3,2,1,0:T(8,128)S(1)}, f32[3,4,16,128]{3,2,1,0:T(8,128)S(1)}, u32[]{:S(2)}, u32[]{:S(2)}) %collective-permute-start.1) | collective-permute-done | bytes 98336 | tf_op jit(solution)/shard_map/ppermute | solution.py:705
  12.0 5.0 %collective-permute-start.2 = (f32[3,24,4,128]{3,2,1,0:T(4,128)S(1)}, f32[3,24,4,128]{3,2,1,0:T(4,128)S(1)}, u32[]{:S(2)}, u32[]{:S(2)}) collective-permute-start(f32[3,24,4,128]{3,2,1,0:T(4,128)S(1)} %pad_maximum_fusion), channel_id=1, source_target_pairs={{0,1},{1,2},{2,3},{3,4},{4,5},{5,6},{6,7},{7,8},{8,9},{9,10},{10,1... | collective-permute-start | bytes 442376 | tf_op jit(solution)/shard_map/ppermute | solution.py:712
  17.1 3.0 %collective-permute-start.3 = (f32[3,24,4,128]{3,2,1,0:T(4,128)S(1)}, f32[3,24,4,128]{3,2,1,0:T(4,128)S(1)}, u32[]{:S(2)}, u32[]{:S(2)}) collective-permute-start(f32[3,24,4,128]{3,2,1,0:T(4,128)S(1)} %pad_maximum_fusion.1), channel_id=1, source_target_pairs={{1,0},{2,1},{3,2},{4,3},{5,4},{6,5},{7,6},{8,7},{9,8},{10,9},{11,1... | collective-permute-start | bytes 442376 | tf_op jit(solution)/shard_map/ppermute | solution.py:713
  21.1 2.5 %collective-permute-done.3.refs_5_ = f32[3,24,4,128]{3,2,1,0:T(4,128)S(1)} collective-permute-done((f32[3,24,4,128]{3,2,1,0:T(4,128)S(1)}, f32[3,24,4,128]{3,2,1,0:T(4,128)S(1)}, u32[]{:S(2)}, u32[]{:S(2)}) %collective-permute-start.3) | collective-permute-done | bytes 147488 | tf_op jit(solution)/shard_map/ppermute | solution.py:713
  23.5 3.7 %fine_down.1 = (f32[3,8,8,128]{3,2,1,0:T(8,128)S(1)}, f32[2,20,24,128]{3,2,1,0:T(8,128)S(1)}, f32[2,20,24,128]{3,2,1,0:T(8,128)S(1)}, f32[2,20,24,128]{3,2,1,0:T...) custom-call(f32[2,16,16,128]{3,2,1,0:T(8,128)S(1)} %copy-done.1, ...), custom_call_target="tpu_custom_call" | custom-call | tf_op jit(solution)/shard_map/fine_down/pallas_call | solution.py:659
  27.3 3.5 %collective-permute-start.4 = (f32[3,8,8,128]{3,2,1,0:T(8,128)S(1)}, f32[3,8,8,128]{3,2,1,0:T(8,128)S(1)}, u32[]{:S(2)}, u32[]{:S(2)}) collective-permute-start(f32[3,8,8,128]{3,2,1,0:T(8,128)S(1)} %get-tuple-element.27), channel_id=1, source_target_pairs={{0,32},{32,64},{64,96},{96,128},{128,160},{160,192},{192,224},{224... | collective-permute-start | bytes 294920 | tf_op jit(solution)/shard_map/ppermute | solution.py:680
  30.8 1.3 collective-permute-start.5
  32.5 5.0 %collective-permute-done.5 = f32[3,8,8,128]{3,2,1,0:T(8,128)S(1)} collective-permute-done((f32[3,8,8,128]{3,2,1,0:T(8,128)S(1)}, f32[3,8,8,128]{3,2,1,0:T(8,128)S(1)}, u32[]{:S(2)}, u32[]{:S(2)}) %collective-permute-start.5) | collective-permute-done | bytes 98336 | tf_op jit(solution)/shard_map/ppermute | solution.py:681
  37.5 3.1 %collective-permute-start.6 = (f32[3,24,8,128]{3,2,1,0:T(8,128)S(1)}, f32[3,24,8,128]{3,2,1,0:T(8,128)S(1)}, u32[]{:S(2)}, u32[]{:S(2)}) collective-permute-start(f32[3,24,8,128]{3,2,1,0:T(8,128)S(1)} %constant_dynamic-update-slice_fusion.refs_0_), channel_id=1, source_target_pairs={{0,1},{1,2},{2,3},{3,4},{4,5},{5,6},{6,7},{7,8},{8,9},{9,10},{10,1... | collective-permute-start | bytes 884744 | tf_op jit(solution)/shard_map/ppermute | solution.py:680
  40.6 1.9 %collective-permute-start.7 = (f32[3,24,8,128]{3,2,1,0:T(8,128)S(1)}, f32[3,24,8,128]{3,2,1,0:T(8,128)S(1)}, u32[]{:S(2)}, u32[]{:S(2)}) collective-permute-start(f32[3,24,8,128]{3,2,1,0:T(8,128)S(1)} %constant_dynamic-update-slice_fusion.refs_0_), channel_id=1, source_target_pairs={{1,0},{2,1},{3,2},{4,3},{5,4},{6,5},{7,6},{8,7},{9,8},{10,9},{11,1... | collective-permute-start | bytes 884744 | tf_op jit(solution)/shard_map/ppermute | solution.py:681
  42.6 1.7 %collective-permute-done.6.refs_1_ = f32[3,24,8,128]{3,2,1,0:T(8,128)S(1)} collective-permute-done((f32[3,24,8,128]{3,2,1,0:T(8,128)S(1)}, f32[3,24,8,128]{3,2,1,0:T(8,128)S(1)}, u32[]{:S(2)}, u32[]{:S(2)}) %collective-permute-start.6) | collective-permute-done | bytes 294944 | tf_op jit(solution)/shard_map/ppermute | solution.py:680
  44.3 4.4 %collective-permute-done.7.refs_2_ = f32[3,24,8,128]{3,2,1,0:T(8,128)S(1)} collective-permute-done((f32[3,24,8,128]{3,2,1,0:T(8,128)S(1)}, f32[3,24,8,128]{3,2,1,0:T(8,128)S(1)}, u32[]{:S(2)}, u32[]{:S(2)}) %collective-permute-start.7) | collective-permute-done | bytes 294944 | tf_op jit(solution)/shard_map/ppermute | solution.py:681
  48.7 5.0 %middle_down.1 = (f32[8,128]{1,0:T(8,128)S(1)}, f32[4,4,128]{2,1,0:T(4,128)S(1)}, f32[2,14,24,128]{3,2,1,0:T(8,128)S(1)}, f32[2,14,24,128]{3,2,1,0:T(8,128)S(1)}...) custom-call(f32[3,24,8,128]{3,2,1,0:T(8,128)S(1)} %constant_dynamic-, ...), custom_call_target="tpu_custom_call" | custom-call | tf_op jit(solution)/shard_map/middle_down/pallas_call | solution.py:659
  60.2 24.5 %all_to_all.10 = f32[16,8,128]{2,1,0:T(8,128)S(1)} all-to-all(f32[16,8,128]{2,1,0:T(8,128)S(1)} %broadcast_in_dim.4), channel_id=1, replica_groups=mesh['gz'=16,'gy'=32] {'gz'}, dimensions={0} | all-to-all | bytes 131072 | tf_op jit(solution)/shard_map/all_to_all | solution.py:694
  85.7 10.2 %all-to-all-start.1 = ((f32[32,3,16,128]{3,2,1,0:T(8,128)}), f32[32,3,16,128]{3,2,1,0:T(8,128)S(1)}, u32[]{:S(2)}, u32[]{:S(2)}) async-start(f32[32,3,16,128]{3,2,1,0:T(8,128)} %broadcast_in_dim.5), calls=%async_computation.1 | async-start | bytes 1572864 | tf_op jit(solution)/shard_map/all_to_all | solution.py:694
  95.9 2.6 %collective-permute-start.8 = (f32[4,4,128]{2,1,0:T(4,128)S(1)}, f32[4,4,128]{2,1,0:T(4,128)S(1)}, u32[]{:S(2)}, u32[]{:S(2)}) collective-permute-start(f32[4,4,128]{2,1,0:T(4,128)S(1)} %get-tuple-element.30), channel_id=1, source_target_pairs={{0,32},{32,64},{64,96},{96,128},{128,160},{160,192},{192,224},{224... | collective-permute-start | bytes 24584 | tf_op jit(solution)/shard_map/ppermute | solution.py:680
  98.6 1.3 collective-permute-start.9
  99.9 3.4 %collective-permute-done.9 = f32[4,4,128]{2,1,0:T(4,128)S(1)} collective-permute-done((f32[4,4,128]{2,1,0:T(4,128)S(1)}, f32[4,4,128]{2,1,0:T(4,128)S(1)}, u32[]{:S(2)}, u32[]{:S(2)}) %collective-permute-start.9) | collective-permute-done | bytes 8224 | tf_op jit(solution)/shard_map/ppermute | solution.py:681
  103.3 4.7 %collective-permute-start.10 = (f32[12,4,128]{2,1,0:T(4,128)S(1)}, f32[12,4,128]{2,1,0:T(4,128)S(1)}, u32[]{:S(2)}, u32[]{:S(2)}) collective-permute-start(f32[12,4,128]{2,1,0:T(4,128)S(1)} %constant_dynamic-update-slice_fusion.3.refs_1_), channel_id=1, source_target_pairs={{0,1},{1,2},{2,3},{3,4},{4,5},{5,6},{6,7},{7,8},{8,9},{9,10},{10,1... | collective-permute-start | bytes 73736 | tf_op jit(solution)/shard_map/ppermute | solution.py:680
  107.9 1.9 %collective-permute-start.11 = (f32[12,4,128]{2,1,0:T(4,128)S(1)}, f32[12,4,128]{2,1,0:T(4,128)S(1)}, u32[]{:S(2)}, u32[]{:S(2)}) collective-permute-start(f32[12,4,128]{2,1,0:T(4,128)S(1)} %constant_dynamic-update-slice_fusion.3.refs_1_), channel_id=1, source_target_pairs={{1,0},{2,1},{3,2},{4,3},{5,4},{6,5},{7,6},{8,7},{9,8},{10,9},{11,1... | collective-permute-start | bytes 73736 | tf_op jit(solution)/shard_map/ppermute | solution.py:681
  109.9 3.2 %collective-permute-done.11.refs_3_ = f32[12,4,128]{2,1,0:T(4,128)S(1)} collective-permute-done((f32[12,4,128]{2,1,0:T(4,128)S(1)}, f32[12,4,128]{2,1,0:T(4,128)S(1)}, u32[]{:S(2)}, u32[]{:S(2)}) %collective-permute-start.11) | collective-permute-done | bytes 24608 | tf_op jit(solution)/shard_map/ppermute | solution.py:681
  122.8 13.3 %coarse_and_up.1 = f32[2,16,16,128]{3,2,1,0:T(8,128)} custom-call(f32[32,3,16,128]{3,2,1,0:T(8,128)S(1)} %all-to-all-done.1.refs_0_, f32[12,4,128]{2,1,0:T(4,128)S(1)} %constant_dynamic-update-slice_fusion.3.refs_1_, f32[12,4,128]{2,1,0:T(4,128)S(1)} %collective-permute-done.10.refs_2_, f32[12,4,128]{2,1,0:T(4,128)S(1)} %collective-permute-done.11.refs_3_, ...), custom_call_target="tpu_custom_call" | custom-call | tf_op jit(solution)/shard_map/coarse_and_up/pallas_call | solution.py:659
  (73 shorter events, 20.3 us)
Async XLA Ops:
  1.7 6.0 %copy-start.1 = (f32[2,16,16,128]{3,2,1,0:T(8,128)S(1)}, f32[2,16,16,128]{3,2,1,0:T(8,128)}, u32[]{:S(2)}) copy-start(f32[2,16,16,128]{3,2,1,0:T(8,128)} %refs_0_.1) | copy-start | bytes 786436
  1.7 10.2 %collective-permute-start = (f32[3,4,16,128]{3,2,1,0:T(8,128)S(1)}, f32[3,4,16,128]{3,2,1,0:T(8,128)S(1)}, u32[]{:S(2)}, u32[]{:S(2)}) collective-permute-start(f32[3,4,16,128]{3,2,1,0:T(8,128)S(1)} %pad_maximum_fusion.2), channel_id=1, source_target_pairs={{0,32},{32,64},{64,96},{96,128},{128,160},{160,192},{192,224},{224... | collective-permute-start | bytes 294920 | tf_op jit(solution)/shard_map/ppermute | solution.py:704
  6.2 1.5 %copy-start = (s32[16,16,128]{2,1,0:T(8,128)S(1)}, s32[16,16,128]{2,1,0:T(8,128)}, u32[]{:S(2)}) copy-start(s32[16,16,128]{2,1,0:T(8,128)} %refs_1_.1) | copy-start | bytes 393220
  6.2 5.7 %collective-permute-start.1 = (f32[3,4,16,128]{3,2,1,0:T(8,128)S(1)}, f32[3,4,16,128]{3,2,1,0:T(8,128)S(1)}, u32[]{:S(2)}, u32[]{:S(2)}) collective-permute-start(f32[3,4,16,128]{3,2,1,0:T(8,128)S(1)} %pad_maximum_fusion.3), channel_id=1, source_target_pairs={{32,0},{64,32},{96,64},{128,96},{160,128},{192,160},{224,192},{256... | collective-permute-start | bytes 294920 | tf_op jit(solution)/shard_map/ppermute | solution.py:705
  12.0 9.1 %collective-permute-start.2 = (f32[3,24,4,128]{3,2,1,0:T(4,128)S(1)}, f32[3,24,4,128]{3,2,1,0:T(4,128)S(1)}, u32[]{:S(2)}, u32[]{:S(2)}) collective-permute-start(f32[3,24,4,128]{3,2,1,0:T(4,128)S(1)} %pad_maximum_fusion), channel_id=1, source_target_pairs={{0,1},{1,2},{2,3},{3,4},{4,5},{5,6},{6,7},{7,8},{8,9},{9,10},{10,1... | collective-permute-start | bytes 442376 | tf_op jit(solution)/shard_map/ppermute | solution.py:712
  17.0 3.0 %copy-start.22 = (f32[4,4]{1,0:T(4,128)S(1)}, f32[4,4]{1,0:T(4,128)}, u32[]{:S(2)}) copy-start(f32[4,4]{1,0:T(4,128)} %refs_6_.1) | copy-start | bytes 196
  17.1 6.5 %collective-permute-start.3 = (f32[3,24,4,128]{3,2,1,0:T(4,128)S(1)}, f32[3,24,4,128]{3,2,1,0:T(4,128)S(1)}, u32[]{:S(2)}, u32[]{:S(2)}) collective-permute-start(f32[3,24,4,128]{3,2,1,0:T(4,128)S(1)} %pad_maximum_fusion.1), channel_id=1, source_target_pairs={{1,0},{2,1},{3,2},{4,3},{5,4},{6,5},{7,6},{8,7},{9,8},{10,9},{11,1... | collective-permute-start | bytes 442376 | tf_op jit(solution)/shard_map/ppermute | solution.py:713
  27.3 21.4 %copy-start.2 = (f32[2,20,24,128]{3,2,1,0:T(8,128)}, f32[2,20,24,128]{3,2,1,0:T(8,128)S(1)}, u32[]{:S(2)}) copy-start(f32[2,20,24,128]{3,2,1,0:T(8,128)S(1)} %get-tuple-element.46.refs_19_) | copy-start | bytes 1474564
  27.3 5.2 %collective-permute-start.4 = (f32[3,8,8,128]{3,2,1,0:T(8,128)S(1)}, f32[3,8,8,128]{3,2,1,0:T(8,128)S(1)}, u32[]{:S(2)}, u32[]{:S(2)}) collective-permute-start(f32[3,8,8,128]{3,2,1,0:T(8,128)S(1)} %get-tuple-element.27), channel_id=1, source_target_pairs={{0,32},{32,64},{64,96},{96,128},{128,160},{160,192},{192,224},{224... | collective-permute-start | bytes 294920 | tf_op jit(solution)/shard_map/ppermute | solution.py:680
  30.8 6.7 %collective-permute-start.5 = (f32[3,8,8,128]{3,2,1,0:T(8,128)S(1)}, f32[3,8,8,128]{3,2,1,0:T(8,128)S(1)}, u32[]{:S(2)}, u32[]{:S(2)}) collective-permute-start(f32[3,8,8,128]{3,2,1,0:T(8,128)S(1)} %get-tuple-element.27), channel_id=1, source_target_pairs={{32,0},{64,32},{96,64},{128,96},{160,128},{192,160},{224,192},{256... | collective-permute-start | bytes 294920 | tf_op jit(solution)/shard_map/ppermute | solution.py:681
  37.5 6.8 %collective-permute-start.6 = (f32[3,24,8,128]{3,2,1,0:T(8,128)S(1)}, f32[3,24,8,128]{3,2,1,0:T(8,128)S(1)}, u32[]{:S(2)}, u32[]{:S(2)}) collective-permute-start(f32[3,24,8,128]{3,2,1,0:T(8,128)S(1)} %constant_dynamic-update-slice_fusion.refs_0_), channel_id=1, source_target_pairs={{0,1},{1,2},{2,3},{3,4},{4,5},{5,6},{6,7},{7,8},{8,9},{9,10},{10,1... | collective-permute-start | bytes 884744 | tf_op jit(solution)/shard_map/ppermute | solution.py:680
  40.6 8.0 %collective-permute-start.7 = (f32[3,24,8,128]{3,2,1,0:T(8,128)S(1)}, f32[3,24,8,128]{3,2,1,0:T(8,128)S(1)}, u32[]{:S(2)}, u32[]{:S(2)}) collective-permute-start(f32[3,24,8,128]{3,2,1,0:T(8,128)S(1)} %constant_dynamic-update-slice_fusion.refs_0_), channel_id=1, source_target_pairs={{1,0},{2,1},{3,2},{4,3},{5,4},{6,5},{7,6},{8,7},{9,8},{10,9},{11,1... | collective-permute-start | bytes 884744 | tf_op jit(solution)/shard_map/ppermute | solution.py:681
  85.7 27.4 %all-to-all-start.1 = ((f32[32,3,16,128]{3,2,1,0:T(8,128)}), f32[32,3,16,128]{3,2,1,0:T(8,128)S(1)}, u32[]{:S(2)}, u32[]{:S(2)}) async-start(f32[32,3,16,128]{3,2,1,0:T(8,128)} %broadcast_in_dim.5), calls=%async_computation.1 | async-start | bytes 1572864 | tf_op jit(solution)/shard_map/all_to_all | solution.py:694
  95.9 4.0 %collective-permute-start.8 = (f32[4,4,128]{2,1,0:T(4,128)S(1)}, f32[4,4,128]{2,1,0:T(4,128)S(1)}, u32[]{:S(2)}, u32[]{:S(2)}) collective-permute-start(f32[4,4,128]{2,1,0:T(4,128)S(1)} %get-tuple-element.30), channel_id=1, source_target_pairs={{0,32},{32,64},{64,96},{96,128},{128,160},{160,192},{192,224},{224... | collective-permute-start | bytes 24584 | tf_op jit(solution)/shard_map/ppermute | solution.py:680
  98.6 4.7 %collective-permute-start.9 = (f32[4,4,128]{2,1,0:T(4,128)S(1)}, f32[4,4,128]{2,1,0:T(4,128)S(1)}, u32[]{:S(2)}, u32[]{:S(2)}) collective-permute-start(f32[4,4,128]{2,1,0:T(4,128)S(1)} %get-tuple-element.30), channel_id=1, source_target_pairs={{32,0},{64,32},{96,64},{128,96},{160,128},{192,160},{224,192},{256... | collective-permute-start | bytes 24584 | tf_op jit(solution)/shard_map/ppermute | solution.py:681
  103.3 6.6 %collective-permute-start.10 = (f32[12,4,128]{2,1,0:T(4,128)S(1)}, f32[12,4,128]{2,1,0:T(4,128)S(1)}, u32[]{:S(2)}, u32[]{:S(2)}) collective-permute-start(f32[12,4,128]{2,1,0:T(4,128)S(1)} %constant_dynamic-update-slice_fusion.3.refs_1_), channel_id=1, source_target_pairs={{0,1},{1,2},{2,3},{3,4},{4,5},{5,6},{6,7},{7,8},{8,9},{9,10},{10,1... | collective-permute-start | bytes 73736 | tf_op jit(solution)/shard_map/ppermute | solution.py:680
  107.9 5.1 %collective-permute-start.11 = (f32[12,4,128]{2,1,0:T(4,128)S(1)}, f32[12,4,128]{2,1,0:T(4,128)S(1)}, u32[]{:S(2)}, u32[]{:S(2)}) collective-permute-start(f32[12,4,128]{2,1,0:T(4,128)S(1)} %constant_dynamic-update-slice_fusion.3.refs_1_), channel_id=1, source_target_pairs={{1,0},{2,1},{3,2},{4,3},{5,4},{6,5},{7,6},{8,7},{9,8},{10,9},{11,1... | collective-permute-start | bytes 73736 | tf_op jit(solution)/shard_map/ppermute | solution.py:681
  113.1 1.0 copy-start.3
  114.1 1.0 copy-start.5
  115.1 1.0 copy-start.7
  116.1 1.0 copy-start.9
  117.1 1.0 copy-start.11
  118.0 1.0 copy-start.13
  119.0 1.0 copy-start.15
  (12 other events, 9.3 us)

commit v4 on v3

--- a/solution.py
+++ b/solution.py
@@ -12,7 +12,8 @@
 keep = 1.0 - relax
 mass_scale = 0.01
 F32 = jnp.float32
-VMEM_BYTES = 40 * 1024 * 1024
+MESSAGE = 24
+MOST_VMEM = 60 * 1024 * 1024
 
 
 def lanes(rows):
@@ -48,20 +49,17 @@
     return jnp.where(even, q, ahead_x(q, -1)), jnp.where(even, ahead_x(q, 1), q)
 
 
-def each(lo, hi, body, most=11):
-    n = hi - lo
-    step = max(k for k in range(1, most + 1) if n % k == 0)
-    if step == n:
-        for z in range(lo, hi):
-            body(z)
-        return
+def each(lo, hi, body, step=4):
+    full = (hi - lo) // step
 
     def run(i, carry):
         for j in range(step):
             body(lo + i * step + j)
         return carry
 
-    lax.fori_loop(0, n // step, run, 0)
+    lax.fori_loop(0, full, run, 0)
+    for z in range(lo + full * step, hi):
+        body(z)
 
 
 def sent(copies):
@@ -210,7 +208,7 @@
 def fine_kernel(
     sizes, source, labels, zb, za, left, right, table, near_c, msg_out, *rest
 ):
-    keeps, (v, f, tz, ty, tx, w, lab, s, m, g, first, buf, sem) = rest[:6], rest[6:]
+    keeps, v, f, tz, ty, tx, w, lab, s, m, g, first, buf, sem = rest
     first_z = lax.axis_index("gz") * 16 - 4
     first_y = lax.axis_index("gy") * 16
 
@@ -238,7 +236,7 @@
     each(1, 23, faces)
 
     def kept(i, ref):
-        return pltpu.make_async_copy(ref.at[:, KEPT0], keeps[i], sem.at[i])
+        return pltpu.make_async_copy(ref.at[:, KEPT0], keeps.at[i], sem.at[i])
 
     copies = sent([kept(i, ref) for i, ref in enumerate((v, f, tz, ty, tx, w)) if i])
     each(2, 22, lambda z: put(v, z, swept(z, 1, first, f, tz, ty, tx, w)))
@@ -263,9 +261,9 @@
 
 def middle_kernel(
     sizes, mid, left, right, far_c,
-    row_out, c_out, *rest
+    msg_out, *rest
 ):
-    keeps, rest = rest[:10], rest[10:]
+    keeps, rest = rest[0], rest[1:]
     v, f, tz, ty, tx, w, tz2, ty2, tx2, w2, s, m, g, first, buf, s2, m2, f2, g2, first2, v2, buf2, stack, sem = rest
     gz, gy = lax.axis_index("gz"), lax.axis_index("gy")
 
@@ -285,7 +283,7 @@
     each(1, 23, faces)
 
     def kept(i, ref):
-        return pltpu.make_async_copy(ref.at[:, KEPT1], keeps[i], sem.at[i])
+        return pltpu.make_async_copy(ref.at[:, KEPT1], keeps.at[i], sem.at[i])
 
     copies = sent([kept(i, ref) for i, ref in enumerate((v, f, tz, ty, tx, w)) if i])
     each(2, 22, lambda z: put(v, z, swept(z, 2, first, f, tz, ty, tx, w)))
@@ -316,12 +314,12 @@
     tz2[1, 0] = 0.5 * (s2[1, 0] + s2[1, 1])
     each(2, 10, lambda z: put(first2, z, times(faces2(z), pair(f2, z))))
     faces2(10)
-    copies += sent([pltpu.make_async_copy(ref, keeps[6 + i], sem.at[6 + i]) for i, ref in enumerate((tz2, ty2, tx2, w2))])
+    copies += sent([pltpu.make_async_copy(ref, keeps.at[6 + i, :, 0:12, 0:16], sem.at[6 + i]) for i, ref in enumerate((tz2, ty2, tx2, w2))])
     each(3, 9, lambda z: put(v2, z, swept(z, 4, first2, f2, tz2, ty2, tx2, w2)))
     which = lanes(4) & 3
     for z in range(4):
         a, b = pair(v2, z + 4), pair(f2, z + 4)
-        c_out[z] = jnp.where(
+        msg_out[8 + 4 * z : 12 + 4 * z] = jnp.where(
             which < 2, jnp.where(which == 0, a[0][0:4], a[1][0:4]), jnp.where(which == 2, b[0][0:4], b[1][0:4])
         )
     for z in range(2):
@@ -331,11 +329,26 @@
     for z in range(2):
         for c in (0, 1):
             stack[4 * c + 2 * z : 4 * c + 2 * z + 2] = 0.5 * pair_x(rows_paired(buf2, (c, z), 0, 2), 4)
-    row_out[0:1] = packed_row(stack[...])
-    row_out[1:2] = far_c[:, 0:LANES]
-    row_out[2:3] = far_c[:, LANES : 2 * LANES]
-    row_out[3:8] = jnp.zeros((5, LANES), F32)
+    msg_out[0:1] = packed_row(stack[...])
+    msg_out[1:2] = far_c[:, 0:LANES]
+    msg_out[2:3] = far_c[:, LANES : 2 * LANES]
+    msg_out[3:8] = jnp.zeros((5, LANES), F32)
     landed(copies)
+
+
+def spread_kernel(column, cells, near):
+    ny, _, nz, _ = cells.shape
+    for k in range(3):
+        q = column[pl.ds(k, nz, stride=MESSAGE), :]
+        for p in range(ny):
+            cells[p, k] = q
+    mine = lax.axis_index("gz")
+    for d in (-1, 0, 1):
+        p = jnp.clip(mine + d, 0, nz - 1)
+        on = jnp.where((mine + d >= 0) & (mine + d < nz), 1.0, 0.0)
+        q = on * column[pl.ds(pl.multiple_of(p * MESSAGE + 8, 8), 16), :]
+        for z in range(4):
+            near[4 * d + 4 + z] = q[4 * z : 4 * z + 4]
 
 
 def real_lanes(rows):
@@ -561,13 +574,17 @@
 
 
 def up_kernel(counts, cells, cmid, cleft, cright, *rest):
-    keeps, out, rest = rest[:16], rest[16], rest[17:]
+    kept1, kept0, out, rest = rest[0], rest[1], rest[2], rest[3:]
     tz2, ty2, tx2, w2, v1, f1, tz1, ty1, tx1, w1, v0, f0, tz0, ty0, tx0, w0 = rest[:16]
     t3, w3, g3, t4, s3, va, vb, ea, near, a2, b2, f2, e1, a1, b1, e0, a0, b0, sem = rest[16:]
     copies = []
     for i, dst in enumerate(rest[:16]):
-        dst = dst if i < 4 else dst.at[:, KEPT1] if i < 10 else dst.at[:, KEPT0]
-        copies.append(pltpu.make_async_copy(keeps[i], dst, sem.at[i]))
+        src, dst = (
+            (kept1.at[6 + i, :, 0:12, 0:16], dst) if i < 4
+            else (kept1.at[i - 4], dst.at[:, KEPT1]) if i < 10
+            else (kept0.at[i - 10], dst.at[:, KEPT0])
+        )
+        copies.append(pltpu.make_async_copy(src, dst, sem.at[i]))
     sent(copies)
     nz = counts[0]
     gz = lax.axis_index("gz")
@@ -651,7 +668,7 @@
     each(4, 20, last)
 
 
-def run(kernel, name, args, outs, scratch, smem=(), far_in=(), far_out=(), copies=0):
+def run(kernel, name, args, outs, scratch, smem=(), far_in=(), far_out=(), copies=0, vmem=32 * 1024 * 1024):
     def specs(n, smem, far):
         spaces = [pltpu.SMEM if i in smem else pltpu.HBM if i in far else pltpu.VMEM for i in range(n)]
         return [pl.BlockSpec(memory_space=space) for space in spaces]
@@ -664,7 +681,7 @@
         out_specs=specs(len(outs), (), far_out),
         scratch_shapes=[pltpu.VMEM(s, F32) if isinstance(s, tuple) else s for s in scratch]
         + ([pltpu.SemaphoreType.DMA((copies,))] if copies else []),
-        compiler_params=pltpu.CompilerParams(vmem_limit_bytes=VMEM_BYTES),
+        compiler_params=pltpu.CompilerParams(vmem_limit_bytes=vmem),
     )(*args)
 
 
@@ -689,23 +706,20 @@
     return mid, left, right
 
 
-def shared(block, axis):
-    n = lax.axis_size(axis)
-    return lax.all_to_all(jnp.broadcast_to(block[None], (n, *block.shape)), axis, 0, 0)
-
-
 def body(source, labels, phase_table):
     nz, ny = lax.axis_size("gz"), lax.axis_size("gy")
 
+    marks = lax.optimization_barrier(labels.astype(F32))[None]
+
     def edge(lo, hi):
-        return jnp.concatenate([source[:, lo:hi], labels[None, lo:hi].astype(F32)], axis=0)
+        return jnp.concatenate([source[:, lo:hi], marks[:, lo:hi]], axis=0)
 
     up, down = shifts("gz")
     zb = lax.ppermute(edge(12, 16), "gz", up)
     za = lax.ppermute(edge(0, 4), "gz", down)
 
     def side(lo, hi):
-        own = jnp.concatenate([source[:, :, lo:hi], labels[None, :, lo:hi].astype(F32)], axis=0)
+        own = jnp.concatenate([source[:, :, lo:hi], marks[:, :, lo:hi]], axis=0)
         return jnp.concatenate([zb[:, :, lo:hi], own, za[:, :, lo:hi]], axis=1)
 
     up, down = shifts("gy")
@@ -720,24 +734,26 @@
     win, win2 = (2, 24, 24, LANES), (2, 12, 16, LANES)
     win0 = (2, KEPT0.stop - KEPT0.start, 24, LANES)
     win1 = (2, KEPT1.stop - KEPT1.start, 24, LANES)
-    msg, *state0 = run(
+    msg, state0 = run(
         lambda *refs: fine_kernel((16 * nz, 16 * ny), *refs), "fine_down",
         (source, labels, zb, za, left, right, phase_table, near_c),
-        [(3, 8, 8, LANES)] + [win0] * 6,
+        [(3, 8, 8, LANES), (12, *win0)],
         [win] * 6 + [pltpu.VMEM((24, 24, LANES), jnp.int32)] + [win] * 4 + [(2, 8, 24, LANES)],
-        smem=(6,), far_out=range(1, 7), copies=6,
+        smem=(6,), far_out=(1,), copies=6, vmem=MOST_VMEM,
     )
-    row, c_own, *state = run(
+    msg, state1 = run(
         lambda *refs: middle_kernel(((8 * nz, 8 * ny), (4 * nz, 4 * ny)), *refs), "middle_down",
         (*window(msg, 1, 8), far_c),
-        [(8, LANES), (4, 4, LANES)] + [win1] * 6 + [win2] * 4,
+        [(MESSAGE, LANES), (20, *win1)],
         [win] * 6 + [win2] * 4 + [win] * 4 + [(2, 12, 24, LANES)] + [win2] * 6 + [(2, 2, 16, LANES), (8, LANES)],
-        far_out=range(2, 12), copies=10,
+        far_out=(1,), copies=10, vmem=MOST_VMEM,
     )
-    state1, state2 = state[:6], state[6:]
-    column = shared(row, "gz")[:, 0:3].transpose(1, 0, 2)
-    cells = shared(column, "gy")
-    cwin = window(c_own, 0, 4)
+    column = lax.all_to_all(jnp.broadcast_to(msg[None], (nz, MESSAGE, LANES)), "gz", 0, 0)
+    cells, cmid = run(
+        spread_kernel, "spread", (column.reshape(nz * MESSAGE, LANES),), [(ny, 3, nz, LANES), (12, 4, LANES)], [],
+    )
+    cells = lax.all_to_all(cells, "gy", 0, 0)
+    cwin = (cmid, *around(cmid, "gy", 1, 4))
 
     def whole(n, pad):
         return (n, ny + 2 * pad, nz, LANES)
@@ -745,13 +761,13 @@
     small = (ny // 8, nz, LANES)
     return run(
         lambda *refs: up_kernel((nz, ny), *refs), "coarse_and_up",
-        (cells, *cwin, *state2, *state1, *state0),
+        (cells, *cwin, state1, state0),
         [(2, 16, 16, LANES)],
         [win2] * 4 + [win] * 12
         + [whole(12, 2), whole(2, 2), whole(2, 2), (12, *small)]
         + [whole(1, 1)[1:]] + [whole(1, 3)[1:]] * 2 + [small, (3, nz, LANES)]
         + [win2] * 3 + [(2, 12, 24, LANES), win, win, win, win, win],
-        far_in=range(4, 20), copies=16,
+        far_in=(4, 5), copies=16, vmem=MOST_VMEM,
     )[0]
 
 

time: 138 us -> 125 us (0.906)
  local copies, waits for them, and re-layouts: 18.1 us -> 8.6 us
  waiting for transfers between devices: 24.7 us -> 20.1 us
  starting transfers between devices: 44.5 us -> 41.3 us
  Pallas kernels: 23.1 us -> 25.8 us
  blocking collectives: 24.5 us -> 26.9 us
    unnamed x50 -> x32, local copies, waits for them, and re-layouts: 16.2 us -> 5.95 us
    ppermute x4 -> x3, waiting for transfers between devices: 16 us -> 9 us  [around(): lax.ppermute(lax.slice_in_dim(block, 0, width, axis=dim), axis, down)]
    all_to_all x1, waiting for transfers between devices: 0.01 us -> 6.13 us  [body(): cells = lax.all_to_all(cells, 'gy', 0, 0)]
    pallas_call x4 -> x5, Pallas kernels: 23.1 us -> 25.8 us  [run(): pl.pallas_call(kernel, name=name, out_shape=[jax.ShapeDtypeStruct(s, F32)...]
    ppermute x4 -> x3, starting transfers between devices: 14 us -> 11.4 us  [around(): lax.ppermute(lax.slice_in_dim(block, size - width, size, axis=dim), axis,...]
    ppermute x1, waiting for transfers between devices: 2.46 us -> 0.01 us  [body(): right = lax.ppermute(side(0, 4), 'gy', down)]
    all_to_all x1, blocking collectives: 24.5 us -> 26.9 us  [body(): lax.all_to_all(jnp.broadcast_to(msg[None], (nz, MESSAGE, LANES)), 'gz', 0...]
    ppermute x4 -> x3, starting transfers between devices: 6.43 us -> 5.36 us  [around(): lax.ppermute(lax.slice_in_dim(block, 0, width, axis=dim), axis, down)]
  transfers between devices with their start and end apart: 13 -> 11, of which waited for: 8 -> 7; matrix products, arithmetic and copies ran while one was open for 0% -> 2% of each run, Pallas kernels for 1% -> 1%
where the time goes in v4:
time: 125 us; the launch traced here: 124 us
  starting transfers between devices  41.3 us (33%)
  blocking collectives  26.9 us (22%)
  Pallas kernels  25.8 us (21%)
  waiting for transfers between devices  20.1 us (16%)
  local copies, waits for them, and re-layouts  8.6 us (7%)
    all_to_all x1, blocking collectives, body(): lax.all_to_all(jnp.broadcast_to(msg[None], (nz, MESSAGE, LANES)), 'gz', 0...  26.9 us
    pallas_call x5, Pallas kernels, run(): pl.pallas_call(kernel, name=name, out_shape=[jax.ShapeDtypeStruct(s, F32)...  25.8 us
    ppermute x3, starting transfers between devices, around(): lax.ppermute(lax.slice_in_dim(block, size - width, size, axis=dim), axis,...  11.4 us
    all_to_all x1, starting transfers between devices, body(): cells = lax.all_to_all(cells, 'gy', 0, 0)  10.9 us
    ppermute x3, waiting for transfers between devices, around(): lax.ppermute(lax.slice_in_dim(block, 0, width, axis=dim), axis, down)  9 us
    all_to_all x1, waiting for transfers between devices, body(): cells = lax.all_to_all(cells, 'gy', 0, 0)  6.13 us
    unnamed x32, local copies, waits for them, and re-layouts  5.95 us
    ppermute x3, starting transfers between devices, around(): lax.ppermute(lax.slice_in_dim(block, 0, width, axis=dim), axis, down)  5.36 us
  transfers between devices with their start and end apart: 11, of which 7 were waited for; matrix products, arithmetic and copies ran while one was open for 2% of the time, Pallas kernels for 1%

profile of v4, /device:TPU:1, one launch (start us, length us, event | category | flops | bytes accessed | tf_op | source)
XLA Modules:
  0.0 124.0 jit_solution(16328048613030045086)
XLA Ops:
  1.8 4.4 %collective-permute-start = (f32[3,4,16,128]{3,2,1,0:T(8,128)S(1)}, f32[3,4,16,128]{3,2,1,0:T(8,128)S(1)}, u32[]{:S(2)}, u32[]{:S(2)}) collective-permute-start(f32[3,4,16,128]{3,2,1,0:T(8,128)S(1)} %pad_maximum_fusion.2), channel_id=1, source_target_pairs={{0,32},{32,64},{64,96},{96,128},{128,160},{160,192},{192,224},{224... | collective-permute-start | bytes 294920 | tf_op jit(solution)/shard_map/ppermute | solution.py:718
  6.2 1.3 %collective-permute-start.1 = (f32[3,4,16,128]{3,2,1,0:T(8,128)S(1)}, f32[3,4,16,128]{3,2,1,0:T(8,128)S(1)}, u32[]{:S(2)}, u32[]{:S(2)}) collective-permute-start(f32[3,4,16,128]{3,2,1,0:T(8,128)S(1)} %pad_maximum_fusion.3), channel_id=1, source_target_pairs={{32,0},{64,32},{96,64},{128,96},{160,128},{192,160},{224,192},{256... | collective-permute-start | bytes 294920 | tf_op jit(solution)/shard_map/ppermute | solution.py:719
  7.5 1.0 fusion
  8.6 3.2 %collective-permute-done.1.refs_3_ = f32[3,4,16,128]{3,2,1,0:T(8,128)S(1)} collective-permute-done((f32[3,4,16,128]{3,2,1,0:T(8,128)S(1)}, f32[3,4,16,128]{3,2,1,0:T(8,128)S(1)}, u32[]{:S(2)}, u32[]{:S(2)}) %collective-permute-start.1) | collective-permute-done | bytes 98336 | tf_op jit(solution)/shard_map/ppermute | solution.py:719
  11.8 5.0 %collective-permute-start.2 = (f32[3,24,4,128]{3,2,1,0:T(4,128)S(1)}, f32[3,24,4,128]{3,2,1,0:T(4,128)S(1)}, u32[]{:S(2)}, u32[]{:S(2)}) collective-permute-start(f32[3,24,4,128]{3,2,1,0:T(4,128)S(1)} %pad_maximum_fusion), channel_id=1, source_target_pairs={{0,1},{1,2},{2,3},{3,4},{4,5},{5,6},{6,7},{7,8},{8,9},{9,10},{10,1... | collective-permute-start | bytes 442376 | tf_op jit(solution)/shard_map/ppermute | solution.py:726
  16.9 3.0 %collective-permute-start.3 = (f32[3,24,4,128]{3,2,1,0:T(4,128)S(1)}, f32[3,24,4,128]{3,2,1,0:T(4,128)S(1)}, u32[]{:S(2)}, u32[]{:S(2)}) collective-permute-start(f32[3,24,4,128]{3,2,1,0:T(4,128)S(1)} %pad_maximum_fusion.1), channel_id=1, source_target_pairs={{1,0},{2,1},{3,2},{4,3},{5,4},{6,5},{7,6},{8,7},{9,8},{10,9},{11,1... | collective-permute-start | bytes 442376 | tf_op jit(solution)/shard_map/ppermute | solution.py:727
  21.5 1.0 coefficients.1
  24.4 4.5 %fine_down.1 = (f32[3,8,8,128]{3,2,1,0:T(8,128)}, f32[12,2,20,24,128]{4,3,2,1,0:T(8,128)}) custom-call(f32[2,16,16,128]{3,2,1,0:T(8,128)} %refs_0_.1, s32[16,16,128]{2,1,0:T(8,128)} %refs_1_.1, f32[3,4,16,128]{3,2,1,0:T(8,128)} %copy-done.9, f32[3,4,16,128]{3,2,1,0:T(8,128)} %copy-done.10, f32[3,24,4,128]{3,2,1,0:T(4,128)} %copy-done.11, ...), custom_call_target="tpu_custom_call" | custom-call | tf_op jit(solution)/shard_map/fine_down/pallas_call | solution.py:676
  28.9 3.2 %collective-permute-start.4 = (f32[3,8,8,128]{3,2,1,0:T(8,128)}, f32[3,8,8,128]{3,2,1,0:T(8,128)S(1)}, u32[]{:S(2)}, u32[]{:S(2)}) collective-permute-start(f32[3,8,8,128]{3,2,1,0:T(8,128)} %get-tuple-element.14), channel_id=1, source_target_pairs={{0,32},{32,64},{64,96},{96,128},{128,160},{160,192},{192,224},{224... | collective-permute-start | bytes 294920 | tf_op jit(solution)/shard_map/ppermute | solution.py:697
  32.1 1.3 %collective-permute-start.5 = (f32[3,8,8,128]{3,2,1,0:T(8,128)}, f32[3,8,8,128]{3,2,1,0:T(8,128)S(1)}, u32[]{:S(2)}, u32[]{:S(2)}) collective-permute-start(f32[3,8,8,128]{3,2,1,0:T(8,128)} %get-tuple-element.14), channel_id=1, source_target_pairs={{32,0},{64,32},{96,64},{128,96},{160,128},{192,160},{224,192},{256... | collective-permute-start | bytes 294920 | tf_op jit(solution)/shard_map/ppermute | solution.py:698
  34.9 4.0 %collective-permute-done.5 = f32[3,8,8,128]{3,2,1,0:T(8,128)S(1)} collective-permute-done((f32[3,8,8,128]{3,2,1,0:T(8,128)}, f32[3,8,8,128]{3,2,1,0:T(8,128)S(1)}, u32[]{:S(2)}, u32[]{:S(2)}) %collective-permute-start.5) | collective-permute-done | bytes 98336 | tf_op jit(solution)/shard_map/ppermute | solution.py:698
  38.9 1.9 %collective-permute-start.7 = (f32[3,24,8,128]{3,2,1,0:T(8,128)S(1)}, f32[3,24,8,128]{3,2,1,0:T(8,128)S(1)}, u32[]{:S(2)}, u32[]{:S(2)}) collective-permute-start(f32[3,24,8,128]{3,2,1,0:T(8,128)S(1)} %constant_dynamic-update-slice_fusion.refs_0_), channel_id=1, source_target_pairs={{1,0},{2,1},{3,2},{4,3},{5,4},{6,5},{7,6},{8,7},{9,8},{10,9},{11,1... | collective-permute-start | bytes 884744 | tf_op jit(solution)/shard_map/ppermute | solution.py:698
  40.9 4.8 %collective-permute-start.6 = (f32[3,24,8,128]{3,2,1,0:T(8,128)S(1)}, f32[3,24,8,128]{3,2,1,0:T(8,128)S(1)}, u32[]{:S(2)}, u32[]{:S(2)}) collective-permute-start(f32[3,24,8,128]{3,2,1,0:T(8,128)S(1)} %constant_dynamic-update-slice_fusion.refs_0_), channel_id=1, source_target_pairs={{0,1},{1,2},{2,3},{3,4},{4,5},{5,6},{6,7},{7,8},{8,9},{9,10},{10,1... | collective-permute-start | bytes 884744 | tf_op jit(solution)/shard_map/ppermute | solution.py:697
  45.7 2.5 %collective-permute-done.7.refs_2_ = f32[3,24,8,128]{3,2,1,0:T(8,128)S(1)} collective-permute-done((f32[3,24,8,128]{3,2,1,0:T(8,128)S(1)}, f32[3,24,8,128]{3,2,1,0:T(8,128)S(1)}, u32[]{:S(2)}, u32[]{:S(2)}) %collective-permute-start.7) | collective-permute-done | bytes 294944 | tf_op jit(solution)/shard_map/ppermute | solution.py:698
  48.2 1.2 collective-permute-done.6.refs_1_
  50.1 6.9 %middle_down.1 = (f32[24,128]{1,0:T(8,128)}, f32[20,2,14,24,128]{4,3,2,1,0:T(8,128)}) custom-call(f32[3,24,8,128]{3,2,1,0:T(8,128)} %copy-done.6, f32[3,24,8,128]{3,2,1,0:T(8,128)} %copy-done.8, f32[3,24,8,128]{3,2,1,0:T(8,128)} %copy-done.7, f32[1,256]{1,0:T(1,128)} %copy-done.4), custom_call_target="tpu_custom_call" | custom-call | tf_op jit(solution)/shard_map/middle_down/pallas_call | solution.py:676
  57.7 26.9 %all_to_all.10 = f32[16,24,128]{2,1,0:T(8,128)S(1)} all-to-all(f32[16,24,128]{2,1,0:T(8,128)S(1)} %broadcast_in_dim.10), channel_id=1, replica_groups=mesh['gz'=16,'gy'=32] {'gz'}, dimensions={0} | all-to-all | bytes 393216 | tf_op jit(solution)/shard_map/all_to_all | solution.py:751
  84.5 0.9 spread.1
  85.5 10.9 %all-to-all-start.1 = ((f32[32,3,16,128]{3,2,1,0:T(8,128)}), f32[32,3,16,128]{3,2,1,0:T(8,128)S(1)}, u32[]{:S(2)}, u32[]{:S(2)}) async-start(f32[32,3,16,128]{3,2,1,0:T(8,128)} %get-tuple-element.17), calls=%async_computation.1 | async-start | bytes 1572864 | tf_op jit(solution)/shard_map/all_to_all | solution.py:755
  96.4 2.1 %collective-permute-start.9 = (f32[12,4,128]{2,1,0:T(4,128)S(1)}, f32[12,4,128]{2,1,0:T(4,128)S(1)}, u32[]{:S(2)}, u32[]{:S(2)}) collective-permute-start(f32[12,4,128]{2,1,0:T(4,128)S(1)} %get-tuple-element.18.refs_1_), channel_id=1, source_target_pairs={{1,0},{2,1},{3,2},{4,3},{5,4},{6,5},{7,6},{8,7},{9,8},{10,9},{11,1... | collective-permute-start | bytes 73736 | tf_op jit(solution)/shard_map/ppermute | solution.py:698
  98.5 3.4 %collective-permute-start.8 = (f32[12,4,128]{2,1,0:T(4,128)S(1)}, f32[12,4,128]{2,1,0:T(4,128)S(1)}, u32[]{:S(2)}, u32[]{:S(2)}) collective-permute-start(f32[12,4,128]{2,1,0:T(4,128)S(1)} %get-tuple-element.18.refs_1_), channel_id=1, source_target_pairs={{0,1},{1,2},{2,3},{3,4},{4,5},{5,6},{6,7},{7,8},{8,9},{9,10},{10,1... | collective-permute-start | bytes 73736 | tf_op jit(solution)/shard_map/ppermute | solution.py:697
  101.9 2.5 %collective-permute-done.9.refs_3_ = f32[12,4,128]{2,1,0:T(4,128)S(1)} collective-permute-done((f32[12,4,128]{2,1,0:T(4,128)S(1)}, f32[12,4,128]{2,1,0:T(4,128)S(1)}, u32[]{:S(2)}, u32[]{:S(2)}) %collective-permute-start.9) | collective-permute-done | bytes 24608 | tf_op jit(solution)/shard_map/ppermute | solution.py:698
  104.5 6.1 %all-to-all-done.1.refs_0_ = f32[32,3,16,128]{3,2,1,0:T(8,128)S(1)} async-done(((f32[32,3,16,128]{3,2,1,0:T(8,128)}), f32[32,3,16,128]{3,2,1,0:T(8,128)S(1)}, u32[]{:S(2)}, u32[]{:S(2)}) %all-to-all-start.1) | async-done | bytes 786464 | tf_op jit(solution)/shard_map/all_to_all | solution.py:755
  111.5 12.5 %coarse_and_up.1 = f32[2,16,16,128]{3,2,1,0:T(8,128)} custom-call(f32[32,3,16,128]{3,2,1,0:T(8,128)} %copy-done.5, f32[12,4,128]{2,1,0:T(4,128)} %copy-done.2, f32[12,4,128]{2,1,0:T(4,128)} %copy-done.14, f32[12,4,128]{2,1,0:T(4,128)} %copy-done.13, f32[20,2,14,24,128]{4,3,2,1,0:T(8,128)} %get-tuple-element.19.refs_4_, ...), custom_call_target="tpu_custom_call" | custom-call | tf_op jit(solution)/shard_map/coarse_and_up/pallas_call | solution.py:676
  (49 shorter events, 9.3 us)
Async XLA Ops:
  1.8 6.7 %collective-permute-start = (f32[3,4,16,128]{3,2,1,0:T(8,128)S(1)}, f32[3,4,16,128]{3,2,1,0:T(8,128)S(1)}, u32[]{:S(2)}, u32[]{:S(2)}) collective-permute-start(f32[3,4,16,128]{3,2,1,0:T(8,128)S(1)} %pad_maximum_fusion.2), channel_id=1, source_target_pairs={{0,32},{32,64},{64,96},{96,128},{128,160},{160,192},{192,224},{224... | collective-permute-start | bytes 294920 | tf_op jit(solution)/shard_map/ppermute | solution.py:718
  6.2 5.5 %collective-permute-start.1 = (f32[3,4,16,128]{3,2,1,0:T(8,128)S(1)}, f32[3,4,16,128]{3,2,1,0:T(8,128)S(1)}, u32[]{:S(2)}, u32[]{:S(2)}) collective-permute-start(f32[3,4,16,128]{3,2,1,0:T(8,128)S(1)} %pad_maximum_fusion.3), channel_id=1, source_target_pairs={{32,0},{64,32},{96,64},{128,96},{160,128},{192,160},{224,192},{256... | collective-permute-start | bytes 294920 | tf_op jit(solution)/shard_map/ppermute | solution.py:719
  8.6 15.1 %copy-start.9 = (f32[3,4,16,128]{3,2,1,0:T(8,128)}, f32[3,4,16,128]{3,2,1,0:T(8,128)S(1)}, u32[]{:S(2)}) copy-start(f32[3,4,16,128]{3,2,1,0:T(8,128)S(1)} %collective-permute-done.refs_2_) | copy-start | bytes 294916
  11.8 11.9 %copy-start.10 = (f32[3,4,16,128]{3,2,1,0:T(8,128)}, f32[3,4,16,128]{3,2,1,0:T(8,128)S(1)}, u32[]{:S(2)}) copy-start(f32[3,4,16,128]{3,2,1,0:T(8,128)S(1)} %collective-permute-done.1.refs_3_) | copy-start | bytes 294916
  11.8 11.9 %collective-permute-start.2 = (f32[3,24,4,128]{3,2,1,0:T(4,128)S(1)}, f32[3,24,4,128]{3,2,1,0:T(4,128)S(1)}, u32[]{:S(2)}, u32[]{:S(2)}) collective-permute-start(f32[3,24,4,128]{3,2,1,0:T(4,128)S(1)} %pad_maximum_fusion), channel_id=1, source_target_pairs={{0,1},{1,2},{2,3},{3,4},{4,5},{5,6},{6,7},{7,8},{8,9},{9,10},{10,1... | collective-permute-start | bytes 442376 | tf_op jit(solution)/shard_map/ppermute | solution.py:726
  16.9 6.8 %collective-permute-start.3 = (f32[3,24,4,128]{3,2,1,0:T(4,128)S(1)}, f32[3,24,4,128]{3,2,1,0:T(4,128)S(1)}, u32[]{:S(2)}, u32[]{:S(2)}) collective-permute-start(f32[3,24,4,128]{3,2,1,0:T(4,128)S(1)} %pad_maximum_fusion.1), channel_id=1, source_target_pairs={{1,0},{2,1},{3,2},{4,3},{5,4},{6,5},{7,6},{8,7},{9,8},{10,9},{11,1... | collective-permute-start | bytes 442376 | tf_op jit(solution)/shard_map/ppermute | solution.py:727
  19.9 0.9 copy-start
  20.8 0.7 copy-start.3
  23.7 0.7 copy-start.11
  23.7 0.7 copy-start.12
  28.9 5.1 %collective-permute-start.4 = (f32[3,8,8,128]{3,2,1,0:T(8,128)}, f32[3,8,8,128]{3,2,1,0:T(8,128)S(1)}, u32[]{:S(2)}, u32[]{:S(2)}) collective-permute-start(f32[3,8,8,128]{3,2,1,0:T(8,128)} %get-tuple-element.14), channel_id=1, source_target_pairs={{0,32},{32,64},{64,96},{96,128},{128,160},{160,192},{192,224},{224... | collective-permute-start | bytes 294920 | tf_op jit(solution)/shard_map/ppermute | solution.py:697
  32.1 6.9 %collective-permute-start.5 = (f32[3,8,8,128]{3,2,1,0:T(8,128)}, f32[3,8,8,128]{3,2,1,0:T(8,128)S(1)}, u32[]{:S(2)}, u32[]{:S(2)}) collective-permute-start(f32[3,8,8,128]{3,2,1,0:T(8,128)} %get-tuple-element.14), channel_id=1, source_target_pairs={{32,0},{64,32},{96,64},{128,96},{160,128},{192,160},{224,192},{256... | collective-permute-start | bytes 294920 | tf_op jit(solution)/shard_map/ppermute | solution.py:698
  38.9 10.4 %copy-start.6 = (f32[3,24,8,128]{3,2,1,0:T(8,128)}, f32[3,24,8,128]{3,2,1,0:T(8,128)S(1)}, u32[]{:S(2)}) copy-start(f32[3,24,8,128]{3,2,1,0:T(8,128)S(1)} %constant_dynamic-update-slice_fusion.refs_0_) | copy-start | bytes 884740
  38.9 9.2 %collective-permute-start.7 = (f32[3,24,8,128]{3,2,1,0:T(8,128)S(1)}, f32[3,24,8,128]{3,2,1,0:T(8,128)S(1)}, u32[]{:S(2)}, u32[]{:S(2)}) collective-permute-start(f32[3,24,8,128]{3,2,1,0:T(8,128)S(1)} %constant_dynamic-update-slice_fusion.refs_0_), channel_id=1, source_target_pairs={{1,0},{2,1},{3,2},{4,3},{5,4},{6,5},{7,6},{8,7},{9,8},{10,9},{11,1... | collective-permute-start | bytes 884744 | tf_op jit(solution)/shard_map/ppermute | solution.py:698
  40.9 8.5 %collective-permute-start.6 = (f32[3,24,8,128]{3,2,1,0:T(8,128)S(1)}, f32[3,24,8,128]{3,2,1,0:T(8,128)S(1)}, u32[]{:S(2)}, u32[]{:S(2)}) collective-permute-start(f32[3,24,8,128]{3,2,1,0:T(8,128)S(1)} %constant_dynamic-update-slice_fusion.refs_0_), channel_id=1, source_target_pairs={{0,1},{1,2},{2,3},{3,4},{4,5},{5,6},{6,7},{7,8},{8,9},{9,10},{10,1... | collective-permute-start | bytes 884744 | tf_op jit(solution)/shard_map/ppermute | solution.py:697
  48.2 1.2 copy-start.7
  49.4 0.7 copy-start.8
  85.5 25.1 %copy-start.2 = (f32[12,4,128]{2,1,0:T(4,128)}, f32[12,4,128]{2,1,0:T(4,128)S(1)}, u32[]{:S(2)}) copy-start(f32[12,4,128]{2,1,0:T(4,128)S(1)} %get-tuple-element.18.refs_1_) | copy-start | bytes 73732
  85.5 25.1 %all-to-all-start.1 = ((f32[32,3,16,128]{3,2,1,0:T(8,128)}), f32[32,3,16,128]{3,2,1,0:T(8,128)S(1)}, u32[]{:S(2)}, u32[]{:S(2)}) async-start(f32[32,3,16,128]{3,2,1,0:T(8,128)} %get-tuple-element.17), calls=%async_computation.1 | async-start | bytes 1572864 | tf_op jit(solution)/shard_map/all_to_all | solution.py:755
  96.4 8.1 %collective-permute-start.9 = (f32[12,4,128]{2,1,0:T(4,128)S(1)}, f32[12,4,128]{2,1,0:T(4,128)S(1)}, u32[]{:S(2)}, u32[]{:S(2)}) collective-permute-start(f32[12,4,128]{2,1,0:T(4,128)S(1)} %get-tuple-element.18.refs_1_), channel_id=1, source_target_pairs={{1,0},{2,1},{3,2},{4,3},{5,4},{6,5},{7,6},{8,7},{9,8},{10,9},{11,1... | collective-permute-start | bytes 73736 | tf_op jit(solution)/shard_map/ppermute | solution.py:698
  98.5 5.9 %collective-permute-start.8 = (f32[12,4,128]{2,1,0:T(4,128)S(1)}, f32[12,4,128]{2,1,0:T(4,128)S(1)}, u32[]{:S(2)}, u32[]{:S(2)}) collective-permute-start(f32[12,4,128]{2,1,0:T(4,128)S(1)} %get-tuple-element.18.refs_1_), channel_id=1, source_target_pairs={{0,1},{1,2},{2,3},{3,4},{4,5},{5,6},{6,7},{7,8},{8,9},{9,10},{10,1... | collective-permute-start | bytes 73736 | tf_op jit(solution)/shard_map/ppermute | solution.py:697
  104.5 6.1 %copy-start.13 = (f32[12,4,128]{2,1,0:T(4,128)}, f32[12,4,128]{2,1,0:T(4,128)S(1)}, u32[]{:S(2)}) copy-start(f32[12,4,128]{2,1,0:T(4,128)S(1)} %collective-permute-done.9.refs_3_) | copy-start | bytes 73732
  104.5 6.1 %copy-start.14 = (f32[12,4,128]{2,1,0:T(4,128)}, f32[12,4,128]{2,1,0:T(4,128)S(1)}, u32[]{:S(2)}) copy-start(f32[12,4,128]{2,1,0:T(4,128)S(1)} %collective-permute-done.8.refs_2_) | copy-start | bytes 73732
  110.6 0.9 copy-start.5
  (2 other events, 1.2 us)

commit v5 on v4

--- a/solution.py
+++ b/solution.py
@@ -13,7 +13,7 @@
 mass_scale = 0.01
 F32 = jnp.float32
 MESSAGE = 24
-MOST_VMEM = 60 * 1024 * 1024
+MOST_VMEM = 51 * 1024 * 1024
 
 
 def lanes(rows):
@@ -319,7 +319,7 @@
     which = lanes(4) & 3
     for z in range(4):
         a, b = pair(v2, z + 4), pair(f2, z + 4)
-        msg_out[8 + 4 * z : 12 + 4 * z] = jnp.where(
+        msg_out[0, 8 + 4 * z : 12 + 4 * z] = jnp.where(
             which < 2, jnp.where(which == 0, a[0][0:4], a[1][0:4]), jnp.where(which == 2, b[0][0:4], b[1][0:4])
         )
     for z in range(2):
@@ -329,10 +329,13 @@
     for z in range(2):
         for c in (0, 1):
             stack[4 * c + 2 * z : 4 * c + 2 * z + 2] = 0.5 * pair_x(rows_paired(buf2, (c, z), 0, 2), 4)
-    msg_out[0:1] = packed_row(stack[...])
-    msg_out[1:2] = far_c[:, 0:LANES]
-    msg_out[2:3] = far_c[:, LANES : 2 * LANES]
-    msg_out[3:8] = jnp.zeros((5, LANES), F32)
+    msg_out[0, 0:1] = packed_row(stack[...])
+    msg_out[0, 1:2] = far_c[:, 0:LANES]
+    msg_out[0, 2:3] = far_c[:, LANES : 2 * LANES]
+    msg_out[0, 3:8] = jnp.zeros((5, LANES), F32)
+    message = msg_out[0]
+    for g in range(1, msg_out.shape[0]):
+        msg_out[g] = message
     landed(copies)
 
 
@@ -576,7 +579,7 @@
 def up_kernel(counts, cells, cmid, cleft, cright, *rest):
     kept1, kept0, out, rest = rest[0], rest[1], rest[2], rest[3:]
     tz2, ty2, tx2, w2, v1, f1, tz1, ty1, tx1, w1, v0, f0, tz0, ty0, tx0, w0 = rest[:16]
-    t3, w3, g3, t4, s3, va, vb, ea, near, a2, b2, f2, e1, a1, b1, e0, a0, b0, sem = rest[16:]
+    t3, w3, g3, t4, s3, va, vb, ea, near, a2, b2, f2, e1, a1, b1, e0, a0, b0, done, sem = rest[16:]
     copies = []
     for i, dst in enumerate(rest[:16]):
         src, dst = (
@@ -662,10 +665,16 @@
 
     def last(z):
         q = swept(z, 1, b0, f0, tz0, ty0, tx0, w0)
-        out[0, z - 4] = q[0][0:16]
-        out[1, z - 4] = q[1][0:16]
-
-    each(4, 20, last)
+        done[0, z - 4] = q[0][0:16]
+        done[1, z - 4] = q[1][0:16]
+
+    copies = []
+    for i in range(4):
+        part = slice(4 * i, 4 * i + 4)
+        for z in range(4):
+            last(4 * i + z + 4)
+        copies += sent([pltpu.make_async_copy(done.at[:, part], out.at[:, part], sem.at[16 + i])])
+    landed(copies)
 
 
 def run(kernel, name, args, outs, scratch, smem=(), far_in=(), far_out=(), copies=0, vmem=32 * 1024 * 1024):
@@ -737,18 +746,18 @@
     msg, state0 = run(
         lambda *refs: fine_kernel((16 * nz, 16 * ny), *refs), "fine_down",
         (source, labels, zb, za, left, right, phase_table, near_c),
-        [(3, 8, 8, LANES), (12, *win0)],
+        [(3, 8, 8, LANES), (20, *win0)],
         [win] * 6 + [pltpu.VMEM((24, 24, LANES), jnp.int32)] + [win] * 4 + [(2, 8, 24, LANES)],
         smem=(6,), far_out=(1,), copies=6, vmem=MOST_VMEM,
     )
     msg, state1 = run(
         lambda *refs: middle_kernel(((8 * nz, 8 * ny), (4 * nz, 4 * ny)), *refs), "middle_down",
         (*window(msg, 1, 8), far_c),
-        [(MESSAGE, LANES), (20, *win1)],
+        [(nz, MESSAGE, LANES), (32, *win1)],
         [win] * 6 + [win2] * 4 + [win] * 4 + [(2, 12, 24, LANES)] + [win2] * 6 + [(2, 2, 16, LANES), (8, LANES)],
         far_out=(1,), copies=10, vmem=MOST_VMEM,
     )
-    column = lax.all_to_all(jnp.broadcast_to(msg[None], (nz, MESSAGE, LANES)), "gz", 0, 0)
+    column = lax.all_to_all(msg, "gz", 0, 0)
     cells, cmid = run(
         spread_kernel, "spread", (column.reshape(nz * MESSAGE, LANES),), [(ny, 3, nz, LANES), (12, 4, LANES)], [],
     )
@@ -766,8 +775,8 @@
         [win2] * 4 + [win] * 12
         + [whole(12, 2), whole(2, 2), whole(2, 2), (12, *small)]
         + [whole(1, 1)[1:]] + [whole(1, 3)[1:]] * 2 + [small, (3, nz, LANES)]
-        + [win2] * 3 + [(2, 12, 24, LANES), win, win, win, win, win],
-        far_in=(4, 5), copies=16, vmem=MOST_VMEM,
+        + [win2] * 3 + [(2, 12, 24, LANES), win, win, win, win, win, (2, 16, 16, LANES)],
+        far_in=(4, 5), far_out=(0,), copies=20, vmem=MOST_VMEM,
     )[0]
 
 

time: 125 us -> 120 us (0.960)
  Pallas kernels: 25.8 us -> 21.5 us
  local copies, waits for them, and re-layouts: 8.6 us -> 6.06 us
  waiting for transfers between devices: 20.1 us -> 21.7 us
    pallas_call x5, Pallas kernels: 25.8 us -> 21.5 us  [run(): pl.pallas_call(kernel, name=name, out_shape=[jax.ShapeDtypeStruct(s, F32)...]
    unnamed x32 -> x12, local copies, waits for them, and re-layouts: 5.95 us -> 4.13 us
  transfers between devices with their start and end apart: 11 -> 11, of which waited for: 7 -> 8; matrix products, arithmetic and copies ran while one was open for 2% -> 1% of each run, Pallas kernels for 1% -> 1%
where the time goes in v5:
time: 120 us; the launch traced here: 119 us
  starting transfers between devices  41.2 us (34%)
  blocking collectives  27.2 us (23%)
  waiting for transfers between devices  21.7 us (18%)
  Pallas kernels  21.5 us (18%)
  local copies, waits for them, and re-layouts  6.06 us (5%)
    all_to_all x1, blocking collectives, body(): column = lax.all_to_all(msg, 'gz', 0, 0)  27.2 us
    pallas_call x5, Pallas kernels, run(): pl.pallas_call(kernel, name=name, out_shape=[jax.ShapeDtypeStruct(s, F32)...  21.5 us
    all_to_all x1, starting transfers between devices, body(): cells = lax.all_to_all(cells, 'gy', 0, 0)  11.6 us
    ppermute x3, starting transfers between devices, around(): lax.ppermute(lax.slice_in_dim(block, size - width, size, axis=dim), axis,...  10.6 us
    ppermute x3, waiting for transfers between devices, around(): lax.ppermute(lax.slice_in_dim(block, 0, width, axis=dim), axis, down)  9.99 us
    all_to_all x1, waiting for transfers between devices, body(): cells = lax.all_to_all(cells, 'gy', 0, 0)  6.14 us
    ppermute x3, starting transfers between devices, around(): lax.ppermute(lax.slice_in_dim(block, 0, width, axis=dim), axis, down)  5.36 us
    ppermute x1, starting transfers between devices, body(): left = lax.ppermute(side(12, 16), 'gy', up)  5.01 us
  transfers between devices with their start and end apart: 11, of which 8 were waited for; matrix products, arithmetic and copies ran while one was open for 1% of the time, Pallas kernels for 1%

profile of v5, /device:TPU:1, one launch (start us, length us, event | category | flops | bytes accessed | tf_op | source)
XLA Modules:
  0.0 119.0 jit_solution(13016933501941890417)
XLA Ops:
  1.8 4.4 %collective-permute-start = (f32[3,4,16,128]{3,2,1,0:T(8,128)S(1)}, f32[3,4,16,128]{3,2,1,0:T(8,128)S(1)}, u32[]{:S(2)}, u32[]{:S(2)}) collective-permute-start(f32[3,4,16,128]{3,2,1,0:T(8,128)S(1)} %pad_maximum_fusion.2), channel_id=1, source_target_pairs={{0,32},{32,64},{64,96},{96,128},{128,160},{160,192},{192,224},{224... | collective-permute-start | bytes 294920 | tf_op jit(solution)/shard_map/ppermute | solution.py:727
  6.2 1.3 %collective-permute-start.1 = (f32[3,4,16,128]{3,2,1,0:T(8,128)S(1)}, f32[3,4,16,128]{3,2,1,0:T(8,128)S(1)}, u32[]{:S(2)}, u32[]{:S(2)}) collective-permute-start(f32[3,4,16,128]{3,2,1,0:T(8,128)S(1)} %pad_maximum_fusion.3), channel_id=1, source_target_pairs={{32,0},{64,32},{96,64},{128,96},{160,128},{192,160},{224,192},{256... | collective-permute-start | bytes 294920 | tf_op jit(solution)/shard_map/ppermute | solution.py:728
  7.5 1.0 fusion
  8.6 3.2 %collective-permute-done.1.refs_3_ = f32[3,4,16,128]{3,2,1,0:T(8,128)S(1)} collective-permute-done((f32[3,4,16,128]{3,2,1,0:T(8,128)S(1)}, f32[3,4,16,128]{3,2,1,0:T(8,128)S(1)}, u32[]{:S(2)}, u32[]{:S(2)}) %collective-permute-start.1) | collective-permute-done | bytes 98336 | tf_op jit(solution)/shard_map/ppermute | solution.py:728
  11.8 5.0 %collective-permute-start.2 = (f32[3,24,4,128]{3,2,1,0:T(4,128)S(1)}, f32[3,24,4,128]{3,2,1,0:T(4,128)S(1)}, u32[]{:S(2)}, u32[]{:S(2)}) collective-permute-start(f32[3,24,4,128]{3,2,1,0:T(4,128)S(1)} %pad_maximum_fusion), channel_id=1, source_target_pairs={{0,1},{1,2},{2,3},{3,4},{4,5},{5,6},{6,7},{7,8},{8,9},{9,10},{10,1... | collective-permute-start | bytes 442376 | tf_op jit(solution)/shard_map/ppermute | solution.py:735
  16.9 3.0 %collective-permute-start.3 = (f32[3,24,4,128]{3,2,1,0:T(4,128)S(1)}, f32[3,24,4,128]{3,2,1,0:T(4,128)S(1)}, u32[]{:S(2)}, u32[]{:S(2)}) collective-permute-start(f32[3,24,4,128]{3,2,1,0:T(4,128)S(1)} %pad_maximum_fusion.1), channel_id=1, source_target_pairs={{1,0},{2,1},{3,2},{4,3},{5,4},{6,5},{7,6},{8,7},{9,8},{10,9},{11,1... | collective-permute-start | bytes 442376 | tf_op jit(solution)/shard_map/ppermute | solution.py:736
  21.5 1.0 coefficients.1
  25.9 3.2 %fine_down.1 = (f32[3,8,8,128]{3,2,1,0:T(8,128)S(1)}, f32[20,2,20,24,128]{4,3,2,1,0:T(8,128)}) custom-call(f32[2,16,16,128]{3,2,1,0:T(8,128)S(1)} %copy-done.2, s32[16,16,128]{2,1,0:T(8,128)S(1)} %copy-done.1, f32[3,4,16,128]{3,2,1,0:T(8,128)S(1)} %collective-permute-done.refs_2_, f32[3,4,16,128]{3,2,1,0:T(8,128)S(1)} %collective-permute-done.1.refs_3_, ...), custom_call_target="tpu_custom_call" | custom-call | tf_op jit(solution)/shard_map/fine_down/pallas_call | solution.py:685
  29.1 3.5 %collective-permute-start.4 = (f32[3,8,8,128]{3,2,1,0:T(8,128)S(1)}, f32[3,8,8,128]{3,2,1,0:T(8,128)S(1)}, u32[]{:S(2)}, u32[]{:S(2)}) collective-permute-start(f32[3,8,8,128]{3,2,1,0:T(8,128)S(1)} %get-tuple-element.14), channel_id=1, source_target_pairs={{0,32},{32,64},{64,96},{96,128},{128,160},{160,192},{192,224},{224... | collective-permute-start | bytes 294920 | tf_op jit(solution)/shard_map/ppermute | solution.py:706
  32.7 1.3 %collective-permute-start.5 = (f32[3,8,8,128]{3,2,1,0:T(8,128)S(1)}, f32[3,8,8,128]{3,2,1,0:T(8,128)S(1)}, u32[]{:S(2)}, u32[]{:S(2)}) collective-permute-start(f32[3,8,8,128]{3,2,1,0:T(8,128)S(1)} %get-tuple-element.14), channel_id=1, source_target_pairs={{32,0},{64,32},{96,64},{128,96},{160,128},{192,160},{224,192},{256... | collective-permute-start | bytes 294920 | tf_op jit(solution)/shard_map/ppermute | solution.py:707
  34.3 5.0 %collective-permute-done.5 = f32[3,8,8,128]{3,2,1,0:T(8,128)S(1)} collective-permute-done((f32[3,8,8,128]{3,2,1,0:T(8,128)S(1)}, f32[3,8,8,128]{3,2,1,0:T(8,128)S(1)}, u32[]{:S(2)}, u32[]{:S(2)}) %collective-permute-start.5) | collective-permute-done | bytes 98336 | tf_op jit(solution)/shard_map/ppermute | solution.py:707
  39.4 1.9 %collective-permute-start.7 = (f32[3,24,8,128]{3,2,1,0:T(8,128)S(1)}, f32[3,24,8,128]{3,2,1,0:T(8,128)S(1)}, u32[]{:S(2)}, u32[]{:S(2)}) collective-permute-start(f32[3,24,8,128]{3,2,1,0:T(8,128)S(1)} %constant_dynamic-update-slice_fusion.refs_0_), channel_id=1, source_target_pairs={{1,0},{2,1},{3,2},{4,3},{5,4},{6,5},{7,6},{8,7},{9,8},{10,9},{11,1... | collective-permute-start | bytes 884744 | tf_op jit(solution)/shard_map/ppermute | solution.py:707
  41.3 3.6 %collective-permute-start.6 = (f32[3,24,8,128]{3,2,1,0:T(8,128)S(1)}, f32[3,24,8,128]{3,2,1,0:T(8,128)S(1)}, u32[]{:S(2)}, u32[]{:S(2)}) collective-permute-start(f32[3,24,8,128]{3,2,1,0:T(8,128)S(1)} %constant_dynamic-update-slice_fusion.refs_0_), channel_id=1, source_target_pairs={{0,1},{1,2},{2,3},{3,4},{4,5},{5,6},{6,7},{7,8},{8,9},{9,10},{10,1... | collective-permute-start | bytes 884744 | tf_op jit(solution)/shard_map/ppermute | solution.py:706
  44.9 2.5 %collective-permute-done.7.refs_2_ = f32[3,24,8,128]{3,2,1,0:T(8,128)S(1)} collective-permute-done((f32[3,24,8,128]{3,2,1,0:T(8,128)S(1)}, f32[3,24,8,128]{3,2,1,0:T(8,128)S(1)}, u32[]{:S(2)}, u32[]{:S(2)}) %collective-permute-start.7) | collective-permute-done | bytes 294944 | tf_op jit(solution)/shard_map/ppermute | solution.py:707
  47.4 1.2 collective-permute-done.6.refs_1_
  48.6 5.2 %middle_down.1 = (f32[16,24,128]{2,1,0:T(8,128)S(1)}, f32[32,2,14,24,128]{4,3,2,1,0:T(8,128)}) custom-call(f32[3,24,8,128]{3,2,1,0:T(8,128)S(1)} %constant_dynamic-update-slice_fusion.refs_0_, f32[3,24,8,128]{3,2,1,0:T(8,128)S(1)} %collective-permute-done.6.refs_1_, f32[3,24,8,128]{3,2,1,0:T(8,128)S(1)} %collective-permute-done.7.refs_2_, ...), custom_call_target="tpu_custom_call" | custom-call | tf_op jit(solution)/shard_map/middle_down/pallas_call | solution.py:685
  53.8 27.2 %all_to_all.10 = f32[16,24,128]{2,1,0:T(8,128)S(1)} all-to-all(f32[16,24,128]{2,1,0:T(8,128)S(1)} %get-tuple-element.16), channel_id=1, replica_groups=mesh['gz'=16,'gy'=32] {'gz'}, dimensions={0} | all-to-all | bytes 393216 | tf_op jit(solution)/shard_map/all_to_all | solution.py:760
  81.0 1.0 spread.1
  81.9 11.6 %all-to-all-start.1 = ((f32[32,3,16,128]{3,2,1,0:T(8,128)}), f32[32,3,16,128]{3,2,1,0:T(8,128)S(1)}, u32[]{:S(2)}, u32[]{:S(2)}) async-start(f32[32,3,16,128]{3,2,1,0:T(8,128)} %get-tuple-element.17), calls=%async_computation.1 | async-start | bytes 1572864 | tf_op jit(solution)/shard_map/all_to_all | solution.py:764
  93.6 2.1 %collective-permute-start.9 = (f32[12,4,128]{2,1,0:T(4,128)S(1)}, f32[12,4,128]{2,1,0:T(4,128)S(1)}, u32[]{:S(2)}, u32[]{:S(2)}) collective-permute-start(f32[12,4,128]{2,1,0:T(4,128)S(1)} %get-tuple-element.18.refs_1_), channel_id=1, source_target_pairs={{1,0},{2,1},{3,2},{4,3},{5,4},{6,5},{7,6},{8,7},{9,8},{10,9},{11,1... | collective-permute-start | bytes 73736 | tf_op jit(solution)/shard_map/ppermute | solution.py:707
  95.7 3.4 %collective-permute-start.8 = (f32[12,4,128]{2,1,0:T(4,128)S(1)}, f32[12,4,128]{2,1,0:T(4,128)S(1)}, u32[]{:S(2)}, u32[]{:S(2)}) collective-permute-start(f32[12,4,128]{2,1,0:T(4,128)S(1)} %get-tuple-element.18.refs_1_), channel_id=1, source_target_pairs={{0,1},{1,2},{2,3},{3,4},{4,5},{5,6},{6,7},{7,8},{8,9},{9,10},{10,1... | collective-permute-start | bytes 73736 | tf_op jit(solution)/shard_map/ppermute | solution.py:706
  99.2 2.5 %collective-permute-done.9.refs_3_ = f32[12,4,128]{2,1,0:T(4,128)S(1)} collective-permute-done((f32[12,4,128]{2,1,0:T(4,128)S(1)}, f32[12,4,128]{2,1,0:T(4,128)S(1)}, u32[]{:S(2)}, u32[]{:S(2)}) %collective-permute-start.9) | collective-permute-done | bytes 24608 | tf_op jit(solution)/shard_map/ppermute | solution.py:707
  101.7 6.1 %all-to-all-done.1.refs_0_ = f32[32,3,16,128]{3,2,1,0:T(8,128)S(1)} async-done(((f32[32,3,16,128]{3,2,1,0:T(8,128)}), f32[32,3,16,128]{3,2,1,0:T(8,128)S(1)}, u32[]{:S(2)}, u32[]{:S(2)}) %all-to-all-start.1) | async-done | bytes 786464 | tf_op jit(solution)/shard_map/all_to_all | solution.py:764
  107.8 11.2 %coarse_and_up.1 = f32[2,16,16,128]{3,2,1,0:T(8,128)} custom-call(f32[32,3,16,128]{3,2,1,0:T(8,128)S(1)} %all-to-all-done.1.refs_0_, f32[12,4,128]{2,1,0:T(4,128)S(1)} %get-tuple-element.18.refs_1_, f32[12,4,128]{2,1,0:T(4,128)S(1)} %collective-permute-done.8.refs_2_, f32[12,4,128]{2,1,0:T(4,128)S(1)} %collective-permute-done.9.refs_3_, ...), custom_call_target="tpu_custom_call" | custom-call | tf_op jit(solution)/shard_map/coarse_and_up/pallas_call | solution.py:685
  (28 shorter events, 7.3 us)
Async XLA Ops:
  1.8 6.7 %collective-permute-start = (f32[3,4,16,128]{3,2,1,0:T(8,128)S(1)}, f32[3,4,16,128]{3,2,1,0:T(8,128)S(1)}, u32[]{:S(2)}, u32[]{:S(2)}) collective-permute-start(f32[3,4,16,128]{3,2,1,0:T(8,128)S(1)} %pad_maximum_fusion.2), channel_id=1, source_target_pairs={{0,32},{32,64},{64,96},{96,128},{128,160},{160,192},{192,224},{224... | collective-permute-start | bytes 294920 | tf_op jit(solution)/shard_map/ppermute | solution.py:727
  6.2 5.5 %collective-permute-start.1 = (f32[3,4,16,128]{3,2,1,0:T(8,128)S(1)}, f32[3,4,16,128]{3,2,1,0:T(8,128)S(1)}, u32[]{:S(2)}, u32[]{:S(2)}) collective-permute-start(f32[3,4,16,128]{3,2,1,0:T(8,128)S(1)} %pad_maximum_fusion.3), channel_id=1, source_target_pairs={{32,0},{64,32},{96,64},{128,96},{160,128},{192,160},{224,192},{256... | collective-permute-start | bytes 294920 | tf_op jit(solution)/shard_map/ppermute | solution.py:728
  11.8 10.6 %collective-permute-start.2 = (f32[3,24,4,128]{3,2,1,0:T(4,128)S(1)}, f32[3,24,4,128]{3,2,1,0:T(4,128)S(1)}, u32[]{:S(2)}, u32[]{:S(2)}) collective-permute-start(f32[3,24,4,128]{3,2,1,0:T(4,128)S(1)} %pad_maximum_fusion), channel_id=1, source_target_pairs={{0,1},{1,2},{2,3},{3,4},{4,5},{5,6},{6,7},{7,8},{8,9},{9,10},{10,1... | collective-permute-start | bytes 442376 | tf_op jit(solution)/shard_map/ppermute | solution.py:735
  16.9 6.5 %collective-permute-start.3 = (f32[3,24,4,128]{3,2,1,0:T(4,128)S(1)}, f32[3,24,4,128]{3,2,1,0:T(4,128)S(1)}, u32[]{:S(2)}, u32[]{:S(2)}) collective-permute-start(f32[3,24,4,128]{3,2,1,0:T(4,128)S(1)} %pad_maximum_fusion.1), channel_id=1, source_target_pairs={{1,0},{2,1},{3,2},{4,3},{5,4},{6,5},{7,6},{8,7},{9,8},{10,9},{11,1... | collective-permute-start | bytes 442376 | tf_op jit(solution)/shard_map/ppermute | solution.py:736
  19.9 0.9 copy-start
  20.8 0.7 copy-start.3
  23.4 0.9 copy-start.1
  24.3 0.9 copy-start.2
  25.2 0.7 copy-start.4
  29.1 5.2 %collective-permute-start.4 = (f32[3,8,8,128]{3,2,1,0:T(8,128)S(1)}, f32[3,8,8,128]{3,2,1,0:T(8,128)S(1)}, u32[]{:S(2)}, u32[]{:S(2)}) collective-permute-start(f32[3,8,8,128]{3,2,1,0:T(8,128)S(1)} %get-tuple-element.14), channel_id=1, source_target_pairs={{0,32},{32,64},{64,96},{96,128},{128,160},{160,192},{192,224},{224... | collective-permute-start | bytes 294920 | tf_op jit(solution)/shard_map/ppermute | solution.py:706
  32.7 6.7 %collective-permute-start.5 = (f32[3,8,8,128]{3,2,1,0:T(8,128)S(1)}, f32[3,8,8,128]{3,2,1,0:T(8,128)S(1)}, u32[]{:S(2)}, u32[]{:S(2)}) collective-permute-start(f32[3,8,8,128]{3,2,1,0:T(8,128)S(1)} %get-tuple-element.14), channel_id=1, source_target_pairs={{32,0},{64,32},{96,64},{128,96},{160,128},{192,160},{224,192},{256... | collective-permute-start | bytes 294920 | tf_op jit(solution)/shard_map/ppermute | solution.py:707
  39.4 8.0 %collective-permute-start.7 = (f32[3,24,8,128]{3,2,1,0:T(8,128)S(1)}, f32[3,24,8,128]{3,2,1,0:T(8,128)S(1)}, u32[]{:S(2)}, u32[]{:S(2)}) collective-permute-start(f32[3,24,8,128]{3,2,1,0:T(8,128)S(1)} %constant_dynamic-update-slice_fusion.refs_0_), channel_id=1, source_target_pairs={{1,0},{2,1},{3,2},{4,3},{5,4},{6,5},{7,6},{8,7},{9,8},{10,9},{11,1... | collective-permute-start | bytes 884744 | tf_op jit(solution)/shard_map/ppermute | solution.py:707
  41.3 7.3 %collective-permute-start.6 = (f32[3,24,8,128]{3,2,1,0:T(8,128)S(1)}, f32[3,24,8,128]{3,2,1,0:T(8,128)S(1)}, u32[]{:S(2)}, u32[]{:S(2)}) collective-permute-start(f32[3,24,8,128]{3,2,1,0:T(8,128)S(1)} %constant_dynamic-update-slice_fusion.refs_0_), channel_id=1, source_target_pairs={{0,1},{1,2},{2,3},{3,4},{4,5},{5,6},{6,7},{7,8},{8,9},{9,10},{10,1... | collective-permute-start | bytes 884744 | tf_op jit(solution)/shard_map/ppermute | solution.py:706
  81.9 25.9 %all-to-all-start.1 = ((f32[32,3,16,128]{3,2,1,0:T(8,128)}), f32[32,3,16,128]{3,2,1,0:T(8,128)S(1)}, u32[]{:S(2)}, u32[]{:S(2)}) async-start(f32[32,3,16,128]{3,2,1,0:T(8,128)} %get-tuple-element.17), calls=%async_computation.1 | async-start | bytes 1572864 | tf_op jit(solution)/shard_map/all_to_all | solution.py:764
  93.6 8.1 %collective-permute-start.9 = (f32[12,4,128]{2,1,0:T(4,128)S(1)}, f32[12,4,128]{2,1,0:T(4,128)S(1)}, u32[]{:S(2)}, u32[]{:S(2)}) collective-permute-start(f32[12,4,128]{2,1,0:T(4,128)S(1)} %get-tuple-element.18.refs_1_), channel_id=1, source_target_pairs={{1,0},{2,1},{3,2},{4,3},{5,4},{6,5},{7,6},{8,7},{9,8},{10,9},{11,1... | collective-permute-start | bytes 73736 | tf_op jit(solution)/shard_map/ppermute | solution.py:707
  95.7 5.9 %collective-permute-start.8 = (f32[12,4,128]{2,1,0:T(4,128)S(1)}, f32[12,4,128]{2,1,0:T(4,128)S(1)}, u32[]{:S(2)}, u32[]{:S(2)}) collective-permute-start(f32[12,4,128]{2,1,0:T(4,128)S(1)} %get-tuple-element.18.refs_1_), channel_id=1, source_target_pairs={{0,1},{1,2},{2,3},{3,4},{4,5},{5,6},{6,7},{7,8},{8,9},{9,10},{10,1... | collective-permute-start | bytes 73736 | tf_op jit(solution)/shard_map/ppermute | solution.py:706

commit v6 on v5

--- a/solution.py
+++ b/solution.py
@@ -165,18 +165,20 @@
     return jnp.sum(jnp.where(lane // 16 == row, cells, 0.0), axis=0, keepdims=True)
 
 
-def lookup(lab, table):
-    out = []
-    for c in range(4):
-        scale = 1.0 if c < 2 else mass_scale
-        val = [table[p, c] * F32(scale) for p in range(PHASES)]
-        out.append(jnp.where(lab == 0, val[0], jnp.where(lab == 1, val[1], jnp.where(lab == 2, val[2], val[3]))))
-    return out
-
-
-def coeff_kernel(labels, table, near_out, far_out, buf, c1, c2, stack):
+def lookup(lab, val):
+    return [
+        jnp.where(lab == 0, val[0][c], jnp.where(lab == 1, val[1][c], jnp.where(lab == 2, val[2][c], val[3][c])))
+        for c in range(4)
+    ]
+
+
+def coeff_kernel(base, table, near_out, far_out, values_out, buf, c1, c2, stack):
+    val = [[table[p, c] * F32(1.0 if c < 2 else mass_scale) for c in range(4)] for p in range(PHASES)]
+    for p in range(PHASES):
+        for c in range(4):
+            values_out[p, c] = jnp.full((8, LANES), val[p][c], F32)
     for z in range(8):
-        a, b = lookup(labels[2 * z], table), lookup(labels[2 * z + 1], table)
+        a, b = lookup(base[2, 2 * z], val), lookup(base[2, 2 * z + 1], val)
         for c in range(4):
             buf[c, z] = a[c] + b[c]
     for z in range(8):
@@ -206,28 +208,29 @@
 
 
 def fine_kernel(
-    sizes, source, labels, zb, za, left, right, table, near_c, msg_out, *rest
+    sizes, base, zb, za, left, right, values, near_c, msg_out, *rest
 ):
     keeps, v, f, tz, ty, tx, w, lab, s, m, g, first, buf, sem = rest
     first_z = lax.axis_index("gz") * 16 - 4
     first_y = lax.axis_index("gy") * 16
 
-    def load(z, own):
-        dst = (f.at[0, z], f.at[1, z], lab.at[z])
-        for c in range(3):
-            dst[c][0:16] = own[c]
-            dst[c][16:20] = right[c, z].astype(dst[c].dtype)
-            dst[c][20:24] = left[c, z].astype(dst[c].dtype)
+    def load(z, own, k):
+        for c, dst in enumerate((f.at[0, z], f.at[1, z], lab.at[z])):
+            dst[0:16] = own[c, k]
+            dst[16:20] = right[c, z]
+            dst[20:24] = left[c, z]
         ok = inside(24, 20, z, first_z, first_y, *sizes)
-        vals = lookup(lab[z], table)
-        for c in (0, 1):
-            s[c, z] = jnp.where(ok, vals[c], 0.0)
-            m[c, z] = vals[2 + c]
+        val = [[values[p, c] for c in range(4)] for p in range(PHASES)]
+        for r in (slice(0, 8), slice(8, 16), slice(16, 24)):
+            got = lookup(lab[z, r], val)
+            for c in (0, 1):
+                s[c, z, r] = jnp.where(ok[r], got[c], 0.0)
+                m[c, z, r] = got[2 + c]
 
     for z in range(4):
-        load(z, (zb[0, z], zb[1, z], zb[2, z].astype(jnp.int32)))
-        load(z + 20, (za[0, z], za[1, z], za[2, z].astype(jnp.int32)))
-    each(0, 16, lambda z: load(z + 4, (source[0, z], source[1, z], labels[z])))
+        load(z, zb, z)
+        load(z + 20, za, z)
+    each(0, 16, lambda z: load(z + 4, base, z))
 
     def faces(z):
         ok = inside(24, 20, z, first_z, first_y, *sizes)
@@ -694,18 +697,28 @@
     )(*args)
 
 
-def shifts(axis):
+def traded(axis, top, bottom):
     n = lax.axis_size(axis)
-    up = [(i, i + 1) for i in range(n - 1)]
-    return up, [(j, i) for i, j in up]
+    even = lax.axis_index(axis) % 2 == 0
+    far = [(i, j) for k in range(2, n, 2) for i, j in ((k - 1, k), (k, k - 1))]
+    close = [(i, i ^ 1) for i in range(n) if i ^ 1 < n]
+    same = top is bottom
+    to_far = top if same else jnp.where(even, bottom, top)
+    to_close = top if same else jnp.where(even, top, bottom)
+    from_far = lax.ppermute(to_far, axis, far)
+    from_close = lax.ppermute(to_close, axis, close)
+    return jnp.where(even, from_far, from_close), jnp.where(even, from_close, from_far)
 
 
 def around(block, axis, dim, width):
-    up, down = shifts(axis)
     size = block.shape[dim]
-    before = lax.ppermute(lax.slice_in_dim(block, size - width, size, axis=dim), axis, up)
-    after = lax.ppermute(lax.slice_in_dim(block, 0, width, axis=dim), axis, down)
-    return before, after
+    if width == size:
+        return traded(axis, block, block)
+    return traded(
+        axis,
+        lax.slice_in_dim(block, size - width, size, axis=dim),
+        lax.slice_in_dim(block, 0, width, axis=dim),
+    )
 
 
 def window(block, dim, width):
@@ -718,26 +731,13 @@
 def body(source, labels, phase_table):
     nz, ny = lax.axis_size("gz"), lax.axis_size("gy")
 
-    marks = lax.optimization_barrier(labels.astype(F32))[None]
-
-    def edge(lo, hi):
-        return jnp.concatenate([source[:, lo:hi], marks[:, lo:hi]], axis=0)
-
-    up, down = shifts("gz")
-    zb = lax.ppermute(edge(12, 16), "gz", up)
-    za = lax.ppermute(edge(0, 4), "gz", down)
-
-    def side(lo, hi):
-        own = jnp.concatenate([source[:, :, lo:hi], marks[:, :, lo:hi]], axis=0)
-        return jnp.concatenate([zb[:, :, lo:hi], own, za[:, :, lo:hi]], axis=1)
-
-    up, down = shifts("gy")
-    left = lax.ppermute(side(12, 16), "gy", up)
-    right = lax.ppermute(side(0, 4), "gy", down)
-
-    near_c, far_c = run(
-        coeff_kernel, "coefficients", (labels, phase_table),
-        [(2, 8, 8, LANES), (1, 2 * LANES)],
+    base = lax.optimization_barrier(jnp.concatenate([source, labels.astype(F32)[None]], axis=0))
+    zb, za = around(base, "gz", 1, 4)
+    left, right = around(jnp.concatenate([zb, base, za], axis=1), "gy", 2, 4)
+
+    near_c, far_c, values = run(
+        coeff_kernel, "coefficients", (base, phase_table),
+        [(2, 8, 8, LANES), (1, 2 * LANES), (PHASES, 4, 8, LANES)],
         [(4, 8, 16, LANES), (4, 8, 8, LANES), (4, 4, 4, LANES), (2, 8, LANES)], smem=(1,),
     )
     win, win2 = (2, 24, 24, LANES), (2, 12, 16, LANES)
@@ -745,10 +745,10 @@
     win1 = (2, KEPT1.stop - KEPT1.start, 24, LANES)
     msg, state0 = run(
         lambda *refs: fine_kernel((16 * nz, 16 * ny), *refs), "fine_down",
-        (source, labels, zb, za, left, right, phase_table, near_c),
+        (base, zb, za, left, right, values, near_c),
         [(3, 8, 8, LANES), (20, *win0)],
-        [win] * 6 + [pltpu.VMEM((24, 24, LANES), jnp.int32)] + [win] * 4 + [(2, 8, 24, LANES)],
-        smem=(6,), far_out=(1,), copies=6, vmem=MOST_VMEM,
+        [win] * 6 + [(24, 24, LANES)] + [win] * 4 + [(2, 8, 24, LANES)],
+        far_out=(1,), copies=6, vmem=MOST_VMEM,
     )
     msg, state1 = run(
         lambda *refs: middle_kernel(((8 * nz, 8 * ny), (4 * nz, 4 * ny)), *refs), "middle_down",

time: 120 us -> 115 us (0.958)
  local copies, waits for them, and re-layouts: 6.06 us -> 0.68 us
  waiting for transfers between devices: 21.7 us -> 18.5 us
  blocking collectives: 27.2 us -> 29.4 us
    unnamed x12 -> x2, local copies, waits for them, and re-layouts: 4.13 us -> 0.68 us
    ppermute x10, waiting for transfers between devices: 15.6 us -> 12.4 us  [the longest x5 8.57 us: traded(): from_far = lax.ppermute(to_far, axis, far)]
    all_to_all x1, blocking collectives: 27.2 us -> 29.4 us  [body(): column = lax.all_to_all(msg, 'gz', 0, 0)]
    slice x6 -> x0, local copies, waits for them, and re-layouts: 1.92 us -> none  [the longest x2 1.01 us: side(): own = jnp.concatenate([source[:, :, lo:hi], marks[:, :, lo:hi]], axis=0)]
    ppermute x10, starting transfers between devices: 29.6 us -> 30.9 us  [the longest x5 19.3 us: traded(): from_close = lax.ppermute(to_close, axis, close)]
  transfers between devices with their start and end apart: 11 -> 11, of which waited for: 8 -> 5; matrix products, arithmetic and copies ran while one was open for 1% -> 0% of each run, Pallas kernels for 1% -> 1%
where the time goes in v6:
time: 115 us; the launch traced here: 114 us
  starting transfers between devices  42.4 us (37%)
  blocking collectives  29.4 us (26%)
  Pallas kernels  20.9 us (18%)
  waiting for transfers between devices  18.5 us (16%)
  other arithmetic  2.12 us (2%)
    all_to_all x1, blocking collectives, body(): column = lax.all_to_all(msg, 'gz', 0, 0)  29.4 us
    pallas_call x5, Pallas kernels, run(): pl.pallas_call(kernel, name=name, out_shape=[jax.ShapeDtypeStruct(s, F32)...  20.9 us
    ppermute x5, starting transfers between devices, traded(): from_close = lax.ppermute(to_close, axis, close)  19.3 us
    ppermute x5, starting transfers between devices, traded(): from_far = lax.ppermute(to_far, axis, far)  11.5 us
    all_to_all x1, starting transfers between devices, body(): cells = lax.all_to_all(cells, 'gy', 0, 0)  11.5 us
    ppermute x5, waiting for transfers between devices, traded(): from_far = lax.ppermute(to_far, axis, far)  8.57 us
    all_to_all x1, waiting for transfers between devices, body(): cells = lax.all_to_all(cells, 'gy', 0, 0)  6.13 us
    ppermute x5, waiting for transfers between devices, traded(): from_close = lax.ppermute(to_close, axis, close)  3.78 us
  transfers between devices with their start and end apart: 11, of which 5 were waited for; matrix products, arithmetic and copies ran while one was open for 0% of the time, Pallas kernels for 1%

profile of v6, /device:TPU:1, one launch (start us, length us, event | category | flops | bytes accessed | tf_op | source)
XLA Modules:
  0.0 114.2 jit_solution(7473111729738354966)
XLA Ops:
  0.0 0.9 convert_bitcast_fusion
  0.9 1.0 pad_maximum_fusion.base.refs_0_
  1.9 4.4 %collective-permute-start.1 = (f32[3,4,16,128]{3,2,1,0:T(8,128)S(1)}, f32[3,4,16,128]{3,2,1,0:T(8,128)S(1)}, u32[]{:S(2)}, u32[]{:S(2)}) collective-permute-start(f32[3,4,16,128]{3,2,1,0:T(8,128)S(1)} %get-tuple-element.28), channel_id=1, source_target_pairs={{0,32},{32,0},{64,96},{96,64},{128,160},{160,128},{192,224},{224,1... | collective-permute-start | bytes 294920 | tf_op jit(solution)/shard_map/ppermute | solution.py:709
  6.3 0.7 collective-permute-start
  7.0 1.3 %collective-permute-done.1 = f32[3,4,16,128]{3,2,1,0:T(8,128)S(1)} collective-permute-done((f32[3,4,16,128]{3,2,1,0:T(8,128)S(1)}, f32[3,4,16,128]{3,2,1,0:T(8,128)S(1)}, u32[]{:S(2)}, u32[]{:S(2)}) %collective-permute-start.1) | collective-permute-done | bytes 98336 | tf_op jit(solution)/shard_map/ppermute | solution.py:709
  8.4 4.8 %collective-permute-start.2 = (f32[3,24,4,128]{3,2,1,0:T(4,128)S(1)}, f32[3,24,4,128]{3,2,1,0:T(4,128)S(1)}, u32[]{:S(2)}, u32[]{:S(2)}) collective-permute-start(f32[3,24,4,128]{3,2,1,0:T(4,128)S(1)} %bitcast.23), channel_id=1, source_target_pairs={{1,2},{2,1},{3,4},{4,3},{5,6},{6,5},{7,8},{8,7},{9,10},{10,9},{11,... | collective-permute-start | bytes 442376 | tf_op jit(solution)/shard_map/ppermute | solution.py:708
  13.3 4.8 %collective-permute-start.3 = (f32[3,24,4,128]{3,2,1,0:T(4,128)S(1)}, f32[3,24,4,128]{3,2,1,0:T(4,128)S(1)}, u32[]{:S(2)}, u32[]{:S(2)}) collective-permute-start(f32[3,24,4,128]{3,2,1,0:T(4,128)S(1)} %get-tuple-element.23), channel_id=1, source_target_pairs={{0,1},{1,0},{2,3},{3,2},{4,5},{5,4},{6,7},{7,6},{8,9},{9,8},{10,11... | collective-permute-start | bytes 442376 | tf_op jit(solution)/shard_map/ppermute | solution.py:709
  18.0 0.7 copy-done
  18.7 1.0 coefficients.1
  19.8 2.6 %fine_down.1 = (f32[3,8,8,128]{3,2,1,0:T(8,128)S(1)}, f32[20,2,20,24,128]{4,3,2,1,0:T(8,128)}) custom-call(f32[3,16,16,128]{3,2,1,0:T(8,128)S(1)} %pad_maximum_fusion.base.refs_0_, f32[3,4,16,128]{3,2,1,0:T(8,128)S(1)} %get-tuple-element.35.refs_1_, f32[3,4,16,128]{3,2,1,0:T(8,128)S(1)} %get-tuple-element.34.refs_2_, f32[3,24,4,128]{3,2,1,0:T(4,128)S(1)} %bitcast.16, ...), custom_call_target="tpu_custom_call" | custom-call | tf_op jit(solution)/shard_map/fine_down/pallas_call | solution.py:688
  22.4 5.6 %collective-permute-start.5 = (f32[3,8,8,128]{3,2,1,0:T(8,128)S(1)}, f32[3,8,8,128]{3,2,1,0:T(8,128)S(1)}, u32[]{:S(2)}, u32[]{:S(2)}) collective-permute-start(f32[3,8,8,128]{3,2,1,0:T(8,128)S(1)} %get-tuple-element.16), channel_id=1, source_target_pairs={{0,32},{32,0},{64,96},{96,64},{128,160},{160,128},{192,224},{224,1... | collective-permute-start | bytes 294920 | tf_op jit(solution)/shard_map/ppermute | solution.py:709
  28.6 2.5 %collective-permute-done.5 = f32[3,8,8,128]{3,2,1,0:T(8,128)S(1)} collective-permute-done((f32[3,8,8,128]{3,2,1,0:T(8,128)S(1)}, f32[3,8,8,128]{3,2,1,0:T(8,128)S(1)}, u32[]{:S(2)}, u32[]{:S(2)}) %collective-permute-start.5) | collective-permute-done | bytes 98336 | tf_op jit(solution)/shard_map/ppermute | solution.py:709
  31.1 2.5 %collective-permute-start.7 = (f32[3,24,8,128]{3,2,1,0:T(8,128)S(1)}, f32[3,24,8,128]{3,2,1,0:T(8,128)S(1)}, u32[]{:S(2)}, u32[]{:S(2)}) collective-permute-start(f32[3,24,8,128]{3,2,1,0:T(8,128)S(1)} %pad_maximum_fusion.1.refs_0_), channel_id=1, source_target_pairs={{0,1},{1,0},{2,3},{3,2},{4,5},{5,4},{6,7},{7,6},{8,9},{9,8},{10,11... | collective-permute-start | bytes 884744 | tf_op jit(solution)/shard_map/ppermute | solution.py:709
  33.7 1.9 %collective-permute-start.6 = (f32[3,24,8,128]{3,2,1,0:T(8,128)S(1)}, f32[3,24,8,128]{3,2,1,0:T(8,128)S(1)}, u32[]{:S(2)}, u32[]{:S(2)}) collective-permute-start(f32[3,24,8,128]{3,2,1,0:T(8,128)S(1)} %pad_maximum_fusion.1.refs_0_), channel_id=1, source_target_pairs={{1,2},{2,1},{3,4},{4,3},{5,6},{6,5},{7,8},{8,7},{9,10},{10,9},{11,... | collective-permute-start | bytes 884744 | tf_op jit(solution)/shard_map/ppermute | solution.py:708
  35.6 6.1 %collective-permute-done.6 = f32[3,24,8,128]{3,2,1,0:T(8,128)S(1)} collective-permute-done((f32[3,24,8,128]{3,2,1,0:T(8,128)S(1)}, f32[3,24,8,128]{3,2,1,0:T(8,128)S(1)}, u32[]{:S(2)}, u32[]{:S(2)}) %collective-permute-start.6) | collective-permute-done | bytes 294944 | tf_op jit(solution)/shard_map/ppermute | solution.py:708
  41.7 5.2 %middle_down.1 = (f32[16,24,128]{2,1,0:T(8,128)S(1)}, f32[32,2,14,24,128]{4,3,2,1,0:T(8,128)}) custom-call(f32[3,24,8,128]{3,2,1,0:T(8,128)S(1)} %pad_maximum_fusion.1.refs_0_, f32[3,24,8,128]{3,2,1,0:T(8,128)S(1)} %get-tuple-element.27.refs_1_, f32[3,24,8,128]{3,2,1,0:T(8,128)S(1)} %get-tuple-element.26.refs_2_, f32[1,256]{1,0:T(1,128)S(1)} %get-tuple-element.17.refs_3_), custom_call_target="tpu_custom_call" | custom-call | tf_op jit(solution)/shard_map/middle_down/pallas_call | solution.py:688
  47.0 29.4 %all_to_all.10 = f32[16,24,128]{2,1,0:T(8,128)S(1)} all-to-all(f32[16,24,128]{2,1,0:T(8,128)S(1)} %get-tuple-element.18), channel_id=1, replica_groups=mesh['gz'=16,'gy'=32] {'gz'}, dimensions={0} | all-to-all | bytes 393216 | tf_op jit(solution)/shard_map/all_to_all | solution.py:760
  76.4 1.0 spread.1
  77.3 11.5 %all-to-all-start.1 = ((f32[32,3,16,128]{3,2,1,0:T(8,128)}), f32[32,3,16,128]{3,2,1,0:T(8,128)S(1)}, u32[]{:S(2)}, u32[]{:S(2)}) async-start(f32[32,3,16,128]{3,2,1,0:T(8,128)} %get-tuple-element.19), calls=%async_computation.1 | async-start | bytes 1572864 | tf_op jit(solution)/shard_map/all_to_all | solution.py:764
  88.8 2.1 %collective-permute-start.9 = (f32[12,4,128]{2,1,0:T(4,128)S(1)}, f32[12,4,128]{2,1,0:T(4,128)S(1)}, u32[]{:S(2)}, u32[]{:S(2)}) collective-permute-start(f32[12,4,128]{2,1,0:T(4,128)S(1)} %get-tuple-element.20.refs_1_), channel_id=1, source_target_pairs={{0,1},{1,0},{2,3},{3,2},{4,5},{5,4},{6,7},{7,6},{8,9},{9,8},{10,11... | collective-permute-start | bytes 73736 | tf_op jit(solution)/shard_map/ppermute | solution.py:709
  91.0 3.5 %collective-permute-start.8 = (f32[12,4,128]{2,1,0:T(4,128)S(1)}, f32[12,4,128]{2,1,0:T(4,128)S(1)}, u32[]{:S(2)}, u32[]{:S(2)}) collective-permute-start(f32[12,4,128]{2,1,0:T(4,128)S(1)} %get-tuple-element.20.refs_1_), channel_id=1, source_target_pairs={{1,2},{2,1},{3,4},{4,3},{5,6},{6,5},{7,8},{8,7},{9,10},{10,9},{11,... | collective-permute-start | bytes 73736 | tf_op jit(solution)/shard_map/ppermute | solution.py:708
  94.4 2.5 %collective-permute-done.8 = f32[12,4,128]{2,1,0:T(4,128)S(1)} collective-permute-done((f32[12,4,128]{2,1,0:T(4,128)S(1)}, f32[12,4,128]{2,1,0:T(4,128)S(1)}, u32[]{:S(2)}, u32[]{:S(2)}) %collective-permute-start.8) | collective-permute-done | bytes 24608 | tf_op jit(solution)/shard_map/ppermute | solution.py:708
  96.9 6.1 %all-to-all-done.1.refs_0_ = f32[32,3,16,128]{3,2,1,0:T(8,128)S(1)} async-done(((f32[32,3,16,128]{3,2,1,0:T(8,128)}), f32[32,3,16,128]{3,2,1,0:T(8,128)S(1)}, u32[]{:S(2)}, u32[]{:S(2)}) %all-to-all-start.1) | async-done | bytes 786464 | tf_op jit(solution)/shard_map/all_to_all | solution.py:764
  103.0 11.2 %coarse_and_up.1 = f32[2,16,16,128]{3,2,1,0:T(8,128)} custom-call(f32[32,3,16,128]{3,2,1,0:T(8,128)S(1)} %all-to-all-done.1.refs_0_, f32[12,4,128]{2,1,0:T(4,128)S(1)} %get-tuple-element.20.refs_1_, f32[12,4,128]{2,1,0:T(4,128)S(1)} %bitcast.18, f32[12,4,128]{2,1,0:T(4,128)S(1)} %bitcast.17, f32[32,2,14,24,128]{4,3,2,1,0:T(8,128)} %get-tuple-element.21.refs_4_, ...), custom_call_target="tpu_custom_call" | custom-call | tf_op jit(solution)/shard_map/coarse_and_up/pallas_call | solution.py:688
  (17 shorter events, 0.9 us)
Async XLA Ops:
  1.9 6.4 %collective-permute-start.1 = (f32[3,4,16,128]{3,2,1,0:T(8,128)S(1)}, f32[3,4,16,128]{3,2,1,0:T(8,128)S(1)}, u32[]{:S(2)}, u32[]{:S(2)}) collective-permute-start(f32[3,4,16,128]{3,2,1,0:T(8,128)S(1)} %get-tuple-element.28), channel_id=1, source_target_pairs={{0,32},{32,0},{64,96},{96,64},{128,160},{160,128},{192,224},{224,1... | collective-permute-start | bytes 294920 | tf_op jit(solution)/shard_map/ppermute | solution.py:709
  6.3 2.0 %collective-permute-start = (f32[3,4,16,128]{3,2,1,0:T(8,128)S(1)}, f32[3,4,16,128]{3,2,1,0:T(8,128)S(1)}, u32[]{:S(2)}, u32[]{:S(2)}) collective-permute-start(f32[3,4,16,128]{3,2,1,0:T(8,128)S(1)} %get-tuple-element.29), channel_id=1, source_target_pairs={{32,64},{64,32},{96,128},{128,96},{160,192},{192,160},{224,256},{2... | collective-permute-start | bytes 294920 | tf_op jit(solution)/shard_map/ppermute | solution.py:708
  8.4 11.3 %collective-permute-start.2 = (f32[3,24,4,128]{3,2,1,0:T(4,128)S(1)}, f32[3,24,4,128]{3,2,1,0:T(4,128)S(1)}, u32[]{:S(2)}, u32[]{:S(2)}) collective-permute-start(f32[3,24,4,128]{3,2,1,0:T(4,128)S(1)} %bitcast.23), channel_id=1, source_target_pairs={{1,2},{2,1},{3,4},{4,3},{5,6},{6,5},{7,8},{8,7},{9,10},{10,9},{11,... | collective-permute-start | bytes 442376 | tf_op jit(solution)/shard_map/ppermute | solution.py:708
  13.3 6.5 %collective-permute-start.3 = (f32[3,24,4,128]{3,2,1,0:T(4,128)S(1)}, f32[3,24,4,128]{3,2,1,0:T(4,128)S(1)}, u32[]{:S(2)}, u32[]{:S(2)}) collective-permute-start(f32[3,24,4,128]{3,2,1,0:T(4,128)S(1)} %get-tuple-element.23), channel_id=1, source_target_pairs={{0,1},{1,0},{2,3},{3,2},{4,5},{5,4},{6,7},{7,6},{8,9},{9,8},{10,11... | collective-permute-start | bytes 442376 | tf_op jit(solution)/shard_map/ppermute | solution.py:709
  18.0 0.7 copy-start
  22.4 8.7 %collective-permute-start.5 = (f32[3,8,8,128]{3,2,1,0:T(8,128)S(1)}, f32[3,8,8,128]{3,2,1,0:T(8,128)S(1)}, u32[]{:S(2)}, u32[]{:S(2)}) collective-permute-start(f32[3,8,8,128]{3,2,1,0:T(8,128)S(1)} %get-tuple-element.16), channel_id=1, source_target_pairs={{0,32},{32,0},{64,96},{96,64},{128,160},{160,128},{192,224},{224,1... | collective-permute-start | bytes 294920 | tf_op jit(solution)/shard_map/ppermute | solution.py:709
  28.0 3.1 %collective-permute-start.4 = (f32[3,8,8,128]{3,2,1,0:T(8,128)S(1)}, f32[3,8,8,128]{3,2,1,0:T(8,128)S(1)}, u32[]{:S(2)}, u32[]{:S(2)}) collective-permute-start(f32[3,8,8,128]{3,2,1,0:T(8,128)S(1)} %get-tuple-element.16), channel_id=1, source_target_pairs={{32,64},{64,32},{96,128},{128,96},{160,192},{192,160},{224,256},{2... | collective-permute-start | bytes 294920 | tf_op jit(solution)/shard_map/ppermute | solution.py:708
  31.1 4.4 %collective-permute-start.7 = (f32[3,24,8,128]{3,2,1,0:T(8,128)S(1)}, f32[3,24,8,128]{3,2,1,0:T(8,128)S(1)}, u32[]{:S(2)}, u32[]{:S(2)}) collective-permute-start(f32[3,24,8,128]{3,2,1,0:T(8,128)S(1)} %pad_maximum_fusion.1.refs_0_), channel_id=1, source_target_pairs={{0,1},{1,0},{2,3},{3,2},{4,5},{5,4},{6,7},{7,6},{8,9},{9,8},{10,11... | collective-permute-start | bytes 884744 | tf_op jit(solution)/shard_map/ppermute | solution.py:709
  33.7 8.0 %collective-permute-start.6 = (f32[3,24,8,128]{3,2,1,0:T(8,128)S(1)}, f32[3,24,8,128]{3,2,1,0:T(8,128)S(1)}, u32[]{:S(2)}, u32[]{:S(2)}) collective-permute-start(f32[3,24,8,128]{3,2,1,0:T(8,128)S(1)} %pad_maximum_fusion.1.refs_0_), channel_id=1, source_target_pairs={{1,2},{2,1},{3,4},{4,3},{5,6},{6,5},{7,8},{8,7},{9,10},{10,9},{11,... | collective-permute-start | bytes 884744 | tf_op jit(solution)/shard_map/ppermute | solution.py:708
  77.3 25.7 %all-to-all-start.1 = ((f32[32,3,16,128]{3,2,1,0:T(8,128)}), f32[32,3,16,128]{3,2,1,0:T(8,128)S(1)}, u32[]{:S(2)}, u32[]{:S(2)}) async-start(f32[32,3,16,128]{3,2,1,0:T(8,128)} %get-tuple-element.19), calls=%async_computation.1 | async-start | bytes 1572864 | tf_op jit(solution)/shard_map/all_to_all | solution.py:764
  88.8 5.6 %collective-permute-start.9 = (f32[12,4,128]{2,1,0:T(4,128)S(1)}, f32[12,4,128]{2,1,0:T(4,128)S(1)}, u32[]{:S(2)}, u32[]{:S(2)}) collective-permute-start(f32[12,4,128]{2,1,0:T(4,128)S(1)} %get-tuple-element.20.refs_1_), channel_id=1, source_target_pairs={{0,1},{1,0},{2,3},{3,2},{4,5},{5,4},{6,7},{7,6},{8,9},{9,8},{10,11... | collective-permute-start | bytes 73736 | tf_op jit(solution)/shard_map/ppermute | solution.py:709
  91.0 5.9 %collective-permute-start.8 = (f32[12,4,128]{2,1,0:T(4,128)S(1)}, f32[12,4,128]{2,1,0:T(4,128)S(1)}, u32[]{:S(2)}, u32[]{:S(2)}) collective-permute-start(f32[12,4,128]{2,1,0:T(4,128)S(1)} %get-tuple-element.20.refs_1_), channel_id=1, source_target_pairs={{1,2},{2,1},{3,4},{4,3},{5,6},{6,5},{7,8},{8,7},{9,10},{10,9},{11,... | collective-permute-start | bytes 73736 | tf_op jit(solution)/shard_map/ppermute | solution.py:708

commit v7 on v6

--- a/solution.py
+++ b/solution.py
@@ -12,7 +12,7 @@
 keep = 1.0 - relax
 mass_scale = 0.01
 F32 = jnp.float32
-MESSAGE = 24
+MESSAGE = (5, 4, LANES)
 MOST_VMEM = 51 * 1024 * 1024
 
 
@@ -283,13 +283,13 @@
         ok = inside(24, 16, z, gz * 8 - 8, gy * 8, *sizes[0])
         put(first, z, times(make_faces(z, 2, ok, s, m, tz, ty, tx, w, g), pair(f, z)))
 
-    each(1, 23, faces)
+    each(2, 22, faces)
 
     def kept(i, ref):
         return pltpu.make_async_copy(ref.at[:, KEPT1], keeps.at[i], sem.at[i])
 
     copies = sent([kept(i, ref) for i, ref in enumerate((v, f, tz, ty, tx, w)) if i])
-    each(2, 22, lambda z: put(v, z, swept(z, 2, first, f, tz, ty, tx, w)))
+    each(3, 21, lambda z: put(v, z, swept(z, 2, first, f, tz, ty, tx, w)))
     copies += sent([kept(0, v)])
 
     def coarser(dst, scale, z):
@@ -322,7 +322,7 @@
     which = lanes(4) & 3
     for z in range(4):
         a, b = pair(v2, z + 4), pair(f2, z + 4)
-        msg_out[0, 8 + 4 * z : 12 + 4 * z] = jnp.where(
+        msg_out[0, z + 1] = jnp.where(
             which < 2, jnp.where(which == 0, a[0][0:4], a[1][0:4]), jnp.where(which == 2, b[0][0:4], b[1][0:4])
         )
     for z in range(2):
@@ -332,29 +332,30 @@
     for z in range(2):
         for c in (0, 1):
             stack[4 * c + 2 * z : 4 * c + 2 * z + 2] = 0.5 * pair_x(rows_paired(buf2, (c, z), 0, 2), 4)
-    msg_out[0, 0:1] = packed_row(stack[...])
-    msg_out[0, 1:2] = far_c[:, 0:LANES]
-    msg_out[0, 2:3] = far_c[:, LANES : 2 * LANES]
-    msg_out[0, 3:8] = jnp.zeros((5, LANES), F32)
+    msg_out[0, 0, 0:1] = packed_row(stack[...])
+    msg_out[0, 0, 1:2] = far_c[:, 0:LANES]
+    msg_out[0, 0, 2:3] = far_c[:, LANES : 2 * LANES]
+    msg_out[0, 0, 3:4] = jnp.zeros((1, LANES), F32)
     message = msg_out[0]
     for g in range(1, msg_out.shape[0]):
         msg_out[g] = message
     landed(copies)
 
 
-def spread_kernel(column, cells, near):
+def spread_kernel(column, cells, near, rows):
     ny, _, nz, _ = cells.shape
     for k in range(3):
-        q = column[pl.ds(k, nz, stride=MESSAGE), :]
+        for g in range(nz):
+            rows[k, g : g + 1] = column[g, 0, k : k + 1]
+        q = rows[k]
         for p in range(ny):
             cells[p, k] = q
     mine = lax.axis_index("gz")
     for d in (-1, 0, 1):
         p = jnp.clip(mine + d, 0, nz - 1)
         on = jnp.where((mine + d >= 0) & (mine + d < nz), 1.0, 0.0)
-        q = on * column[pl.ds(pl.multiple_of(p * MESSAGE + 8, 8), 16), :]
         for z in range(4):
-            near[4 * d + 4 + z] = q[4 * z : 4 * z + 4]
+            near[4 * d + 4 + z] = on * column[p, z + 1]
 
 
 def real_lanes(rows):
@@ -731,7 +732,9 @@
 def body(source, labels, phase_table):
     nz, ny = lax.axis_size("gz"), lax.axis_size("gy")
 
-    base = lax.optimization_barrier(jnp.concatenate([source, labels.astype(F32)[None]], axis=0))
+    channel = lax.broadcasted_iota(jnp.int32, (3, *labels.shape), 0)
+    padded = jnp.pad(source, ((0, 1), (0, 0), (0, 0), (0, 0)))
+    base = lax.optimization_barrier(jnp.where(channel == 2, labels.astype(F32)[None], padded))
     zb, za = around(base, "gz", 1, 4)
     left, right = around(jnp.concatenate([zb, base, za], axis=1), "gy", 2, 4)
 
@@ -753,13 +756,13 @@
     msg, state1 = run(
         lambda *refs: middle_kernel(((8 * nz, 8 * ny), (4 * nz, 4 * ny)), *refs), "middle_down",
         (*window(msg, 1, 8), far_c),
-        [(nz, MESSAGE, LANES), (32, *win1)],
+        [(nz, *MESSAGE), (32, *win1)],
         [win] * 6 + [win2] * 4 + [win] * 4 + [(2, 12, 24, LANES)] + [win2] * 6 + [(2, 2, 16, LANES), (8, LANES)],
         far_out=(1,), copies=10, vmem=MOST_VMEM,
     )
     column = lax.all_to_all(msg, "gz", 0, 0)
     cells, cmid = run(
-        spread_kernel, "spread", (column.reshape(nz * MESSAGE, LANES),), [(ny, 3, nz, LANES), (12, 4, LANES)], [],
+        spread_kernel, "spread", (column,), [(ny, 3, nz, LANES), (12, 4, LANES)], [(3, nz, LANES)],
     )
     cells = lax.all_to_all(cells, "gy", 0, 0)
     cwin = (cmid, *around(cmid, "gy", 1, 4))

time: 115 us -> 114 us (level)
  no operation moved by 1% of the time
where the time goes in v7:
time: 114 us; the launch traced here: 113 us
  starting transfers between devices  41.9 us (37%)
  blocking collectives  29 us (25%)
  Pallas kernels  20.8 us (18%)
  waiting for transfers between devices  18.5 us (16%)
  other arithmetic  2.2 us (2%)
    all_to_all x1, blocking collectives, body(): column = lax.all_to_all(msg, 'gz', 0, 0)  29 us
    pallas_call x5, Pallas kernels, run(): pl.pallas_call(kernel, name=name, out_shape=[jax.ShapeDtypeStruct(s, F32)...  20.8 us
    ppermute x5, starting transfers between devices, traded(): from_close = lax.ppermute(to_close, axis, close)  19.3 us
    ppermute x5, starting transfers between devices, traded(): from_far = lax.ppermute(to_far, axis, far)  11.5 us
    all_to_all x1, starting transfers between devices, body(): cells = lax.all_to_all(cells, 'gy', 0, 0)  11.1 us
    ppermute x5, waiting for transfers between devices, traded(): from_far = lax.ppermute(to_far, axis, far)  8.57 us
    all_to_all x1, waiting for transfers between devices, body(): cells = lax.all_to_all(cells, 'gy', 0, 0)  6.13 us
    ppermute x5, waiting for transfers between devices, traded(): from_close = lax.ppermute(to_close, axis, close)  3.78 us
  transfers between devices with their start and end apart: 11, of which 5 were waited for; matrix products, arithmetic and copies ran while one was open for 0% of the time, Pallas kernels for 1%

profile of v7, /device:TPU:1, one launch (start us, length us, event | category | flops | bytes accessed | tf_op | source)
XLA Modules:
  0.0 113.4 jit_solution(4925003637264873307)
XLA Ops:
  0.0 0.9 convert_element_type.5
  0.9 1.0 pad_select_fusion.base.refs_0_
  2.0 4.4 %collective-permute-start.1 = (f32[3,4,16,128]{3,2,1,0:T(8,128)S(1)}, f32[3,4,16,128]{3,2,1,0:T(8,128)S(1)}, u32[]{:S(2)}, u32[]{:S(2)}) collective-permute-start(f32[3,4,16,128]{3,2,1,0:T(8,128)S(1)} %get-tuple-element.28), channel_id=1, source_target_pairs={{0,32},{32,0},{64,96},{96,64},{128,160},{160,128},{192,224},{224,1... | collective-permute-start | bytes 294920 | tf_op jit(solution)/shard_map/ppermute | solution.py:710
  6.4 0.7 collective-permute-start
  7.1 1.3 %collective-permute-done.1 = f32[3,4,16,128]{3,2,1,0:T(8,128)S(1)} collective-permute-done((f32[3,4,16,128]{3,2,1,0:T(8,128)S(1)}, f32[3,4,16,128]{3,2,1,0:T(8,128)S(1)}, u32[]{:S(2)}, u32[]{:S(2)}) %collective-permute-start.1) | collective-permute-done | bytes 98336 | tf_op jit(solution)/shard_map/ppermute | solution.py:710
  8.5 4.8 %collective-permute-start.2 = (f32[3,24,4,128]{3,2,1,0:T(4,128)S(1)}, f32[3,24,4,128]{3,2,1,0:T(4,128)S(1)}, u32[]{:S(2)}, u32[]{:S(2)}) collective-permute-start(f32[3,24,4,128]{3,2,1,0:T(4,128)S(1)} %bitcast.19), channel_id=1, source_target_pairs={{1,2},{2,1},{3,4},{4,3},{5,6},{6,5},{7,8},{8,7},{9,10},{10,9},{11,... | collective-permute-start | bytes 442376 | tf_op jit(solution)/shard_map/ppermute | solution.py:709
  13.3 4.8 %collective-permute-start.3 = (f32[3,24,4,128]{3,2,1,0:T(4,128)S(1)}, f32[3,24,4,128]{3,2,1,0:T(4,128)S(1)}, u32[]{:S(2)}, u32[]{:S(2)}) collective-permute-start(f32[3,24,4,128]{3,2,1,0:T(4,128)S(1)} %get-tuple-element.23), channel_id=1, source_target_pairs={{0,1},{1,0},{2,3},{3,2},{4,5},{5,4},{6,7},{7,6},{8,9},{9,8},{10,11... | collective-permute-start | bytes 442376 | tf_op jit(solution)/shard_map/ppermute | solution.py:710
  18.1 0.7 copy-done
  18.8 1.0 coefficients.1
  19.9 2.6 %fine_down.1 = (f32[3,8,8,128]{3,2,1,0:T(8,128)S(1)}, f32[20,2,20,24,128]{4,3,2,1,0:T(8,128)}) custom-call(f32[3,16,16,128]{3,2,1,0:T(8,128)S(1)} %pad_select_fusion.base.refs_0_, f32[3,4,16,128]{3,2,1,0:T(8,128)S(1)} %get-tuple-element.35.refs_1_, f32[3,4,16,128]{3,2,1,0:T(8,128)S(1)} %get-tuple-element.34.refs_2_, f32[3,24,4,128]{3,2,1,0:T(4,128)S(1)} %bitcast.12, ...), custom_call_target="tpu_custom_call" | custom-call | tf_op jit(solution)/shard_map/fine_down/pallas_call | solution.py:689
  22.5 5.6 %collective-permute-start.5 = (f32[3,8,8,128]{3,2,1,0:T(8,128)S(1)}, f32[3,8,8,128]{3,2,1,0:T(8,128)S(1)}, u32[]{:S(2)}, u32[]{:S(2)}) collective-permute-start(f32[3,8,8,128]{3,2,1,0:T(8,128)S(1)} %get-tuple-element.16), channel_id=1, source_target_pairs={{0,32},{32,0},{64,96},{96,64},{128,160},{160,128},{192,224},{224,1... | collective-permute-start | bytes 294920 | tf_op jit(solution)/shard_map/ppermute | solution.py:710
  28.7 2.5 %collective-permute-done.5 = f32[3,8,8,128]{3,2,1,0:T(8,128)S(1)} collective-permute-done((f32[3,8,8,128]{3,2,1,0:T(8,128)S(1)}, f32[3,8,8,128]{3,2,1,0:T(8,128)S(1)}, u32[]{:S(2)}, u32[]{:S(2)}) %collective-permute-start.5) | collective-permute-done | bytes 98336 | tf_op jit(solution)/shard_map/ppermute | solution.py:710
  31.2 2.5 %collective-permute-start.7 = (f32[3,24,8,128]{3,2,1,0:T(8,128)S(1)}, f32[3,24,8,128]{3,2,1,0:T(8,128)S(1)}, u32[]{:S(2)}, u32[]{:S(2)}) collective-permute-start(f32[3,24,8,128]{3,2,1,0:T(8,128)S(1)} %pad_maximum_fusion.refs_0_), channel_id=1, source_target_pairs={{0,1},{1,0},{2,3},{3,2},{4,5},{5,4},{6,7},{7,6},{8,9},{9,8},{10,11... | collective-permute-start | bytes 884744 | tf_op jit(solution)/shard_map/ppermute | solution.py:710
  33.7 1.9 %collective-permute-start.6 = (f32[3,24,8,128]{3,2,1,0:T(8,128)S(1)}, f32[3,24,8,128]{3,2,1,0:T(8,128)S(1)}, u32[]{:S(2)}, u32[]{:S(2)}) collective-permute-start(f32[3,24,8,128]{3,2,1,0:T(8,128)S(1)} %pad_maximum_fusion.refs_0_), channel_id=1, source_target_pairs={{1,2},{2,1},{3,4},{4,3},{5,6},{6,5},{7,8},{8,7},{9,10},{10,9},{11,... | collective-permute-start | bytes 884744 | tf_op jit(solution)/shard_map/ppermute | solution.py:709
  35.7 6.1 %collective-permute-done.6 = f32[3,24,8,128]{3,2,1,0:T(8,128)S(1)} collective-permute-done((f32[3,24,8,128]{3,2,1,0:T(8,128)S(1)}, f32[3,24,8,128]{3,2,1,0:T(8,128)S(1)}, u32[]{:S(2)}, u32[]{:S(2)}) %collective-permute-start.6) | collective-permute-done | bytes 294944 | tf_op jit(solution)/shard_map/ppermute | solution.py:709
  41.8 5.1 %middle_down.1 = (f32[16,5,4,128]{3,2,1,0:T(4,128)S(1)}, f32[32,2,14,24,128]{4,3,2,1,0:T(8,128)}) custom-call(f32[3,24,8,128]{3,2,1,0:T(8,128)S(1)} %pad_maximum_fusion.refs_0_, f32[3,24,8,128]{3,2,1,0:T(8,128)S(1)} %get-tuple-element.27.refs_1_, f32[3,24,8,128]{3,2,1,0:T(8,128)S(1)} %get-tuple-element.26.refs_2_, f32[1,256]{1,0:T(1,128)S(1)} %get-tuple-element.17.refs_3_), custom_call_target="tpu_custom_call" | custom-call | tf_op jit(solution)/shard_map/middle_down/pallas_call | solution.py:689
  46.9 29.0 %all_to_all.10.column = f32[16,5,4,128]{3,2,1,0:T(4,128)S(1)} all-to-all(f32[16,5,4,128]{3,2,1,0:T(4,128)S(1)} %get-tuple-element.18), channel_id=1, replica_groups=mesh['gz'=16,'gy'=32] {'gz'}, dimensions={0} | all-to-all | bytes 327680 | tf_op jit(solution)/shard_map/all_to_all | solution.py:763
  75.9 1.0 spread.1
  76.9 11.1 %all-to-all-start.1 = ((f32[32,3,16,128]{3,2,1,0:T(8,128)}), f32[32,3,16,128]{3,2,1,0:T(8,128)S(1)}, u32[]{:S(2)}, u32[]{:S(2)}) async-start(f32[32,3,16,128]{3,2,1,0:T(8,128)} %get-tuple-element.19), calls=%async_computation.1 | async-start | bytes 1572864 | tf_op jit(solution)/shard_map/all_to_all | solution.py:767
  88.0 2.1 %collective-permute-start.9 = (f32[12,4,128]{2,1,0:T(4,128)S(1)}, f32[12,4,128]{2,1,0:T(4,128)S(1)}, u32[]{:S(2)}, u32[]{:S(2)}) collective-permute-start(f32[12,4,128]{2,1,0:T(4,128)S(1)} %get-tuple-element.20.refs_1_), channel_id=1, source_target_pairs={{0,1},{1,0},{2,3},{3,2},{4,5},{5,4},{6,7},{7,6},{8,9},{9,8},{10,11... | collective-permute-start | bytes 73736 | tf_op jit(solution)/shard_map/ppermute | solution.py:710
  90.1 3.5 %collective-permute-start.8 = (f32[12,4,128]{2,1,0:T(4,128)S(1)}, f32[12,4,128]{2,1,0:T(4,128)S(1)}, u32[]{:S(2)}, u32[]{:S(2)}) collective-permute-start(f32[12,4,128]{2,1,0:T(4,128)S(1)} %get-tuple-element.20.refs_1_), channel_id=1, source_target_pairs={{1,2},{2,1},{3,4},{4,3},{5,6},{6,5},{7,8},{8,7},{9,10},{10,9},{11,... | collective-permute-start | bytes 73736 | tf_op jit(solution)/shard_map/ppermute | solution.py:709
  93.6 2.5 %collective-permute-done.8 = f32[12,4,128]{2,1,0:T(4,128)S(1)} collective-permute-done((f32[12,4,128]{2,1,0:T(4,128)S(1)}, f32[12,4,128]{2,1,0:T(4,128)S(1)}, u32[]{:S(2)}, u32[]{:S(2)}) %collective-permute-start.8) | collective-permute-done | bytes 24608 | tf_op jit(solution)/shard_map/ppermute | solution.py:709
  96.1 6.1 %all-to-all-done.1.refs_0_ = f32[32,3,16,128]{3,2,1,0:T(8,128)S(1)} async-done(((f32[32,3,16,128]{3,2,1,0:T(8,128)}), f32[32,3,16,128]{3,2,1,0:T(8,128)S(1)}, u32[]{:S(2)}, u32[]{:S(2)}) %all-to-all-start.1) | async-done | bytes 786464 | tf_op jit(solution)/shard_map/all_to_all | solution.py:767
  102.2 11.2 %coarse_and_up.1 = f32[2,16,16,128]{3,2,1,0:T(8,128)} custom-call(f32[32,3,16,128]{3,2,1,0:T(8,128)S(1)} %all-to-all-done.1.refs_0_, f32[12,4,128]{2,1,0:T(4,128)S(1)} %get-tuple-element.20.refs_1_, f32[12,4,128]{2,1,0:T(4,128)S(1)} %bitcast.14, f32[12,4,128]{2,1,0:T(4,128)S(1)} %bitcast.13, f32[32,2,14,24,128]{4,3,2,1,0:T(8,128)} %get-tuple-element.21.refs_4_, ...), custom_call_target="tpu_custom_call" | custom-call | tf_op jit(solution)/shard_map/coarse_and_up/pallas_call | solution.py:689
  (18 shorter events, 0.9 us)
Async XLA Ops:
  2.0 6.4 %collective-permute-start.1 = (f32[3,4,16,128]{3,2,1,0:T(8,128)S(1)}, f32[3,4,16,128]{3,2,1,0:T(8,128)S(1)}, u32[]{:S(2)}, u32[]{:S(2)}) collective-permute-start(f32[3,4,16,128]{3,2,1,0:T(8,128)S(1)} %get-tuple-element.28), channel_id=1, source_target_pairs={{0,32},{32,0},{64,96},{96,64},{128,160},{160,128},{192,224},{224,1... | collective-permute-start | bytes 294920 | tf_op jit(solution)/shard_map/ppermute | solution.py:710
  6.4 2.0 %collective-permute-start = (f32[3,4,16,128]{3,2,1,0:T(8,128)S(1)}, f32[3,4,16,128]{3,2,1,0:T(8,128)S(1)}, u32[]{:S(2)}, u32[]{:S(2)}) collective-permute-start(f32[3,4,16,128]{3,2,1,0:T(8,128)S(1)} %get-tuple-element.29), channel_id=1, source_target_pairs={{32,64},{64,32},{96,128},{128,96},{160,192},{192,160},{224,256},{2... | collective-permute-start | bytes 294920 | tf_op jit(solution)/shard_map/ppermute | solution.py:709
  8.5 11.3 %collective-permute-start.2 = (f32[3,24,4,128]{3,2,1,0:T(4,128)S(1)}, f32[3,24,4,128]{3,2,1,0:T(4,128)S(1)}, u32[]{:S(2)}, u32[]{:S(2)}) collective-permute-start(f32[3,24,4,128]{3,2,1,0:T(4,128)S(1)} %bitcast.19), channel_id=1, source_target_pairs={{1,2},{2,1},{3,4},{4,3},{5,6},{6,5},{7,8},{8,7},{9,10},{10,9},{11,... | collective-permute-start | bytes 442376 | tf_op jit(solution)/shard_map/ppermute | solution.py:709
  13.3 6.5 %collective-permute-start.3 = (f32[3,24,4,128]{3,2,1,0:T(4,128)S(1)}, f32[3,24,4,128]{3,2,1,0:T(4,128)S(1)}, u32[]{:S(2)}, u32[]{:S(2)}) collective-permute-start(f32[3,24,4,128]{3,2,1,0:T(4,128)S(1)} %get-tuple-element.23), channel_id=1, source_target_pairs={{0,1},{1,0},{2,3},{3,2},{4,5},{5,4},{6,7},{7,6},{8,9},{9,8},{10,11... | collective-permute-start | bytes 442376 | tf_op jit(solution)/shard_map/ppermute | solution.py:710
  18.1 0.7 copy-start
  22.5 8.7 %collective-permute-start.5 = (f32[3,8,8,128]{3,2,1,0:T(8,128)S(1)}, f32[3,8,8,128]{3,2,1,0:T(8,128)S(1)}, u32[]{:S(2)}, u32[]{:S(2)}) collective-permute-start(f32[3,8,8,128]{3,2,1,0:T(8,128)S(1)} %get-tuple-element.16), channel_id=1, source_target_pairs={{0,32},{32,0},{64,96},{96,64},{128,160},{160,128},{192,224},{224,1... | collective-permute-start | bytes 294920 | tf_op jit(solution)/shard_map/ppermute | solution.py:710
  28.0 3.1 %collective-permute-start.4 = (f32[3,8,8,128]{3,2,1,0:T(8,128)S(1)}, f32[3,8,8,128]{3,2,1,0:T(8,128)S(1)}, u32[]{:S(2)}, u32[]{:S(2)}) collective-permute-start(f32[3,8,8,128]{3,2,1,0:T(8,128)S(1)} %get-tuple-element.16), channel_id=1, source_target_pairs={{32,64},{64,32},{96,128},{128,96},{160,192},{192,160},{224,256},{2... | collective-permute-start | bytes 294920 | tf_op jit(solution)/shard_map/ppermute | solution.py:709
  31.2 4.4 %collective-permute-start.7 = (f32[3,24,8,128]{3,2,1,0:T(8,128)S(1)}, f32[3,24,8,128]{3,2,1,0:T(8,128)S(1)}, u32[]{:S(2)}, u32[]{:S(2)}) collective-permute-start(f32[3,24,8,128]{3,2,1,0:T(8,128)S(1)} %pad_maximum_fusion.refs_0_), channel_id=1, source_target_pairs={{0,1},{1,0},{2,3},{3,2},{4,5},{5,4},{6,7},{7,6},{8,9},{9,8},{10,11... | collective-permute-start | bytes 884744 | tf_op jit(solution)/shard_map/ppermute | solution.py:710
  33.7 8.0 %collective-permute-start.6 = (f32[3,24,8,128]{3,2,1,0:T(8,128)S(1)}, f32[3,24,8,128]{3,2,1,0:T(8,128)S(1)}, u32[]{:S(2)}, u32[]{:S(2)}) collective-permute-start(f32[3,24,8,128]{3,2,1,0:T(8,128)S(1)} %pad_maximum_fusion.refs_0_), channel_id=1, source_target_pairs={{1,2},{2,1},{3,4},{4,3},{5,6},{6,5},{7,8},{8,7},{9,10},{10,9},{11,... | collective-permute-start | bytes 884744 | tf_op jit(solution)/shard_map/ppermute | solution.py:709
  76.9 25.3 %all-to-all-start.1 = ((f32[32,3,16,128]{3,2,1,0:T(8,128)}), f32[32,3,16,128]{3,2,1,0:T(8,128)S(1)}, u32[]{:S(2)}, u32[]{:S(2)}) async-start(f32[32,3,16,128]{3,2,1,0:T(8,128)} %get-tuple-element.19), calls=%async_computation.1 | async-start | bytes 1572864 | tf_op jit(solution)/shard_map/all_to_all | solution.py:767
  88.0 5.6 %collective-permute-start.9 = (f32[12,4,128]{2,1,0:T(4,128)S(1)}, f32[12,4,128]{2,1,0:T(4,128)S(1)}, u32[]{:S(2)}, u32[]{:S(2)}) collective-permute-start(f32[12,4,128]{2,1,0:T(4,128)S(1)} %get-tuple-element.20.refs_1_), channel_id=1, source_target_pairs={{0,1},{1,0},{2,3},{3,2},{4,5},{5,4},{6,7},{7,6},{8,9},{9,8},{10,11... | collective-permute-start | bytes 73736 | tf_op jit(solution)/shard_map/ppermute | solution.py:710
  90.1 5.9 %collective-permute-start.8 = (f32[12,4,128]{2,1,0:T(4,128)S(1)}, f32[12,4,128]{2,1,0:T(4,128)S(1)}, u32[]{:S(2)}, u32[]{:S(2)}) collective-permute-start(f32[12,4,128]{2,1,0:T(4,128)S(1)} %get-tuple-element.20.refs_1_), channel_id=1, source_target_pairs={{1,2},{2,1},{3,4},{4,3},{5,6},{6,5},{7,8},{8,7},{9,10},{10,9},{11,... | collective-permute-start | bytes 73736 | tf_op jit(solution)/shard_map/ppermute | solution.py:709

commit v8 on v7

--- a/solution.py
+++ b/solution.py
@@ -706,8 +706,11 @@
     same = top is bottom
     to_far = top if same else jnp.where(even, bottom, top)
     to_close = top if same else jnp.where(even, top, bottom)
+    from_close = lax.ppermute(to_close, axis, close)
     from_far = lax.ppermute(to_far, axis, far)
-    from_close = lax.ppermute(to_close, axis, close)
+    if same:
+        odd = jnp.logical_not(even)
+        return jnp.where(odd, from_close, from_far), jnp.where(odd, from_far, from_close)
     return jnp.where(even, from_far, from_close), jnp.where(even, from_close, from_far)
 
 

time: 114 us -> 111 us (0.974)
  waiting for transfers between devices: 18.5 us -> 14.9 us
  starting transfers between devices: 41.9 us -> 43.8 us
  blocking collectives: 29 us -> 27.5 us
    ppermute x5, waiting for transfers between devices: 8.57 us -> 5.07 us  [traded(): from_far = lax.ppermute(to_far, axis, far)]
    ppermute x5, starting transfers between devices: 11.5 us -> 14.1 us  [traded(): from_far = lax.ppermute(to_far, axis, far)]
    all_to_all x1, starting transfers between devices: 11.1 us -> 9.4 us  [body(): cells = lax.all_to_all(cells, 'gy', 0, 0)]
    all_to_all x1, blocking collectives: 29 us -> 27.5 us  [body(): column = lax.all_to_all(msg, 'gz', 0, 0)]
where the time goes in v8:
time: 111 us; the launch traced here: 110 us
  starting transfers between devices  43.8 us (39%)
  blocking collectives  27.5 us (25%)
  Pallas kernels  20.8 us (19%)
  waiting for transfers between devices  14.9 us (13%)
  other arithmetic  2.2 us (2%)
    all_to_all x1, blocking collectives, body(): column = lax.all_to_all(msg, 'gz', 0, 0)  27.5 us
    pallas_call x5, Pallas kernels, run(): pl.pallas_call(kernel, name=name, out_shape=[jax.ShapeDtypeStruct(s, F32)...  20.8 us
    ppermute x5, starting transfers between devices, traded(): from_close = lax.ppermute(to_close, axis, close)  20.3 us
    ppermute x5, starting transfers between devices, traded(): from_far = lax.ppermute(to_far, axis, far)  14.1 us
    all_to_all x1, starting transfers between devices, body(): cells = lax.all_to_all(cells, 'gy', 0, 0)  9.4 us
    all_to_all x1, waiting for transfers between devices, body(): cells = lax.all_to_all(cells, 'gy', 0, 0)  6.13 us
    ppermute x5, waiting for transfers between devices, traded(): from_far = lax.ppermute(to_far, axis, far)  5.07 us
    ppermute x5, waiting for transfers between devices, traded(): from_close = lax.ppermute(to_close, axis, close)  3.68 us
  transfers between devices with their start and end apart: 11, of which 5 were waited for; matrix products, arithmetic and copies ran while one was open for 0% of the time, Pallas kernels for 1%

profile of v8, /device:TPU:1, one launch (start us, length us, event | category | flops | bytes accessed | tf_op | source)
XLA Modules:
  0.0 110.1 jit_solution(14132336977544093289)
XLA Ops:
  0.0 0.9 convert_element_type.5
  0.9 1.0 pad_select_fusion.base.refs_0_
  2.0 4.4 %collective-permute-start.1 = (f32[3,4,16,128]{3,2,1,0:T(8,128)S(1)}, f32[3,4,16,128]{3,2,1,0:T(8,128)S(1)}, u32[]{:S(2)}, u32[]{:S(2)}) collective-permute-start(f32[3,4,16,128]{3,2,1,0:T(8,128)S(1)} %get-tuple-element.28), channel_id=1, source_target_pairs={{0,32},{32,0},{64,96},{96,64},{128,160},{160,128},{192,224},{224,1... | collective-permute-start | bytes 294920 | tf_op jit(solution)/shard_map/ppermute | solution.py:709
  6.4 0.7 collective-permute-start
  7.1 1.3 %collective-permute-done.1 = f32[3,4,16,128]{3,2,1,0:T(8,128)S(1)} collective-permute-done((f32[3,4,16,128]{3,2,1,0:T(8,128)S(1)}, f32[3,4,16,128]{3,2,1,0:T(8,128)S(1)}, u32[]{:S(2)}, u32[]{:S(2)}) %collective-permute-start.1) | collective-permute-done | bytes 98336 | tf_op jit(solution)/shard_map/ppermute | solution.py:709
  8.5 4.8 %collective-permute-start.2 = (f32[3,24,4,128]{3,2,1,0:T(4,128)S(1)}, f32[3,24,4,128]{3,2,1,0:T(4,128)S(1)}, u32[]{:S(2)}, u32[]{:S(2)}) collective-permute-start(f32[3,24,4,128]{3,2,1,0:T(4,128)S(1)} %bitcast.19), channel_id=1, source_target_pairs={{1,2},{2,1},{3,4},{4,3},{5,6},{6,5},{7,8},{8,7},{9,10},{10,9},{11,... | collective-permute-start | bytes 442376 | tf_op jit(solution)/shard_map/ppermute | solution.py:710
  13.3 4.8 %collective-permute-start.3 = (f32[3,24,4,128]{3,2,1,0:T(4,128)S(1)}, f32[3,24,4,128]{3,2,1,0:T(4,128)S(1)}, u32[]{:S(2)}, u32[]{:S(2)}) collective-permute-start(f32[3,24,4,128]{3,2,1,0:T(4,128)S(1)} %get-tuple-element.23), channel_id=1, source_target_pairs={{0,1},{1,0},{2,3},{3,2},{4,5},{5,4},{6,7},{7,6},{8,9},{9,8},{10,11... | collective-permute-start | bytes 442376 | tf_op jit(solution)/shard_map/ppermute | solution.py:709
  18.1 0.7 copy-done
  18.8 1.0 coefficients.1
  19.9 2.6 %fine_down.1 = (f32[3,8,8,128]{3,2,1,0:T(8,128)S(1)}, f32[20,2,20,24,128]{4,3,2,1,0:T(8,128)}) custom-call(f32[3,16,16,128]{3,2,1,0:T(8,128)S(1)} %pad_select_fusion.base.refs_0_, f32[3,4,16,128]{3,2,1,0:T(8,128)S(1)} %get-tuple-element.35.refs_1_, f32[3,4,16,128]{3,2,1,0:T(8,128)S(1)} %get-tuple-element.34.refs_2_, f32[3,24,4,128]{3,2,1,0:T(4,128)S(1)} %bitcast.12, ...), custom_call_target="tpu_custom_call" | custom-call | tf_op jit(solution)/shard_map/fine_down/pallas_call | solution.py:689
  23.1 7.3 %collective-permute-start.4 = (f32[3,8,8,128]{3,2,1,0:T(8,128)S(1)}, f32[3,8,8,128]{3,2,1,0:T(8,128)S(1)}, u32[]{:S(2)}, u32[]{:S(2)}) collective-permute-start(f32[3,8,8,128]{3,2,1,0:T(8,128)S(1)} %get-tuple-element.16), channel_id=1, source_target_pairs={{0,32},{32,0},{64,96},{96,64},{128,160},{160,128},{192,224},{224,1... | collective-permute-start | bytes 294920 | tf_op jit(solution)/shard_map/ppermute | solution.py:709
  30.5 2.4 %collective-permute-done.4 = f32[3,8,8,128]{3,2,1,0:T(8,128)S(1)} collective-permute-done((f32[3,8,8,128]{3,2,1,0:T(8,128)S(1)}, f32[3,8,8,128]{3,2,1,0:T(8,128)S(1)}, u32[]{:S(2)}, u32[]{:S(2)}) %collective-permute-start.4) | collective-permute-done | bytes 98336 | tf_op jit(solution)/shard_map/ppermute | solution.py:709
  32.9 4.4 %collective-permute-start.7 = (f32[3,24,8,128]{3,2,1,0:T(8,128)S(1)}, f32[3,24,8,128]{3,2,1,0:T(8,128)S(1)}, u32[]{:S(2)}, u32[]{:S(2)}) collective-permute-start(f32[3,24,8,128]{3,2,1,0:T(8,128)S(1)} %pad_maximum_fusion.refs_0_), channel_id=1, source_target_pairs={{1,2},{2,1},{3,4},{4,3},{5,6},{6,5},{7,8},{8,7},{9,10},{10,9},{11,... | collective-permute-start | bytes 884744 | tf_op jit(solution)/shard_map/ppermute | solution.py:710
  37.3 1.9 %collective-permute-start.6 = (f32[3,24,8,128]{3,2,1,0:T(8,128)S(1)}, f32[3,24,8,128]{3,2,1,0:T(8,128)S(1)}, u32[]{:S(2)}, u32[]{:S(2)}) collective-permute-start(f32[3,24,8,128]{3,2,1,0:T(8,128)S(1)} %pad_maximum_fusion.refs_0_), channel_id=1, source_target_pairs={{0,1},{1,0},{2,3},{3,2},{4,5},{5,4},{6,7},{7,6},{8,9},{9,8},{10,11... | collective-permute-start | bytes 884744 | tf_op jit(solution)/shard_map/ppermute | solution.py:709
  39.3 2.5 %collective-permute-done.7 = f32[3,24,8,128]{3,2,1,0:T(8,128)S(1)} collective-permute-done((f32[3,24,8,128]{3,2,1,0:T(8,128)S(1)}, f32[3,24,8,128]{3,2,1,0:T(8,128)S(1)}, u32[]{:S(2)}, u32[]{:S(2)}) %collective-permute-start.7) | collective-permute-done | bytes 294944 | tf_op jit(solution)/shard_map/ppermute | solution.py:710
  41.8 5.1 %middle_down.1 = (f32[16,5,4,128]{3,2,1,0:T(4,128)S(1)}, f32[32,2,14,24,128]{4,3,2,1,0:T(8,128)}) custom-call(f32[3,24,8,128]{3,2,1,0:T(8,128)S(1)} %pad_maximum_fusion.refs_0_, f32[3,24,8,128]{3,2,1,0:T(8,128)S(1)} %get-tuple-element.27.refs_1_, f32[3,24,8,128]{3,2,1,0:T(8,128)S(1)} %get-tuple-element.26.refs_2_, f32[1,256]{1,0:T(1,128)S(1)} %get-tuple-element.17.refs_3_), custom_call_target="tpu_custom_call" | custom-call | tf_op jit(solution)/shard_map/middle_down/pallas_call | solution.py:689
  46.8 27.5 %all_to_all.10.column = f32[16,5,4,128]{3,2,1,0:T(4,128)S(1)} all-to-all(f32[16,5,4,128]{3,2,1,0:T(4,128)S(1)} %get-tuple-element.18), channel_id=1, replica_groups=mesh['gz'=16,'gy'=32] {'gz'}, dimensions={0} | all-to-all | bytes 327680 | tf_op jit(solution)/shard_map/all_to_all | solution.py:766
  74.3 1.0 spread.1
  75.3 9.4 %all-to-all-start.1 = ((f32[32,3,16,128]{3,2,1,0:T(8,128)}), f32[32,3,16,128]{3,2,1,0:T(8,128)S(1)}, u32[]{:S(2)}, u32[]{:S(2)}) async-start(f32[32,3,16,128]{3,2,1,0:T(8,128)} %get-tuple-element.19), calls=%async_computation.1 | async-start | bytes 1572864 | tf_op jit(solution)/shard_map/all_to_all | solution.py:770
  84.7 3.5 %collective-permute-start.9 = (f32[12,4,128]{2,1,0:T(4,128)S(1)}, f32[12,4,128]{2,1,0:T(4,128)S(1)}, u32[]{:S(2)}, u32[]{:S(2)}) collective-permute-start(f32[12,4,128]{2,1,0:T(4,128)S(1)} %get-tuple-element.20.refs_1_), channel_id=1, source_target_pairs={{1,2},{2,1},{3,4},{4,3},{5,6},{6,5},{7,8},{8,7},{9,10},{10,9},{11,... | collective-permute-start | bytes 73736 | tf_op jit(solution)/shard_map/ppermute | solution.py:710
  88.2 1.9 %collective-permute-start.8 = (f32[12,4,128]{2,1,0:T(4,128)S(1)}, f32[12,4,128]{2,1,0:T(4,128)S(1)}, u32[]{:S(2)}, u32[]{:S(2)}) collective-permute-start(f32[12,4,128]{2,1,0:T(4,128)S(1)} %get-tuple-element.20.refs_1_), channel_id=1, source_target_pairs={{0,1},{1,0},{2,3},{3,2},{4,5},{5,4},{6,7},{7,6},{8,9},{9,8},{10,11... | collective-permute-start | bytes 73736 | tf_op jit(solution)/shard_map/ppermute | solution.py:709
  90.2 2.6 %collective-permute-done.9 = f32[12,4,128]{2,1,0:T(4,128)S(1)} collective-permute-done((f32[12,4,128]{2,1,0:T(4,128)S(1)}, f32[12,4,128]{2,1,0:T(4,128)S(1)}, u32[]{:S(2)}, u32[]{:S(2)}) %collective-permute-start.9) | collective-permute-done | bytes 24608 | tf_op jit(solution)/shard_map/ppermute | solution.py:710
  92.8 6.1 %all-to-all-done.1.refs_0_ = f32[32,3,16,128]{3,2,1,0:T(8,128)S(1)} async-done(((f32[32,3,16,128]{3,2,1,0:T(8,128)}), f32[32,3,16,128]{3,2,1,0:T(8,128)S(1)}, u32[]{:S(2)}, u32[]{:S(2)}) %all-to-all-start.1) | async-done | bytes 786464 | tf_op jit(solution)/shard_map/all_to_all | solution.py:770
  98.9 11.2 %coarse_and_up.1 = f32[2,16,16,128]{3,2,1,0:T(8,128)} custom-call(f32[32,3,16,128]{3,2,1,0:T(8,128)S(1)} %all-to-all-done.1.refs_0_, f32[12,4,128]{2,1,0:T(4,128)S(1)} %get-tuple-element.20.refs_1_, f32[12,4,128]{2,1,0:T(4,128)S(1)} %bitcast.14, f32[12,4,128]{2,1,0:T(4,128)S(1)} %bitcast.13, f32[32,2,14,24,128]{4,3,2,1,0:T(8,128)} %get-tuple-element.21.refs_4_, ...), custom_call_target="tpu_custom_call" | custom-call | tf_op jit(solution)/shard_map/coarse_and_up/pallas_call | solution.py:689
  (18 shorter events, 0.9 us)
Async XLA Ops:
  2.0 6.4 %collective-permute-start.1 = (f32[3,4,16,128]{3,2,1,0:T(8,128)S(1)}, f32[3,4,16,128]{3,2,1,0:T(8,128)S(1)}, u32[]{:S(2)}, u32[]{:S(2)}) collective-permute-start(f32[3,4,16,128]{3,2,1,0:T(8,128)S(1)} %get-tuple-element.28), channel_id=1, source_target_pairs={{0,32},{32,0},{64,96},{96,64},{128,160},{160,128},{192,224},{224,1... | collective-permute-start | bytes 294920 | tf_op jit(solution)/shard_map/ppermute | solution.py:709
  6.4 2.0 %collective-permute-start = (f32[3,4,16,128]{3,2,1,0:T(8,128)S(1)}, f32[3,4,16,128]{3,2,1,0:T(8,128)S(1)}, u32[]{:S(2)}, u32[]{:S(2)}) collective-permute-start(f32[3,4,16,128]{3,2,1,0:T(8,128)S(1)} %get-tuple-element.29), channel_id=1, source_target_pairs={{32,64},{64,32},{96,128},{128,96},{160,192},{192,160},{224,256},{2... | collective-permute-start | bytes 294920 | tf_op jit(solution)/shard_map/ppermute | solution.py:710
  8.5 11.3 %collective-permute-start.2 = (f32[3,24,4,128]{3,2,1,0:T(4,128)S(1)}, f32[3,24,4,128]{3,2,1,0:T(4,128)S(1)}, u32[]{:S(2)}, u32[]{:S(2)}) collective-permute-start(f32[3,24,4,128]{3,2,1,0:T(4,128)S(1)} %bitcast.19), channel_id=1, source_target_pairs={{1,2},{2,1},{3,4},{4,3},{5,6},{6,5},{7,8},{8,7},{9,10},{10,9},{11,... | collective-permute-start | bytes 442376 | tf_op jit(solution)/shard_map/ppermute | solution.py:710
  13.3 6.5 %collective-permute-start.3 = (f32[3,24,4,128]{3,2,1,0:T(4,128)S(1)}, f32[3,24,4,128]{3,2,1,0:T(4,128)S(1)}, u32[]{:S(2)}, u32[]{:S(2)}) collective-permute-start(f32[3,24,4,128]{3,2,1,0:T(4,128)S(1)} %get-tuple-element.23), channel_id=1, source_target_pairs={{0,1},{1,0},{2,3},{3,2},{4,5},{5,4},{6,7},{7,6},{8,9},{9,8},{10,11... | collective-permute-start | bytes 442376 | tf_op jit(solution)/shard_map/ppermute | solution.py:709
  18.1 0.7 copy-start
  22.5 8.0 %collective-permute-start.5 = (f32[3,8,8,128]{3,2,1,0:T(8,128)S(1)}, f32[3,8,8,128]{3,2,1,0:T(8,128)S(1)}, u32[]{:S(2)}, u32[]{:S(2)}) collective-permute-start(f32[3,8,8,128]{3,2,1,0:T(8,128)S(1)} %get-tuple-element.16), channel_id=1, source_target_pairs={{32,64},{64,32},{96,128},{128,96},{160,192},{192,160},{224,256},{2... | collective-permute-start | bytes 294920 | tf_op jit(solution)/shard_map/ppermute | solution.py:710
  23.1 9.7 %collective-permute-start.4 = (f32[3,8,8,128]{3,2,1,0:T(8,128)S(1)}, f32[3,8,8,128]{3,2,1,0:T(8,128)S(1)}, u32[]{:S(2)}, u32[]{:S(2)}) collective-permute-start(f32[3,8,8,128]{3,2,1,0:T(8,128)S(1)} %get-tuple-element.16), channel_id=1, source_target_pairs={{0,32},{32,0},{64,96},{96,64},{128,160},{160,128},{192,224},{224,1... | collective-permute-start | bytes 294920 | tf_op jit(solution)/shard_map/ppermute | solution.py:709
  32.9 8.8 %collective-permute-start.7 = (f32[3,24,8,128]{3,2,1,0:T(8,128)S(1)}, f32[3,24,8,128]{3,2,1,0:T(8,128)S(1)}, u32[]{:S(2)}, u32[]{:S(2)}) collective-permute-start(f32[3,24,8,128]{3,2,1,0:T(8,128)S(1)} %pad_maximum_fusion.refs_0_), channel_id=1, source_target_pairs={{1,2},{2,1},{3,4},{4,3},{5,6},{6,5},{7,8},{8,7},{9,10},{10,9},{11,... | collective-permute-start | bytes 884744 | tf_op jit(solution)/shard_map/ppermute | solution.py:710
  37.3 4.4 %collective-permute-start.6 = (f32[3,24,8,128]{3,2,1,0:T(8,128)S(1)}, f32[3,24,8,128]{3,2,1,0:T(8,128)S(1)}, u32[]{:S(2)}, u32[]{:S(2)}) collective-permute-start(f32[3,24,8,128]{3,2,1,0:T(8,128)S(1)} %pad_maximum_fusion.refs_0_), channel_id=1, source_target_pairs={{0,1},{1,0},{2,3},{3,2},{4,5},{5,4},{6,7},{7,6},{8,9},{9,8},{10,11... | collective-permute-start | bytes 884744 | tf_op jit(solution)/shard_map/ppermute | solution.py:709
  75.3 23.6 %all-to-all-start.1 = ((f32[32,3,16,128]{3,2,1,0:T(8,128)}), f32[32,3,16,128]{3,2,1,0:T(8,128)S(1)}, u32[]{:S(2)}, u32[]{:S(2)}) async-start(f32[32,3,16,128]{3,2,1,0:T(8,128)} %get-tuple-element.19), calls=%async_computation.1 | async-start | bytes 1572864 | tf_op jit(solution)/shard_map/all_to_all | solution.py:770
  84.7 8.1 %collective-permute-start.9 = (f32[12,4,128]{2,1,0:T(4,128)S(1)}, f32[12,4,128]{2,1,0:T(4,128)S(1)}, u32[]{:S(2)}, u32[]{:S(2)}) collective-permute-start(f32[12,4,128]{2,1,0:T(4,128)S(1)} %get-tuple-element.20.refs_1_), channel_id=1, source_target_pairs={{1,2},{2,1},{3,4},{4,3},{5,6},{6,5},{7,8},{8,7},{9,10},{10,9},{11,... | collective-permute-start | bytes 73736 | tf_op jit(solution)/shard_map/ppermute | solution.py:710
  88.2 4.5 %collective-permute-start.8 = (f32[12,4,128]{2,1,0:T(4,128)S(1)}, f32[12,4,128]{2,1,0:T(4,128)S(1)}, u32[]{:S(2)}, u32[]{:S(2)}) collective-permute-start(f32[12,4,128]{2,1,0:T(4,128)S(1)} %get-tuple-element.20.refs_1_), channel_id=1, source_target_pairs={{0,1},{1,0},{2,3},{3,2},{4,5},{5,4},{6,7},{7,6},{8,9},{9,8},{10,11... | collective-permute-start | bytes 73736 | tf_op jit(solution)/shard_map/ppermute | solution.py:709
